TPU v7x, 128 devices: a whole 4x4x4 slice. The times are simulated.
128 devices in a mesh: cells: 8 (over x, core), tgt: 16 (over z, y).
Axes of the slice: x: 4, y: 4, z: 4, core: 2. Of those that a mesh axis runs over, the one named last changes fastest.
Arguments:
- placement_a: int32 [128], replicated, may hold values from 0 to 127, as said below
- members_b: int32 [128, 4], replicated, may hold values from 0 to 511, as said below
- source_mass: float32 [128, 256], P('cells'), may hold values from 0.5 to 2
- init_log: float32 [128, 4, 2048], P('cells', None, 'tgt'), may hold values from -4 to 4
Outputs:
- marginals: float32 [128, 4, 2048], P('cells', None, 'tgt')
Inputs may be any that keep to these rules, and one draw needn't show every extreme that they name: `placement_a`: each cell number appears once. `members_b`: each basic cell appears once. Slots 16 * i to 16 * (i + 1) - 1 belong to index i of cells in both partitions; of the basic cells in the A slots of one index, at most 12 lie in the B slots of any one index, and exactly 12 for some pairs of indices.
All inputs are finite; a program needn't handle non-finite values.
Results may differ from a plain program's by a relative error of at most 0.00028.
Values sent between devices are 32-bit elements; how exact they have to be, the bound alone decides.
No kernel may reach another device: no remote copies, remote signals or barrier semaphores. Data moves between devices by JAX's collectives and lax.ppermute only.
A program may use at most 64 MiB of HBM per device.

v0:
```python
import math

import jax
import jax.numpy as jnp
from jax import lax
from jax.sharding import PartitionSpec as P

ITERS = 4
SWEEPS = 4


inverse_eps = 200.0
block_cols = 32
grid_cols = 64


def log_sum(values, axis_number):
    top_score = jnp.max(values, axis=axis_number, keepdims=True)
    exp_sum = jnp.sum(jnp.exp(values - top_score), axis=axis_number, keepdims=True)
    return jnp.squeeze(top_score + jnp.log(exp_sum), axis=axis_number)


def basic_coords(basic_ids, side_px, block_rows):
    pixels = jnp.arange(side_px * side_px, dtype=jnp.int32)
    height = (basic_ids[:, None] // block_cols * side_px + pixels[None, :] // side_px).astype(
        jnp.float32
    ) + 0.5
    across = (basic_ids[:, None] % block_cols * side_px + pixels[None, :] % side_px).astype(
        jnp.float32
    ) + 0.5
    return (height / float(block_rows * side_px), across / float(block_cols * side_px))


def target_coords(start, count, width):
    column = start + jnp.arange(count, dtype=jnp.int32)
    height = (column // grid_cols).astype(jnp.float32) + 0.5
    across = (column % grid_cols).astype(jnp.float32) + 0.5
    return (height / float(width // grid_cols), across / float(grid_cols))


def kernel_cost(row_height, row_across, col_height, col_across):
    return (
        (row_height[:, None] - col_height[None, :]) ** 2
        + (row_across[:, None] - col_across[None, :]) ** 2
    ) * inverse_eps


def route_rows(row_data, receiver_map):
    own_index = lax.axis_index("cells")
    per_device = row_data.shape[0]
    local_pos = own_index * per_device + jnp.arange(per_device, dtype=jnp.int32)
    whole = lax.all_gather(row_data, "cells", axis=0, tiled=True)
    return whole[receiver_map[local_pos]]


def row_reduce(height, across, dual_col, col_height, col_across):

    def scores_of(cell_height, cell_across, cell_dual):
        return cell_dual[None, :] - kernel_cost(cell_height, cell_across, col_height, col_across)

    def partial_peak(cell_data):
        return jnp.max(scores_of(cell_data[0], cell_data[1], cell_data[2]), axis=1)

    top_score = lax.pmax(lax.map(partial_peak, (height, across, dual_col)), "tgt")

    def partial_sum(cell_data):
        scores = scores_of(cell_data[0], cell_data[1], cell_data[2])
        return jnp.sum(jnp.exp(scores - cell_data[3][:, None]), axis=1)

    exp_sum = lax.psum(lax.map(partial_sum, (height, across, dual_col, top_score)), "tgt")
    return top_score + jnp.log(exp_sum)


def half_sweep(basic_ids, log_mass, log_marg, side_px, block_rows, col_height, col_across):
    cell_count = log_mass.shape[0] // 4
    row_count = 4 * side_px * side_px
    height, across = basic_coords(basic_ids, side_px, block_rows)
    height = height.reshape(cell_count, row_count)
    across = across.reshape(cell_count, row_count)
    log_source = log_mass.reshape(cell_count, row_count)
    log_target = log_sum(log_marg.reshape(cell_count, 4, -1), 1)
    dual_col = jnp.zeros(log_target.shape, jnp.float32)
    dual_row = log_source

    def column_part(cell_data):
        kernel = kernel_cost(cell_data[0], cell_data[1], col_height, col_across)
        return log_sum(cell_data[2][:, None] - kernel, 0)

    for iteration in range(ITERS):
        dual_row = log_source - row_reduce(height, across, dual_col, col_height, col_across)
        dual_col = log_target - lax.map(column_part, (height, across, dual_row))

    def final_part(cell_data):
        kernel = kernel_cost(cell_data[0], cell_data[1], col_height, col_across)
        joined = cell_data[2][:, None] + cell_data[3][None, :] - kernel
        return log_sum(joined.reshape(4, side_px * side_px, -1), 1)

    result = lax.map(final_part, (height, across, dual_row, dual_col))
    return result.reshape(4 * cell_count, -1)


def on_device(placement_a, members_b, source_mass, init_log):
    cell_count = init_log.shape[0]
    width_local = init_log.shape[2]
    side_px = math.isqrt(source_mass.shape[1] // 4)
    basic_count = 4 * placement_a.shape[0]
    block_rows = basic_count // block_cols
    per_device = 4 * cell_count
    positions = jnp.arange(basic_count, dtype=jnp.int32)
    ids_a = (4 * placement_a[:, None] + jnp.arange(4, dtype=jnp.int32)[None, :]).reshape(-1)
    ids_b = members_b.reshape(-1)
    where_a = jnp.zeros((basic_count,), jnp.int32).at[ids_a].set(positions)
    where_b = jnp.zeros((basic_count,), jnp.int32).at[ids_b].set(positions)
    a_to_b = where_b[ids_a]
    b_to_a = where_a[ids_b]
    local_pos = lax.axis_index("cells") * per_device + jnp.arange(per_device, dtype=jnp.int32)
    local_a = ids_a[local_pos]
    local_b = ids_b[local_pos]
    shares = lax.axis_size("tgt")
    width_total = width_local * shares
    mass_a = jnp.log(source_mass.reshape(per_device, side_px * side_px))
    mass_b = route_rows(mass_a, b_to_a)
    log_marg = init_log.reshape(per_device, width_local) + math.log(side_px * side_px / width_total)
    for sweep_index in range(SWEEPS):
        if sweep_index % 2 == 0:
            sweep_ids, sweep_mass, send_map, take_map = (local_a, mass_a, a_to_b, b_to_a)
        else:
            sweep_ids, sweep_mass, send_map, take_map = (local_b, mass_b, b_to_a, a_to_b)
        col_height, col_across = target_coords(
            lax.axis_index("tgt") * width_local, width_local, width_total
        )
        log_marg = half_sweep(
            sweep_ids, sweep_mass, log_marg, side_px, block_rows, col_height, col_across
        )
        log_marg = route_rows(log_marg, take_map)
    return jnp.exp(log_marg).reshape(cell_count, 4, width_local)


def solution(mesh):
    placed = (P(), P(), P("cells", None), P("cells", None, "tgt"))
    return jax.shard_map(
        on_device, mesh=mesh, in_specs=placed, out_specs=P("cells", None, "tgt"), check_vma=False
    )
```

profile of v0, /device:TPU:1, one launch (start us, length us, event | category | flops | bytes accessed | tf_op | source)
XLA Modules:
  0.0 2224.2 jit_solution(10152851219377506119)
XLA Ops:
  9.5 62.5 %pmax.104 = f32[16,256]{1,0:T(8,128)S(1)} all-reduce(f32[16,256]{1,0:T(8,128)S(1)} %get-tuple-element.1857), channel_id=1, replica_groups=mesh['cells'=8,'tgt'=16] {'tgt'}, use_global_device_ids=true, to_apply=%region_6.7 | all-reduce | flops 4096 | bytes 32768 | tf_op jit(solution)/shard_map/pmax | solution.py:64
  78.0 55.9 %psum.104 = f32[16,256]{1,0:T(8,128)S(1)} all-reduce(f32[16,256]{1,0:T(8,128)S(1)} %get-tuple-element.1858), channel_id=1, replica_groups=mesh['cells'=8,'tgt'=16] {'tgt'}, use_global_device_ids=true, to_apply=%region_10.11 | all-reduce | flops 4096 | bytes 32768 | tf_op jit(solution)/shard_map/psum | solution.py:70
  147.3 55.6 %pmax.105 = f32[16,256]{1,0:T(8,128)S(1)} all-reduce(f32[16,256]{1,0:T(8,128)S(1)} %get-tuple-element.1860), channel_id=1, replica_groups=mesh['cells'=8,'tgt'=16] {'tgt'}, use_global_device_ids=true, to_apply=%region_18.19 | all-reduce | flops 4096 | bytes 32768 | tf_op jit(solution)/shard_map/pmax | solution.py:64
  209.3 55.6 %psum.105 = f32[16,256]{1,0:T(8,128)S(1)} all-reduce(f32[16,256]{1,0:T(8,128)S(1)} %get-tuple-element.1861), channel_id=1, replica_groups=mesh['cells'=8,'tgt'=16] {'tgt'}, use_global_device_ids=true, to_apply=%region_22.23 | all-reduce | flops 4096 | bytes 32768 | tf_op jit(solution)/shard_map/psum | solution.py:70
  278.2 55.6 %pmax.106 = f32[16,256]{1,0:T(8,128)S(1)} all-reduce(f32[16,256]{1,0:T(8,128)S(1)} %get-tuple-element.1863), channel_id=1, replica_groups=mesh['cells'=8,'tgt'=16] {'tgt'}, use_global_device_ids=true, to_apply=%region_30.31 | all-reduce | flops 4096 | bytes 32768 | tf_op jit(solution)/shard_map/pmax | solution.py:64
  340.2 55.9 %psum.106 = f32[16,256]{1,0:T(8,128)S(1)} all-reduce(f32[16,256]{1,0:T(8,128)S(1)} %get-tuple-element.1864), channel_id=1, replica_groups=mesh['cells'=8,'tgt'=16] {'tgt'}, use_global_device_ids=true, to_apply=%region_34.35 | all-reduce | flops 4096 | bytes 32768 | tf_op jit(solution)/shard_map/psum | solution.py:70
  414.5 55.8 %all-reduce.1 = (f32[16,256]{1,0:T(8,128)S(1)}, f32[16,256]{1,0:T(8,128)S(1)}) all-reduce(f32[16,256]{1,0:T(8,128)S(1)} %get-tuple-element.1866, f32[16,256]{1,0:T(8,128)S(1)} %get-tuple-element.1870), channel_id=1, replica_groups=mesh['cells'=8,'tgt'=16] {'tgt'}, use_global_device_ids=true, to_apply=%region_42.43 | all-reduce | flops 8192 | bytes 65536 | tf_op jit(solution)/shard_map/pmax | solution.py:64
  482.7 55.9 %all-reduce = (f32[16,256]{1,0:T(8,128)S(1)}, f32[16,256]{1,0:T(8,128)S(1)}) all-reduce(f32[16,256]{1,0:T(8,128)S(1)} %get-tuple-element.1867, f32[16,256]{1,0:T(8,128)S(1)} %get-tuple-element.1871), channel_id=1, replica_groups=mesh['cells'=8,'tgt'=16] {'tgt'}, use_global_device_ids=true, to_apply=%region_46.47 | all-reduce | flops 8192 | bytes 65536 | tf_op jit(solution)/shard_map/psum | solution.py:70
  558.3 124.4 %all_gather.16 = f32[512,128]{1,0:T(8,128)S(1)} all-gather(f32[64,128]{1,0:T(8,128)S(1)} %bitcast.631), channel_id=1, replica_groups=mesh['cells'=8,'tgt'=16] {'cells'}, dimensions={0}, use_global_device_ids=true | all-gather | bytes 294912 | tf_op jit(solution)/shard_map/all_gather | solution.py:52
  690.4 12.8 all_gather.15
  717.3 55.8 %pmax.109 = f32[16,256]{1,0:T(8,128)S(1)} all-reduce(f32[16,256]{1,0:T(8,128)S(1)} %get-tuple-element.1873), channel_id=1, replica_groups=mesh['cells'=8,'tgt'=16] {'tgt'}, use_global_device_ids=true, to_apply=%region_72.73 | all-reduce | flops 4096 | bytes 32768 | tf_op jit(solution)/shard_map/pmax | solution.py:64
  779.4 56.0 %psum.109 = f32[16,256]{1,0:T(8,128)S(1)} all-reduce(f32[16,256]{1,0:T(8,128)S(1)} %get-tuple-element.1874), channel_id=1, replica_groups=mesh['cells'=8,'tgt'=16] {'tgt'}, use_global_device_ids=true, to_apply=%region_76.77 | all-reduce | flops 4096 | bytes 32768 | tf_op jit(solution)/shard_map/psum | solution.py:70
  848.7 55.8 %pmax.110 = f32[16,256]{1,0:T(8,128)S(1)} all-reduce(f32[16,256]{1,0:T(8,128)S(1)} %get-tuple-element.1876), channel_id=1, replica_groups=mesh['cells'=8,'tgt'=16] {'tgt'}, use_global_device_ids=true, to_apply=%region_84.85 | all-reduce | flops 4096 | bytes 32768 | tf_op jit(solution)/shard_map/pmax | solution.py:64
  910.8 56.0 %psum.110 = f32[16,256]{1,0:T(8,128)S(1)} all-reduce(f32[16,256]{1,0:T(8,128)S(1)} %get-tuple-element.1877), channel_id=1, replica_groups=mesh['cells'=8,'tgt'=16] {'tgt'}, use_global_device_ids=true, to_apply=%region_88.89 | all-reduce | flops 4096 | bytes 32768 | tf_op jit(solution)/shard_map/psum | solution.py:70
  980.2 55.7 %pmax.111 = f32[16,256]{1,0:T(8,128)S(1)} all-reduce(f32[16,256]{1,0:T(8,128)S(1)} %get-tuple-element.1879), channel_id=1, replica_groups=mesh['cells'=8,'tgt'=16] {'tgt'}, use_global_device_ids=true, to_apply=%region_96.97 | all-reduce | flops 4096 | bytes 32768 | tf_op jit(solution)/shard_map/pmax | solution.py:64
  1042.2 56.2 %psum.111 = f32[16,256]{1,0:T(8,128)S(1)} all-reduce(f32[16,256]{1,0:T(8,128)S(1)} %get-tuple-element.1880), channel_id=1, replica_groups=mesh['cells'=8,'tgt'=16] {'tgt'}, use_global_device_ids=true, to_apply=%region_100.101 | all-reduce | flops 4096 | bytes 32768 | tf_op jit(solution)/shard_map/psum | solution.py:70
  1106.3 11.7 while.601
  1118.1 94.9 %all_gather.17 = f32[512,128]{1,0:T(8,128)S(1)} all-gather(f32[64,128]{1,0:T(8,128)S(1)} %bitcast.632), channel_id=1, replica_groups=mesh['cells'=8,'tgt'=16] {'cells'}, dimensions={0}, use_global_device_ids=true | all-gather | bytes 294912 | tf_op jit(solution)/shard_map/all_gather | solution.py:52
  1225.7 55.8 %pmax.112 = f32[16,256]{1,0:T(8,128)S(1)} all-reduce(f32[16,256]{1,0:T(8,128)S(1)} %get-tuple-element.1883), channel_id=1, replica_groups=mesh['cells'=8,'tgt'=16] {'tgt'}, use_global_device_ids=true, to_apply=%region_115.116 | all-reduce | flops 4096 | bytes 32768 | tf_op jit(solution)/shard_map/pmax | solution.py:64
  1287.9 55.8 %psum.112 = f32[16,256]{1,0:T(8,128)S(1)} all-reduce(f32[16,256]{1,0:T(8,128)S(1)} %get-tuple-element.1884), channel_id=1, replica_groups=mesh['cells'=8,'tgt'=16] {'tgt'}, use_global_device_ids=true, to_apply=%region_119.120 | all-reduce | flops 4096 | bytes 32768 | tf_op jit(solution)/shard_map/psum | solution.py:70
  1357.0 55.8 %pmax.113 = f32[16,256]{1,0:T(8,128)S(1)} all-reduce(f32[16,256]{1,0:T(8,128)S(1)} %get-tuple-element.1886), channel_id=1, replica_groups=mesh['cells'=8,'tgt'=16] {'tgt'}, use_global_device_ids=true, to_apply=%region_127.128 | all-reduce | flops 4096 | bytes 32768 | tf_op jit(solution)/shard_map/pmax | solution.py:64
  1419.1 56.0 %psum.113 = f32[16,256]{1,0:T(8,128)S(1)} all-reduce(f32[16,256]{1,0:T(8,128)S(1)} %get-tuple-element.1887), channel_id=1, replica_groups=mesh['cells'=8,'tgt'=16] {'tgt'}, use_global_device_ids=true, to_apply=%region_131.132 | all-reduce | flops 4096 | bytes 32768 | tf_op jit(solution)/shard_map/psum | solution.py:70
  1488.5 55.6 %pmax.114 = f32[16,256]{1,0:T(8,128)S(1)} all-reduce(f32[16,256]{1,0:T(8,128)S(1)} %get-tuple-element.1889), channel_id=1, replica_groups=mesh['cells'=8,'tgt'=16] {'tgt'}, use_global_device_ids=true, to_apply=%region_139.140 | all-reduce | flops 4096 | bytes 32768 | tf_op jit(solution)/shard_map/pmax | solution.py:64
  1550.5 56.2 %psum.114 = f32[16,256]{1,0:T(8,128)S(1)} all-reduce(f32[16,256]{1,0:T(8,128)S(1)} %get-tuple-element.1890), channel_id=1, replica_groups=mesh['cells'=8,'tgt'=16] {'tgt'}, use_global_device_ids=true, to_apply=%region_143.144 | all-reduce | flops 4096 | bytes 32768 | tf_op jit(solution)/shard_map/psum | solution.py:70
  1626.4 95.1 %all_gather.18 = f32[512,128]{1,0:T(8,128)S(1)} all-gather(f32[64,128]{1,0:T(8,128)S(1)} %bitcast.633), channel_id=1, replica_groups=mesh['cells'=8,'tgt'=16] {'cells'}, dimensions={0}, use_global_device_ids=true | all-gather | bytes 294912 | tf_op jit(solution)/shard_map/all_gather | solution.py:52
  1727.5 55.8 %pmax.115 = f32[16,256]{1,0:T(8,128)S(1)} all-reduce(f32[16,256]{1,0:T(8,128)S(1)} %get-tuple-element.1893), channel_id=1, replica_groups=mesh['cells'=8,'tgt'=16] {'tgt'}, use_global_device_ids=true, to_apply=%region_157.158 | all-reduce | flops 4096 | bytes 32768 | tf_op jit(solution)/shard_map/pmax | solution.py:64
  1789.6 55.8 %psum.115 = f32[16,256]{1,0:T(8,128)S(1)} all-reduce(f32[16,256]{1,0:T(8,128)S(1)} %get-tuple-element.1894), channel_id=1, replica_groups=mesh['cells'=8,'tgt'=16] {'tgt'}, use_global_device_ids=true, to_apply=%region_161.162 | all-reduce | flops 4096 | bytes 32768 | tf_op jit(solution)/shard_map/psum | solution.py:70
  1858.7 55.8 %pmax.116 = f32[16,256]{1,0:T(8,128)S(1)} all-reduce(f32[16,256]{1,0:T(8,128)S(1)} %get-tuple-element.1896), channel_id=1, replica_groups=mesh['cells'=8,'tgt'=16] {'tgt'}, use_global_device_ids=true, to_apply=%region_169.170 | all-reduce | flops 4096 | bytes 32768 | tf_op jit(solution)/shard_map/pmax | solution.py:64
  1920.9 56.0 %psum.116 = f32[16,256]{1,0:T(8,128)S(1)} all-reduce(f32[16,256]{1,0:T(8,128)S(1)} %get-tuple-element.1897), channel_id=1, replica_groups=mesh['cells'=8,'tgt'=16] {'tgt'}, use_global_device_ids=true, to_apply=%region_173.174 | all-reduce | flops 4096 | bytes 32768 | tf_op jit(solution)/shard_map/psum | solution.py:70
  1990.2 55.7 %pmax.117 = f32[16,256]{1,0:T(8,128)S(1)} all-reduce(f32[16,256]{1,0:T(8,128)S(1)} %get-tuple-element.1899), channel_id=1, replica_groups=mesh['cells'=8,'tgt'=16] {'tgt'}, use_global_device_ids=true, to_apply=%region_181.182 | all-reduce | flops 4096 | bytes 32768 | tf_op jit(solution)/shard_map/pmax | solution.py:64
  2052.2 56.2 %psum.117 = f32[16,256]{1,0:T(8,128)S(1)} all-reduce(f32[16,256]{1,0:T(8,128)S(1)} %get-tuple-element.1900), channel_id=1, replica_groups=mesh['cells'=8,'tgt'=16] {'tgt'}, use_global_device_ids=true, to_apply=%region_185.186 | all-reduce | flops 4096 | bytes 32768 | tf_op jit(solution)/shard_map/psum | solution.py:70
  2128.1 94.9 %all_gather.19 = f32[512,128]{1,0:T(8,128)S(1)} all-gather(f32[64,128]{1,0:T(8,128)S(1)} %bitcast.630), channel_id=1, replica_groups=mesh['cells'=8,'tgt'=16] {'cells'}, dimensions={0}, use_global_device_ids=true | all-gather | bytes 294912 | tf_op jit(solution)/shard_map/all_gather | solution.py:52
  (4799 shorter events, 621.3 us)
Async XLA Ops:
  0.0 0.7 copy-start.3
  2.0 0.7 copy-start.2
  78.0 55.9 %copy-start = (f32[16,256]{1,0:T(8,128)S(1)}, f32[16,256]{1,0:T(8,128)}, u32[]{:S(2)}) copy-start(f32[16,256]{1,0:T(8,128)} %param.98) | copy-start | bytes 49156
  133.9 7.9 copy-start.1
where the time goes:
time: 2230 us; the launch traced here: 2220 us
  blocking collectives  1880 us (84%)
  other arithmetic  228 us (10%)
  local copies, waits for them, and re-layouts  85.2 us (4%)
  loops' own time  29.8 us (1%)
    pmax x13, blocking collectives, row_reduce(): lax.pmax(lax.map(partial_peak, (height, across, dual_col)), 'tgt')  731 us
    psum x13, blocking collectives, row_reduce(): lax.psum(lax.map(partial_sum, (height, across, dual_col, top_score)), 'tgt')  727 us
    all_gather x5, blocking collectives, route_rows(): whole = lax.all_gather(row_data, 'cells', axis=0, tiled=True)  422 us
    reduce_sum x224, other arithmetic, partial_sum(): return jnp.sum(jnp.exp(scores - cell_data[3][:, None]), axis=1)  57 us
    reduce_sum x292, other arithmetic, log_sum(): jnp.sum(jnp.exp(values - top_score), axis=axis_number, keepdims=True)  55.2 us
    reduce_max x292, other arithmetic, log_sum(): top_score = jnp.max(values, axis=axis_number, keepdims=True)  52.6 us
    reduce_max x224, other arithmetic, partial_peak(): return jnp.max(scores_of(cell_data[0], cell_data[1], cell_data[2]), axis=1)  48.3 us

commit v1 on v0

v1 whole, which is shorter than its diff:
```python
import numpy as np
import ml_dtypes

import jax
import jax.numpy as jnp
from jax import lax
from jax.experimental import pallas as pl
from jax.experimental.pallas import tpu as pltpu
from jax.sharding import Mesh, PartitionSpec as P

F32 = jnp.float32
BF16 = jnp.bfloat16
W = 2048
NT = (((1,), (1,)), ((), ()))
CENTRE = 95


def _halves(matrix):
    high = matrix.astype(ml_dtypes.bfloat16)
    low = (matrix - high.astype(np.float64)).astype(ml_dtypes.bfloat16)
    return np.concatenate([high, low], axis=1)


def _tables():
    j = np.arange(W)
    yh = (j // 64 + 0.5) / 32 - 0.5
    ya = (j % 64 + 0.5) / 64 - 0.5
    r = np.arange(64)
    dh = (r // 8 - 3.5) / 128
    da = (r % 8 - 3.5) / 256
    basic = np.exp(400.0 * (yh[:, None] * dh[None] + ya[:, None] * da[None]))
    cell_da = np.concatenate([da + (k - 1.5) / 32 for k in range(4)])
    cell_dh = np.concatenate([dh] * 4)
    cell = np.exp(400.0 * (yh[:, None] * cell_dh[None] + ya[:, None] * cell_da[None]))
    return _halves(cell), _halves(basic)


def dot(a, b):
    return jnp.dot(a, b, preferred_element_type=F32)


def dot_nt(a, b):
    return lax.dot_general(a, b, NT, preferred_element_type=F32)


def split2(x):
    high = x.astype(BF16)
    return high, (x - high.astype(F32)).astype(BF16)


def split3(x):
    high = x.astype(BF16)
    rest = x - high.astype(F32)
    mid = rest.astype(BF16)
    return high, mid, (rest - mid.astype(F32)).astype(BF16)


def pick(onehot, x):
    o = onehot.astype(BF16)
    high, mid, low = split3(x)
    return (dot(o, high) + dot(o, mid)) + dot(o, low)


def pick2(onehot, x):
    o = onehot.astype(BF16)
    high, low = split2(x)
    return dot(o, high) + dot(o, low)


def targets(first, count):
    j = first + lax.broadcasted_iota(jnp.int32, (1, count), 1)
    yh = (lax.shift_right_logical(j, 6).astype(F32) + 0.5) / 32.0 - 0.5
    ya = (lax.bitwise_and(j, 63).astype(F32) + 0.5) / 64.0 - 0.5
    return yh, ya


def basic_centre(ids):
    row = jnp.floor(ids / 32.0)
    return (row * 8.0 + 4.0) / 128.0 - 0.5, ((ids - row * 32.0) * 8.0 + 4.0) / 256.0 - 0.5


def cell_centre(cells):
    row = jnp.floor(cells / 8.0)
    return (row * 8.0 + 4.0) / 128.0 - 0.5, ((cells - row * 8.0) * 32.0 + 16.0) / 256.0 - 0.5


def tilt(centre, y):
    return (400.0 * centre[0]) * y[0] + (400.0 * centre[1]) * y[1]


def eye_mask():
    return lax.broadcasted_iota(jnp.int32, (128, 128), 0) == lax.broadcasted_iota(jnp.int32, (128, 128), 1)


def to_col(row):
    return jnp.sum(jnp.where(eye_mask(), jnp.broadcast_to(row, (128, 128)), 0.0), axis=1, keepdims=True)


def to_row(col):
    return jnp.sum(jnp.where(eye_mask(), jnp.broadcast_to(col, (128, 128)), 0.0), axis=0, keepdims=True)


def local_cells(placement_row, core):
    dst = lax.broadcasted_iota(jnp.int32, (128, 128), 0)
    src = lax.broadcasted_iota(jnp.int32, (128, 128), 1)
    side = lax.bitwise_xor(lax.shift_right_logical(dst, 6), core)
    slot = lax.bitwise_and(lax.shift_right_logical(dst, 4), 3) * 32 + side * 16 + lax.bitwise_and(dst, 15)
    col = jnp.sum(jnp.where(slot == src, jnp.broadcast_to(placement_row, (128, 128)), 0.0), axis=1, keepdims=True)
    return col, to_row(col)


def own_ids(member_rows, group):
    lane = lax.broadcasted_iota(jnp.int32, (16, 128), 1)
    sub = lax.broadcasted_iota(jnp.int32, (16, 128), 0)
    k = lax.shift_right_logical(sub, 2)
    rows = jnp.zeros((16, 128), F32)
    for i in range(4):
        rows = jnp.where(k == i, jnp.broadcast_to(member_rows[i], (16, 128)), rows)
    return jnp.sum(jnp.where(lane == 4 * group + lax.bitwise_and(sub, 3), rows, 0.0), axis=1, keepdims=True)


def low_half(shape):
    return lax.broadcasted_iota(jnp.int32, shape, 1) < 64


def swap(x):
    return pltpu.roll(x, 64, 1)


def doubled(x, upper):
    mask = low_half(x.shape)
    return jnp.where(mask, swap(x), x) if upper else jnp.where(mask, x, swap(x))


def segment(x, k):
    y = jnp.where(k >= 2.0, x[:, 128:], x[:, :128])
    odd = (k == 1.0) | (k == 3.0)
    z = jnp.where(odd, swap(y), y)
    return jnp.where(low_half(z.shape), z, swap(z))


def cell_sums(u, cell_ref):
    n = u.shape[0]
    x = jnp.concatenate(split2(u), axis=0)
    p = dot(x, cell_ref[...])
    p = p[:n] + p[n:]
    return p[:, :256] + p[:, 256:]


def cell_cols(e, high, low):
    n = e.shape[0]
    eh, el = split2(e)
    p = dot_nt(jnp.concatenate([eh, el], axis=0), high)
    return p[:n] + p[n:] + dot_nt(eh, low)


def basic_sums(t, basic_ref):
    n = t.shape[0]
    p = dot(jnp.concatenate(split2(t), axis=0), basic_ref[...])
    p = p[:n] + p[n:]
    return p + swap(p)


def basic_cols(e, basic):
    n = e.shape[0]
    p = dot_nt(jnp.concatenate(split2(e), axis=0), basic)
    return p[:n] + p[n:]


def sweep_a(log_b, mass, centre, y, cell_ref):
    b = jnp.exp(log_b - jnp.max(log_b, axis=1, keepdims=True))
    high, low = cell_ref[:, :256], cell_ref[:, 256:]
    u = jnp.exp(-200.0 * ((centre[0] - y[0]) ** 2 + (centre[1] - y[1]) ** 2))
    for i in range(4):
        s = cell_sums(u, cell_ref)
        e = mass * (s[:, CENTRE : CENTRE + 1] / s)
        d = cell_cols(e, high, low)
        if i < 3:
            u = b / d
    return e, d


def over_k(x, op):
    y = op(x[:8], x[8:])
    return op(y, pltpu.roll(y, 4, 0))


def twice(x):
    return jnp.concatenate([x, x], axis=0)


def sweep_b(log_b, mass, centre, y, basic_ref):
    r = tilt(centre, y)
    top = 200.0 * (centre[0] * centre[0] + centre[1] * centre[1])
    t = jnp.exp(-200.0 * ((centre[0] - y[0]) ** 2 + (centre[1] - y[1]) ** 2))
    for i in range(4):
        e = mass / basic_sums(t, basic_ref)
        if i == 3:
            break
        d = basic_cols(e, basic_ref[...])
        q = r - top
        peak = over_k(q, jnp.maximum)
        z = over_k(jnp.exp(q - twice(peak)) * d, jnp.add)
        v = r + twice(log_b - peak - jnp.log(z))
        top = jnp.max(v, axis=1, keepdims=True)
        t = jnp.exp(v - top)
    return e, top


def solve_pair(log_b_a, mass_a, mass_b, ids, y, cell_ref, basic_ref, send_ref):
    k = ids - 4.0 * jnp.floor(ids / 4.0)
    at_cell = cell_centre(jnp.floor(ids / 4.0))
    at_basic = basic_centre(ids)
    e_a, d_a = sweep_a(log_b_a, mass_a, at_cell, y, cell_ref)
    e_first = segment(e_a, k)
    d_first = basic_cols(e_first, basic_ref[...])
    v = log_b_a - jnp.log(d_a) + (400.0 * (at_basic[1] - at_cell[1])) * y[1]
    peak = over_k(v, jnp.maximum)
    log_b_b = peak + jnp.log(over_k(jnp.exp(v - twice(peak)) * d_first, jnp.add))
    e_second, top = sweep_b(log_b_b, mass_b, at_basic, y, basic_ref)
    send_ref[0:16, :] = jnp.where(low_half((16, 128)), e_first, e_second)
    send_ref[16:32, :] = jnp.broadcast_to(top, (16, 128))


def member_rows_of(members_ref):
    members = members_ref[...].astype(F32)
    return [to_row(members[:, k : k + 1]) for k in range(4)]


def first_kernel(place_ref, placement_ref, members_ref, own_ref, other_ref, cell_ref, basic_ref,
                 send_ref, mass_a_ref, mass_b_ref):
    cell_col, cell_row = local_cells(placement_ref[...].astype(F32), place_ref[0])
    ids = own_ids(member_rows_of(members_ref), place_ref[1])
    onehot = jnp.where(cell_row == jnp.floor(ids / 4.0), 1.0, 0.0)
    log_b = []
    for t in range(16):
        rows = [ref[x * 16 + t, 0:16, :] for ref in (own_ref, other_ref) for x in range(4)]
        log_b.append(pick(onehot, jnp.concatenate(rows, axis=0)))
    log_b = jnp.concatenate(log_b, axis=1)
    mass = []
    for part in (16, 17):
        rows = jnp.concatenate([own_ref[:, part, :], other_ref[:, part, :]], axis=0)
        mass.append(pick(onehot, rows))
    mass_a = jnp.concatenate(mass, axis=1)
    mass_b = segment(mass_a, ids - 4.0 * jnp.floor(ids / 4.0))
    mass_a_ref[...] = mass_a
    mass_b_ref[...] = mass_b
    solve_pair(log_b, mass_a, mass_b, ids, targets(0, W), cell_ref, basic_ref, send_ref)


def received(recv_ref):
    factors, tops = [], []
    for k in range(4):
        factors.append(jnp.concatenate([recv_ref[g, 4 * k : 4 * k + 4, :] for g in range(32)], axis=0))
        tops.append(jnp.concatenate([recv_ref[g, 16 + 4 * k : 20 + 4 * k, :] for g in range(32)], axis=0))
    return factors, tops


def a_rows(member_rows, cell_col, k):
    want = 4.0 * cell_col + float(k)
    return [jnp.where(row == want, 1.0, 0.0) for row in member_rows]


def pick_parts(onehots, parts, exact):
    get = pick if exact else pick2
    total = get(onehots[0], parts[0])
    for o, p in zip(onehots[1:], parts[1:]):
        total = total + get(o, p)
    return total


def cell_factors(by_k, upper):
    mask = low_half(by_k[0].shape)
    if upper:
        return jnp.concatenate([jnp.where(mask, swap(by_k[i]), by_k[i + 1]) for i in (0, 2)], axis=1)
    return jnp.concatenate([jnp.where(mask, by_k[i], swap(by_k[i + 1])) for i in (0, 2)], axis=1)


def mix(v, d):
    peak = jnp.maximum(jnp.maximum(v[0], v[1]), jnp.maximum(v[2], v[3]))
    z = [jnp.exp(a - peak) * b for a, b in zip(v, d)]
    return peak + jnp.log((z[0] + z[1]) + (z[2] + z[3]))


def second_kernel(place_ref, placement_ref, members_ref, own_ref, other_ref, recv_ref, mass_a_ref, mass_b_ref,
                  cell_ref, basic_ref, send_ref, log_b_ref):
    cell_col, cell_row = local_cells(placement_ref[...].astype(F32), place_ref[0])
    member_rows = member_rows_of(members_ref)
    ids = own_ids(member_rows, place_ref[1])
    own_cells = jnp.floor(ids / 4.0)
    factors, tops = received(recv_ref)
    by_k = [pick_parts(a_rows(member_rows, cell_col, k), factors, False) for k in range(4)]
    e_cell = cell_factors(by_k, False)
    want = jnp.concatenate([4.0 * own_cells + float(k) for k in range(4)], axis=0)
    hits = [jnp.where(row == want, 1.0, 0.0) for row in member_rows]
    slot = (hits[0] + hits[1]) + (hits[2] + hits[3])
    near = [pick2(slot, f) for f in factors]
    near_top = [pick(slot, t)[:, :1] for t in tops]
    near_ids = [jnp.sum(slot * row, axis=1, keepdims=True) for row in member_rows]
    near_cell = [jnp.where(cell_row == jnp.floor(i / 4.0), 1.0, 0.0) for i in near_ids]
    at_near = [basic_centre(i) for i in near_ids]
    own_first = near_ids[0] == want
    own_factor, own_top = near[3], near_top[3]
    for k in range(3):
        same = near_ids[k] == want
        own_factor = jnp.where(same, near[k], own_factor)
        own_top = jnp.where(same, near_top[k], own_top)
    del own_first
    e0 = jnp.concatenate([doubled(f, False) for f in near], axis=0)
    e1 = jnp.concatenate([doubled(f, True) for f in near] + [doubled(own_factor, True)], axis=0)
    at_cell = cell_centre(cell_col)
    at_want = basic_centre(want)
    near_all = jnp.concatenate(near_cell, axis=0)
    for block in range(8):
        y = targets(block * 256, 256)
        lanes = []
        for t in (2 * block, 2 * block + 1):
            rows = [ref[x * 16 + t, 0:16, :] for ref in (own_ref, other_ref) for x in range(4)]
            lanes.append(jnp.concatenate(rows, axis=0))
        log_b0 = jnp.concatenate(lanes, axis=1)
        here = pl.ds(block * 256, 256)
        d_cell = cell_cols(e_cell, cell_ref[here, :256], cell_ref[here, 256:])
        gamma = log_b0 - jnp.log(d_cell) - tilt(at_cell, y)
        gamma = pick(near_all, gamma)
        basic = basic_ref[here, :]
        d0 = basic_cols(e0, basic)
        d1 = basic_cols(e1, basic)
        tilts = [tilt(c, y) for c in at_near]
        rows = [slice(64 * k, 64 * k + 64) for k in range(4)]
        log_b1 = mix([gamma[rows[k]] + tilts[k] for k in range(4)], [d0[rows[k]] for k in range(4)])
        gamma1 = log_b1 - mix([tilts[k] - near_top[k] for k in range(4)], [d1[rows[k]] for k in range(4)])
        v = gamma1 + tilt(at_want, y) - own_top
        d_own = d1[256:]
        log_b_ref[:, here] = mix([v[16 * k : 16 * k + 16] for k in range(4)],
                                 [d_own[16 * k : 16 * k + 16] for k in range(4)])
    solve_pair(log_b_ref[...], mass_a_ref[...], mass_b_ref[...], ids, targets(0, W), cell_ref, basic_ref, send_ref)


def third_kernel(place_ref, placement_ref, members_ref, own_ref, other_ref, first_ref, second_ref, cell_ref,
                 basic_ref, out_ref, keep_ref):
    cell_col, cell_row = local_cells(placement_ref[...].astype(F32), place_ref[0])
    member_rows = member_rows_of(members_ref)
    members = members_ref[...].astype(F32)
    share = place_ref[2]
    y = targets(share * 128, 128)
    here = pl.ds(pl.multiple_of(share * 128, 128), 128)
    high, low, basic = cell_ref[here, :256], cell_ref[here, 256:], basic_ref[here, :]
    rows = [ref[x * 16 + share, 0:16, :] for ref in (own_ref, other_ref) for x in range(4)]
    log_b = jnp.concatenate(rows, axis=0)
    at_cell = cell_centre(cell_col)
    tilt_cell = tilt(at_cell, y)
    b_ids = [members[:, k : k + 1] for k in range(4)]
    b_cell = jnp.concatenate([jnp.where(cell_row == jnp.floor(i / 4.0), 1.0, 0.0) for i in b_ids], axis=0)
    b_tilt = [tilt(basic_centre(i), y) for i in b_ids]
    a_hits = [a_rows(member_rows, cell_col, k) for k in range(4)]
    a_slot = [(h[0] + h[1]) + (h[2] + h[3]) for h in a_hits]
    a_tilt = [tilt(basic_centre(4.0 * cell_col + float(k)), y) for k in range(4)]
    parts = [slice(128 * k, 128 * k + 128) for k in range(4)]
    for turn, ref in enumerate((first_ref, second_ref)):
        factors, tops = received(ref)
        by_k = [pick_parts(a_hits[k], factors, False) for k in range(4)]
        d_cell = cell_cols(cell_factors(by_k, False), high, low)
        gamma = pick(b_cell, log_b - jnp.log(d_cell) - tilt_cell)
        d0 = basic_cols(jnp.concatenate([doubled(f, False) for f in factors], axis=0), basic)
        d1 = basic_cols(jnp.concatenate([doubled(f, True) for f in factors], axis=0), basic)
        log_b1 = mix([gamma[parts[k]] + b_tilt[k] for k in range(4)], [d0[parts[k]] for k in range(4)])
        gamma1 = log_b1 - mix([b_tilt[k] - tops[k] for k in range(4)], [d1[parts[k]] for k in range(4)])
        back = pick(jnp.concatenate(a_slot, axis=0), gamma1)
        da = basic_cols(jnp.concatenate([doubled(f, True) for f in by_k], axis=0), basic)
        a_top = [pick_parts(a_hits[k], tops, True) for k in range(4)]
        v = [back[parts[k]] + a_tilt[k] - a_top[k] for k in range(4)]
        if turn == 0:
            log_b = mix(v, [da[parts[k]] for k in range(4)])
        else:
            for k in range(4):
                keep_ref[k, :, :] = jnp.exp(v[k] + jnp.log(da[parts[k]]))
    mine = pl.ds(pl.multiple_of(place_ref[3] * 16, 16), 16)
    for k in range(4):
        out_ref[:, k, :] = keep_ref[k, mine, :]


def call(body, inputs, outs, scratch=()):
    spec = pl.BlockSpec(memory_space=pltpu.VMEM)
    return pl.pallas_call(
        body,
        out_shape=[jax.ShapeDtypeStruct(s, F32) for s in outs],
        in_specs=[pl.BlockSpec(memory_space=pltpu.SMEM)] + [spec] * (len(inputs) - 1),
        out_specs=[spec] * len(outs),
        scratch_shapes=list(scratch),
        compiler_params=pltpu.CompilerParams(vmem_limit_bytes=48 * 2**20),
    )(*inputs)


def on_device(placement_a, members_b, source_mass, init_log, cell, basic):
    x, c, z, y = (lax.axis_index(name) for name in ("x", "c", "z", "y"))
    share = z * 4 + y
    place = jnp.stack([c, x * 8 + c * 4 + y, share, x]).astype(jnp.int32)
    log_b = jax.nn.logsumexp(init_log, axis=1) + float(np.log(64.0 / W))
    mass = lax.dynamic_slice_in_dim(source_mass, share, 1, 0).reshape(2, 128)
    block = jnp.concatenate([log_b, mass], axis=0)
    own = lax.all_to_all(jnp.broadcast_to(block[None], (64, 18, 128)), ("x", "z", "y"), 0, 0, tiled=True)
    other = lax.ppermute(own, "c", [(0, 1), (1, 0)])
    placement = placement_a.reshape(1, 128)

    def exchange(rows):
        return lax.all_to_all(jnp.broadcast_to(rows[None], (32, 32, 128)), ("x", "c", "y"), 0, 0, tiled=True)

    common = (place, placement, members_b, own, other)
    send, mass_a, mass_b = call(first_kernel, common + (cell, basic), [(32, 128), (16, 256), (16, 128)])
    first = exchange(send)
    (send,) = call(second_kernel, common + (first, mass_a, mass_b, cell, basic), [(32, 128)],
                   [pltpu.VMEM((16, W), F32)])
    second = exchange(send)
    (out,) = call(third_kernel, common + (first, second, cell, basic), [(16, 4, 128)],
                  [pltpu.VMEM((4, 128, 128), F32)])
    return out


def solution(mesh):
    split = Mesh(mesh.devices.reshape(4, 2, 4, 4), ("x", "c", "z", "y"))
    cell, basic = _tables()
    placed = (P(), P(), P(("x", "c"), None), P(("x", "c"), None, ("z", "y")), P(), P())
    body = jax.shard_map(
        on_device, mesh=split, in_specs=placed, out_specs=P(("x", "c"), None, ("z", "y")), check_vma=False
    )

    def run(placement_a, members_b, source_mass, init_log):
        return body(placement_a, members_b, source_mass, init_log, jnp.asarray(cell), jnp.asarray(basic))

    return run
```

time: 2230 us -> 93 us (0.04)
  blocking collectives: 1880 us -> 55.8 us
  other arithmetic: 228 us -> 1.7 us
  local copies, waits for them, and re-layouts: 85.2 us -> 2.68 us
  loops' own time: 29.8 us -> 0 us
  Pallas kernels: 0 us -> 27.7 us
    pmax x13 -> x0, blocking collectives: 731 us -> none  [row_reduce(): lax.pmax(lax.map(partial_peak, (height, across, dual_col)), 'tgt')]
    psum x13 -> x0, blocking collectives: 727 us -> none  [row_reduce(): lax.psum(lax.map(partial_sum, (height, across, dual_col, top_score)), 'tgt')]
    all_gather x5 -> x0, blocking collectives: 422 us -> none  [route_rows(): whole = lax.all_gather(row_data, 'cells', axis=0, tiled=True)]
    reduce_sum x516 -> x1, other arithmetic: 112 us -> 0.79 us  [on_device(): log_b = jax.nn.logsumexp(init_log, axis=1) + float(np.log(64.0 / W))]
    reduce_max x516 -> x1, other arithmetic: 101 us -> 0.81 us  [on_device(): log_b = jax.nn.logsumexp(init_log, axis=1) + float(np.log(64.0 / W))]
    all_to_all x0 -> x3, blocking collectives: none -> 55.8 us  [the longest x2 29.9 us: exchange(): lax.all_to_all(jnp.broadcast_to(rows[None], (32, 32, 128)), ('x', 'c', 'y...]
    another operation x46 -> x0, loops' own time: 29.8 us -> none  [the longest x14 10.9 us: row_reduce(): lax.map(partial_sum, (height, across, dual_col, top_score))]
    pallas_call x0 -> x3, Pallas kernels: none -> 27.7 us  [call(): pl.pallas_call(body, out_shape=[jax.ShapeDtypeStruct(s, F32) for s in out...]
where the time goes in v1:
time: 93 us; the launch traced here: 92.6 us
  blocking collectives  55.8 us (60%)
  Pallas kernels  27.7 us (30%)
  starting transfers between devices  2.72 us (3%)
  local copies, waits for them, and re-layouts  2.68 us (3%)
  waiting for transfers between devices  1.78 us (2%)
  other arithmetic  1.7 us (2%)
    all_to_all x2, blocking collectives, exchange(): lax.all_to_all(jnp.broadcast_to(rows[None], (32, 32, 128)), ('x', 'c', 'y...  29.9 us
    pallas_call x3, Pallas kernels, call(): pl.pallas_call(body, out_shape=[jax.ShapeDtypeStruct(s, F32) for s in out...  27.7 us
    all_to_all x1, blocking collectives, on_device(): lax.all_to_all(jnp.broadcast_to(block[None], (64, 18, 128)), ('x', 'z', '...  26 us
    ppermute x1, starting transfers between devices, on_device(): other = lax.ppermute(own, 'c', [(0, 1), (1, 0)])  2.72 us
  transfers between devices with their start and end apart: 1, of which 1 were waited for; matrix products, arithmetic and copies ran while one was open for 0% of the time, Pallas kernels for 0%

profile of v1, /device:TPU:1, one launch (start us, length us, event | category | flops | bytes accessed | tf_op | source)
XLA Modules:
  0.0 92.6 jit_solution(7999468928291821347)
XLA Ops:
  0.0 0.0 copy-start
  0.0 0.0 copy-start.4
  0.0 0.8 reduce_max.9
  0.8 0.8 exponential_reduce_fusion
  1.6 0.0 copy-done
  1.7 0.1 broadcast_in_dim.9
  1.7 0.0 copy-start.1
  1.8 0.0 copy-start.2
  1.8 0.0 copy-start.3
  1.8 26.0 %all_to_all.15.own_ref = f32[64,18,128]{2,1,0:T(8,128)S(1)} all-to-all(f32[64,18,128]{2,1,0:T(8,128)S(1)} %broadcast_in_dim.9), channel_id=1, replica_groups=mesh['x'=4,'c'=2,'z'=4,'y'=4] {'x','z','y'}, dimensions={0} | all-to-all | bytes 1179648 | tf_op jit(solution)/shard_map/all_to_all | solution.py:401
  27.8 0.9 copy.10
  28.7 2.7 %collective-permute-start = (f32[64,18,128]{2,0,1:T(8,128)}, f32[64,18,128]{2,0,1:T(8,128)}, u32[]{:S(2)}, u32[]{:S(2)}) collective-permute-start(f32[64,18,128]{2,0,1:T(8,128)} %copy.10), channel_id=1, source_target_pairs={{0,16},{16,0},{1,17},{17,1},{2,18},{18,2},{3,19},{19,3},{4,20},{20... | collective-permute-start | bytes 1769480 | tf_op jit(solution)/shard_map/ppermute | solution.py:402
  31.4 0.0 copy-done.4
  31.4 0.1 copy.15.members_ref
  31.5 0.1 pad_add_fusion.place_ref
  31.6 1.8 %collective-permute-done = f32[64,18,128]{2,0,1:T(8,128)} collective-permute-done((f32[64,18,128]{2,0,1:T(8,128)}, f32[64,18,128]{2,0,1:T(8,128)}, u32[]{:S(2)}, u32[]{:S(2)}) %collective-permute-start) | collective-permute-done | bytes 589856 | tf_op jit(solution)/shard_map/ppermute | solution.py:402
  33.4 1.4 %copy.16.other_ref = f32[64,18,128]{2,1,0:T(8,128)S(1)} copy(f32[64,18,128]{2,0,1:T(8,128)} %collective-permute-done) | data formatting | bytes 1179648 | tf_op jit(solution)/shard_map/ppermute | solution.py:402
  34.8 0.0 copy-done.1
  34.8 0.0 copy-done.2
  34.8 0.0 copy-done.3
  34.8 9.3 %shard_map.64 = (f32[32,128]{1,0:T(8,128)S(1)}, f32[16,256]{1,0:T(8,128)S(1)}, f32[16,128]{1,0:T(8,128)S(1)}) custom-call(s32[4]{0:T(128)S(1)} %pad_add_fusion.place_ref, s32[1,128]{1,0:T(1,128)S(1)} %bitcast.6, s32[128,4]{1,0:T(8,128)S(1)} %copy.15.members_ref, f32[64,18,128]{2,1,0:T(8,128)S(1)} %all_to_all.15.own_ref, f32[64,18,128]{2,1,0:T(8,128)S(1)} %copy.16.other_ref, ...), custom_call_target="tpu_custom_call" | custom-call | tf_op jit(solution)/shard_map/pallas_call | solution.py:384
  44.1 0.1 broadcast_in_dim.10
  44.2 14.5 %all_to_all.16.recv_ref.first_ref = f32[32,32,128]{2,1,0:T(8,128)S(1)} all-to-all(f32[32,32,128]{2,1,0:T(8,128)S(1)} %broadcast_in_dim.10), channel_id=1, replica_groups=mesh['x'=4,'c'=2,'z'=4,'y'=4] {'x','c','y'}, dimensions={0} | all-to-all | bytes 1048576 | tf_op jit(solution)/shard_map/all_to_all | solution.py:406
  58.7 13.4 %shard_map.65 = f32[32,128]{1,0:T(8,128)S(1)} custom-call(s32[4]{0:T(128)S(1)} %pad_add_fusion.place_ref, s32[1,128]{1,0:T(1,128)S(1)} %bitcast.7, s32[128,4]{1,0:T(8,128)S(1)} %copy.15.members_ref, f32[64,18,128]{2,1,0:T(8,128)S(1)} %all_to_all.15.own_ref, f32[64,18,128]{2,1,0:T(8,128)S(1)} %copy.16.other_ref, ...), custom_call_target="tpu_custom_call" | custom-call | tf_op jit(solution)/shard_map/pallas_call | solution.py:384
  72.0 0.1 broadcast_in_dim.11
  72.1 15.4 %all_to_all.17.second_ref = f32[32,32,128]{2,1,0:T(8,128)S(1)} all-to-all(f32[32,32,128]{2,1,0:T(8,128)S(1)} %broadcast_in_dim.11), channel_id=1, replica_groups=mesh['x'=4,'c'=2,'z'=4,'y'=4] {'x','c','y'}, dimensions={0} | all-to-all | bytes 1048576 | tf_op jit(solution)/shard_map/all_to_all | solution.py:406
  87.5 5.1 %shard_map.66 = f32[16,4,128]{2,1,0:T(4,128)} custom-call(s32[4]{0:T(128)S(1)} %pad_add_fusion.place_ref, s32[1,128]{1,0:T(1,128)S(1)} %bitcast.8, s32[128,4]{1,0:T(8,128)S(1)} %copy.15.members_ref, f32[64,18,128]{2,1,0:T(8,128)S(1)} %all_to_all.15.own_ref, f32[64,18,128]{2,1,0:T(8,128)S(1)} %copy.16.other_ref, ...), custom_call_target="tpu_custom_call" | custom-call | tf_op jit(solution)/shard_map/pallas_call | solution.py:384
  (4 shorter events, 0.0 us)
Async XLA Ops:
  0.0 1.6 %copy-start = (f32[16,256]{1,0:T(8,128)S(1)}, f32[16,256]{1,0:T(8,128)}, u32[]{:S(2)}) copy-start(f32[16,256]{1,0:T(8,128)} %param.8) | copy-start | bytes 49156
  0.0 31.4 %copy-start.4 = (s32[128,4]{0,1:T(4,128)S(1)}, s32[128,4]{0,1:T(4,128)}, u32[]{:S(2)}) copy-start(s32[128,4]{0,1:T(4,128)} %param.7) | copy-start | bytes 6148
  1.7 33.1 %copy-start.1 = (bf16[2048,512]{1,0:T(8,128)(2,1)S(1)}, bf16[2048,512]{1,0:T(8,128)(2,1)}, u32[]{:S(2)}) copy-start(bf16[2048,512]{1,0:T(8,128)(2,1)} %constant.37.clone.cell_ref) | copy-start | bytes 6291460
  1.8 33.1 %copy-start.2 = (bf16[2048,128]{1,0:T(8,128)(2,1)S(1)}, bf16[2048,128]{1,0:T(8,128)(2,1)}, u32[]{:S(2)}) copy-start(bf16[2048,128]{1,0:T(8,128)(2,1)} %constant.38.clone.basic_ref) | copy-start | bytes 1572868
  1.8 33.1 %copy-start.3 = (s32[128]{0:T(128)S(1)}, s32[128]{0:T(128)}, u32[]{:S(2)}) copy-start(s32[128]{0:T(128)} %param.6) | copy-start | bytes 1540
  28.7 4.7 %collective-permute-start = (f32[64,18,128]{2,0,1:T(8,128)}, f32[64,18,128]{2,0,1:T(8,128)}, u32[]{:S(2)}, u32[]{:S(2)}) collective-permute-start(f32[64,18,128]{2,0,1:T(8,128)} %copy.10), channel_id=1, source_target_pairs={{0,16},{16,0},{1,17},{17,1},{2,18},{18,2},{3,19},{19,3},{4,20},{20... | collective-permute-start | bytes 1769480 | tf_op jit(solution)/shard_map/ppermute | solution.py:402

commit v2 on v1

v2 whole, which is shorter than its diff:
```python
import numpy as np
import ml_dtypes

import jax
import jax.numpy as jnp
from jax import lax
from jax.experimental import pallas as pl
from jax.experimental.pallas import tpu as pltpu
from jax.sharding import Mesh, PartitionSpec as P

F32 = jnp.float32
BF16 = jnp.bfloat16
W = 2048
CENTRE = 128 + 31


def _halves(matrix):
    high = matrix.astype(ml_dtypes.bfloat16)
    low = (matrix - high.astype(np.float64)).astype(ml_dtypes.bfloat16)
    return high, low


def _thrice(matrix):
    high, low = _halves(matrix)
    return np.concatenate([high, high, low], axis=0)


def _tables():
    yh = (np.arange(32) + 0.5) / 32 - 0.5
    ya = (np.arange(64) + 0.5) / 64 - 0.5
    dh = (np.arange(8) - 3.5) / 128
    da = (np.arange(8) - 3.5) / 256
    shifts = [(k - 1.5) / 32 for k in range(4)]

    def whole(shift):
        up = np.exp(400.0 * dh[:, None] * yh[None])
        along = np.exp(400.0 * (da + shift)[:, None] * ya[None])
        return (up[:, None, :, None] * along[None, :, None, :]).reshape(64, W)

    def along(shift):
        part = np.zeros((2, 64, 2, 8, 8))
        for h in range(2):
            part[h, :, h] = np.exp(400.0 * ya[:, None] * (da + shift)[None])[:, None, :]
        return part.reshape(128, 128)

    cells = [along(s) for s in shifts]
    factors = [_thrice(m) for m in cells] + [_thrice(np.concatenate([m.T for m in cells], axis=0))]
    factors += [_thrice(along(0.0)), _thrice(along(0.0).T)]
    wholes = _halves(np.concatenate([whole(s) for s in shifts], axis=0)) + _halves(whole(0.0))
    return np.concatenate(factors, axis=0), np.concatenate(wholes, axis=0)


CELL, BACK, BASIC, BASIC_BACK = 0, 1536, 3072, 3456


def dot(a, b):
    return jnp.dot(a, b, preferred_element_type=F32)


def split2(x):
    high = x.astype(BF16)
    return high, (x - high.astype(F32)).astype(BF16)


def split3(x):
    high = x.astype(BF16)
    rest = x - high.astype(F32)
    mid = rest.astype(BF16)
    return high, mid, (rest - mid.astype(F32)).astype(BF16)


def pick(onehot, x):
    o = onehot.astype(BF16)
    high, mid, low = split3(x)
    return (dot(o, high) + dot(o, mid)) + dot(o, low)


def targets(first, count):
    j = first + lax.broadcasted_iota(jnp.int32, (1, count), 1)
    yh = (lax.shift_right_logical(j, 6).astype(F32) + 0.5) / 32.0 - 0.5
    ya = (lax.bitwise_and(j, 63).astype(F32) + 0.5) / 64.0 - 0.5
    return yh, ya


def basic_centre(ids):
    row = jnp.floor(ids / 32.0)
    return (row * 8.0 + 4.0) / 128.0 - 0.5, ((ids - row * 32.0) * 8.0 + 4.0) / 256.0 - 0.5


def cell_centre(cells):
    row = jnp.floor(cells / 8.0)
    return (row * 8.0 + 4.0) / 128.0 - 0.5, ((cells - row * 8.0) * 32.0 + 16.0) / 256.0 - 0.5


def tilt(centre, y):
    return (400.0 * centre[0]) * y[0] + (400.0 * centre[1]) * y[1]


def eye_mask():
    return lax.broadcasted_iota(jnp.int32, (128, 128), 0) == lax.broadcasted_iota(jnp.int32, (128, 128), 1)


def to_col(row):
    return jnp.sum(jnp.where(eye_mask(), jnp.broadcast_to(row, (128, 128)), 0.0), axis=1, keepdims=True)


def to_row(col):
    return jnp.sum(jnp.where(eye_mask(), jnp.broadcast_to(col, (128, 128)), 0.0), axis=0, keepdims=True)


def local_cells(placement_row, core):
    dst = lax.broadcasted_iota(jnp.int32, (128, 128), 0)
    src = lax.broadcasted_iota(jnp.int32, (128, 128), 1)
    side = lax.bitwise_xor(lax.shift_right_logical(dst, 6), core)
    slot = lax.bitwise_and(lax.shift_right_logical(dst, 4), 3) * 32 + side * 16 + lax.bitwise_and(dst, 15)
    col = jnp.sum(jnp.where(slot == src, jnp.broadcast_to(placement_row, (128, 128)), 0.0), axis=1, keepdims=True)
    return col, to_row(col)


def own_ids(member_rows, group):
    lane = lax.broadcasted_iota(jnp.int32, (16, 128), 1)
    sub = lax.broadcasted_iota(jnp.int32, (16, 128), 0)
    k = lax.shift_right_logical(sub, 2)
    rows = jnp.zeros((16, 128), F32)
    for i in range(4):
        rows = jnp.where(k == i, jnp.broadcast_to(member_rows[i], (16, 128)), rows)
    return jnp.sum(jnp.where(lane == 4 * group + lax.bitwise_and(sub, 3), rows, 0.0), axis=1, keepdims=True)


def low_half(shape):
    return lax.broadcasted_iota(jnp.int32, shape, 1) < 64


def swap(x):
    return pltpu.roll(x, 64, 1)


def doubled(x, upper):
    mask = low_half(x.shape)
    return jnp.where(mask, swap(x), x) if upper else jnp.where(mask, x, swap(x))


def segment(x, k):
    y = jnp.where(k >= 2.0, x[:, 256:], x[:, :256])
    return jnp.where((k == 1.0) | (k == 3.0), y[:, 128:], y[:, :128])


def quadrupled(x):
    return jnp.concatenate([doubled(x[:, :128], False), doubled(x[:, :128], True),
                            doubled(x[:, 128:], False), doubled(x[:, 128:], True)], axis=1)


def thrice(x):
    high, low = split2(x)
    return jnp.concatenate([high, low, high], axis=1)


def up_rows():
    lane = lax.broadcasted_iota(jnp.int32, (16, 128), 1)
    row = 2 * lax.broadcasted_iota(jnp.int32, (16, 128), 0) + lax.shift_right_logical(lane, 6)
    yh = (row.astype(F32) + 0.5) / 32.0 - 0.5
    dh = (lax.bitwise_and(lax.shift_right_logical(lane, 3), 7).astype(F32) - 3.5) / 128.0
    up = jnp.exp(400.0 * yh * dh)
    return [up[t : t + 1, :] for t in range(16)]


def sums(u, factor_ref, up, cells):
    n = u.shape[0]
    x = thrice(jnp.concatenate([u[:, 128 * t : 128 * t + 128] for t in range(16)], axis=0))
    out = []
    for first in [CELL + 384 * k for k in range(4)] if cells else [BASIC]:
        p = dot(x, factor_ref[first : first + 384, :])
        parts = [p[n * t : n * t + n] * h for t, h in enumerate(up)]
        while len(parts) > 1:
            parts = [parts[i] + parts[i + 1] for i in range(0, len(parts), 2)]
        out.append(parts[0] + swap(parts[0]))
    return jnp.concatenate(out, axis=1)


def cols(e, factor_ref, up):
    n, groups = e.shape[0], e.shape[1] // 128
    x = jnp.concatenate([e * jnp.concatenate([h] * groups, axis=1) for h in up], axis=0)
    d = dot(thrice(x), factor_ref[BACK : BACK + 1536, :] if groups == 4 else factor_ref[BASIC_BACK : BASIC_BACK + 384, :])
    return jnp.concatenate([d[n * t : n * t + n] for t in range(16)], axis=1)


def cell_cols(e, whole):
    n = e.shape[0]
    eh, el = split2(e)
    p = dot(jnp.concatenate([eh, el], axis=0), whole[:256])
    return p[:n] + p[n:] + dot(eh, whole[256:512])


def basic_cols(e, whole):
    n = e.shape[0]
    p = dot(jnp.concatenate(split2(e), axis=0), whole[512:])
    return p[:n] + p[n:]


def nearness(centre, y):
    return jnp.exp(-200.0 * ((centre[0] - y[0]) ** 2 + (centre[1] - y[1]) ** 2))


def balanced(mass, s):
    return mass * (s[:, CENTRE : CENTRE + 1] / s)


def sweep_a(log_b, mass, d, factor_ref, up):
    b = jnp.exp(log_b - jnp.max(log_b, axis=1, keepdims=True))
    for _ in range(3):
        e = balanced(mass, sums(b / d, factor_ref, up, True))
        d = cols(e, factor_ref, up)
    return e, d


def over_k(x, op):
    y = op(x[:8], x[8:])
    return op(y, pltpu.roll(y, 4, 0))


def twice(x):
    return jnp.concatenate([x, x], axis=0)


def column_part(r, top, d):
    q = r - top
    peak = over_k(q, jnp.maximum)
    return peak + jnp.log(over_k(jnp.exp(q - twice(peak)) * d, jnp.add))


def sweep_b(log_b, mass, r, part, factor_ref, up):
    for i in range(3):
        v = r + twice(log_b - part)
        top = jnp.max(v, axis=1, keepdims=True)
        e = mass / sums(jnp.exp(v - top), factor_ref, up, False)
        if i < 2:
            part = column_part(r, top, cols(e, factor_ref, up))
    return e, top


def solve_pair(log_b_a, mass_a, mass_b, ids, d, part, factor_ref, up, send_ref):
    y = targets(0, W)
    k = ids - 4.0 * jnp.floor(ids / 4.0)
    at_cell = cell_centre(jnp.floor(ids / 4.0))
    at_basic = basic_centre(ids)
    e_a, d_a = sweep_a(log_b_a, mass_a, d, factor_ref, up)
    e_first = segment(e_a, k)
    d_first = cols(e_first, factor_ref, up)
    v = log_b_a - jnp.log(d_a) + (400.0 * (at_basic[1] - at_cell[1])) * y[1]
    peak = over_k(v, jnp.maximum)
    log_b_b = peak + jnp.log(over_k(jnp.exp(v - twice(peak)) * d_first, jnp.add))
    e_second, top = sweep_b(log_b_b, mass_b, tilt(at_basic, y), part, factor_ref, up)
    rows = jnp.where(low_half((16, 128)), e_first, jnp.log(e_second) - top)
    for i in range(32):
        send_ref[i, :, :] = rows


def member_rows_of(members_ref):
    members = members_ref[...].astype(F32)
    return [to_row(members[:, k : k + 1]) for k in range(4)]


def block_kernel(place_ref, init_hbm, mass_hbm, block_ref, init_ref, mass_ref, sems):
    copies = [pltpu.make_async_copy(init_hbm, init_ref, sems.at[0]), pltpu.make_async_copy(mass_hbm, mass_ref, sems.at[1])]
    for copy in copies:
        copy.start()
    for copy in copies:
        copy.wait()
    x = [init_ref[:, k, :] for k in range(4)]
    peak = jnp.maximum(jnp.maximum(x[0], x[1]), jnp.maximum(x[2], x[3]))
    z = [jnp.exp(a - peak) for a in x]
    log_b = peak + jnp.log((z[0] + z[1]) + (z[2] + z[3])) + float(np.log(64.0 / W))
    row = mass_ref[pl.ds(place_ref[2], 1), :]
    mass = jnp.concatenate([row[:, :128], row[:, 128:]] + [jnp.zeros((6, 128), F32)], axis=0)
    block = jnp.concatenate([log_b, mass], axis=0)
    for i in range(64):
        block_ref[i, :, :] = block


def start_kernel(place_ref, placement_ref, members_ref, factor_ref, sum_a_ref, sum_b_ref, keep_ref):
    ids = own_ids(member_rows_of(members_ref), place_ref[1])
    y = targets(0, W)
    up = up_rows()
    sum_a_ref[...] = sums(nearness(cell_centre(jnp.floor(ids / 4.0)), y), factor_ref, up, True)
    sum_b_ref[...] = sums(nearness(basic_centre(ids), y), factor_ref, up, False)
    keep_ref[...] = factor_ref[...]


def first_kernel(place_ref, placement_ref, members_ref, own_ref, other_ref, sum_a_ref, sum_b_ref, factor_ref,
                 send_ref, table_ref, mass_a_ref, mass_b_ref, d_ref, part_ref):
    cell_col, cell_row = local_cells(placement_ref[...].astype(F32), place_ref[0])
    ids = own_ids(member_rows_of(members_ref), place_ref[1])
    up = up_rows()
    onehot = jnp.where(cell_row == jnp.floor(ids / 4.0), 1.0, 0.0)
    mass = []
    for part in (16, 17):
        rows = jnp.concatenate([own_ref[:, part, :], other_ref[:, part, :]], axis=0)
        mass.append(pick(onehot, rows))
    mass_a = quadrupled(jnp.concatenate(mass, axis=1))
    mass_b = segment(mass_a, ids - 4.0 * jnp.floor(ids / 4.0))
    d = cols(balanced(mass_a, sum_a_ref[...]), factor_ref, up)
    log_b = []
    for t in range(16):
        rows = [ref[x * 16 + t, 0:16, :] for ref in (own_ref, other_ref) for x in range(4)]
        rows = jnp.concatenate(rows, axis=0)
        table_ref[:, 128 * t : 128 * t + 128] = rows
        log_b.append(pick(onehot, rows))
    log_b = jnp.concatenate(log_b, axis=1)
    at_basic = basic_centre(ids)
    top = 200.0 * (at_basic[0] * at_basic[0] + at_basic[1] * at_basic[1])
    part = column_part(tilt(at_basic, targets(0, W)), top, cols(mass_b / sum_b_ref[...], factor_ref, up))
    mass_a_ref[...] = mass_a
    mass_b_ref[...] = mass_b
    d_ref[...] = d
    part_ref[...] = part
    solve_pair(log_b, mass_a, mass_b, ids, d, part, factor_ref, up, send_ref)


def received(recv_ref):
    return [jnp.concatenate([recv_ref[g, 4 * k : 4 * k + 4, :] for g in range(32)], axis=0) for k in range(4)]


def high_top(x):
    return jnp.max(jnp.where(low_half(x.shape), -jnp.inf, x), axis=1, keepdims=True)


def unpack(factors):
    tops = [-high_top(f) for f in factors]
    return ([doubled(f, False) for f in factors],
            [jnp.exp(doubled(f, True) + t) for f, t in zip(factors, tops)], tops)


def a_rows(member_rows, cell_col, k):
    want = 4.0 * cell_col + float(k)
    return [jnp.where(row == want, 1.0, 0.0) for row in member_rows]


def pick_parts(onehots, parts):
    total = pick(onehots[0], parts[0])
    for o, p in zip(onehots[1:], parts[1:]):
        total = total + pick(o, p)
    return total


def cell_factors(by_k):
    mask = low_half(by_k[0].shape)
    return jnp.concatenate([jnp.where(mask, by_k[i], swap(by_k[i + 1])) for i in (0, 2)], axis=1)


def mix(v, d):
    peak = jnp.maximum(jnp.maximum(v[0], v[1]), jnp.maximum(v[2], v[3]))
    z = [jnp.exp(a - peak) * b for a, b in zip(v, d)]
    return peak + jnp.log((z[0] + z[1]) + (z[2] + z[3]))


def second_kernel(place_ref, placement_ref, members_ref, recv_ref, table_ref, mass_a_ref, mass_b_ref, d_ref, part_ref,
                  factor_ref, whole_ref, send_ref, here_ref, log_b_ref):
    here_ref[...] = table_ref[:, pl.ds(pl.multiple_of(place_ref[2] * 128, 128), 128)]
    cell_col, cell_row = local_cells(placement_ref[...].astype(F32), place_ref[0])
    member_rows = member_rows_of(members_ref)
    ids = own_ids(member_rows, place_ref[1])
    own_cells = jnp.floor(ids / 4.0)
    factors = received(recv_ref)
    e_cell = cell_factors([pick_parts(a_rows(member_rows, cell_col, k), factors) for k in range(4)])
    want = jnp.concatenate([4.0 * own_cells + float(k) for k in range(4)], axis=0)
    hits = [jnp.where(row == want, 1.0, 0.0) for row in member_rows]
    slot = (hits[0] + hits[1]) + (hits[2] + hits[3])
    near = [pick(slot, f) for f in factors]
    near_ids = [jnp.sum(slot * row, axis=1, keepdims=True) for row in member_rows]
    near_cell = [jnp.where(cell_row == jnp.floor(i / 4.0), 1.0, 0.0) for i in near_ids]
    at_near = [basic_centre(i) for i in near_ids]
    e0, e1, tops = unpack(near)
    own_factor, own_top = e1[3], tops[3]
    for k in range(3):
        same = near_ids[k] == want
        own_factor = jnp.where(same, e1[k], own_factor)
        own_top = jnp.where(same, tops[k], own_top)
    e0 = jnp.concatenate(e0, axis=0)
    e1 = jnp.concatenate(e1 + [own_factor], axis=0)
    at_cell = cell_centre(cell_col)
    at_want = basic_centre(want)
    near_all = jnp.concatenate(near_cell, axis=0)
    for block in range(8):
        y = targets(block * 256, 256)
        here = pl.ds(block * 256, 256)
        whole = whole_ref[:, here]
        d_cell = cell_cols(e_cell, whole)
        gamma = pick(near_all, table_ref[:, here] - jnp.log(d_cell) - tilt(at_cell, y))
        d0 = basic_cols(e0, whole)
        d1 = basic_cols(e1, whole)
        tilts = [tilt(c, y) for c in at_near]
        rows = [slice(64 * k, 64 * k + 64) for k in range(4)]
        log_b1 = mix([gamma[rows[k]] + tilts[k] for k in range(4)], [d0[rows[k]] for k in range(4)])
        gamma1 = log_b1 - mix([tilts[k] - tops[k] for k in range(4)], [d1[rows[k]] for k in range(4)])
        v = gamma1 + tilt(at_want, y) - own_top
        d_own = d1[256:]
        log_b_ref[:, here] = mix([v[16 * k : 16 * k + 16] for k in range(4)],
                                 [d_own[16 * k : 16 * k + 16] for k in range(4)])
    solve_pair(log_b_ref[...], mass_a_ref[...], mass_b_ref[...], ids, d_ref[...], part_ref[...],
               factor_ref, up_rows(), send_ref)


def local_turn(place_ref, placement_ref, members_ref, recv_ref, whole_ref, log_b):
    cell_col, cell_row = local_cells(placement_ref[...].astype(F32), place_ref[0])
    member_rows = member_rows_of(members_ref)
    members = members_ref[...].astype(F32)
    share = place_ref[2]
    y = targets(share * 128, 128)
    here = pl.ds(pl.multiple_of(share * 128, 128), 128)
    whole = whole_ref[:, here]
    b_ids = [members[:, k : k + 1] for k in range(4)]
    b_cell = jnp.concatenate([jnp.where(cell_row == jnp.floor(i / 4.0), 1.0, 0.0) for i in b_ids], axis=0)
    b_tilt = [tilt(basic_centre(i), y) for i in b_ids]
    a_hits = [a_rows(member_rows, cell_col, k) for k in range(4)]
    a_slot = jnp.concatenate([(h[0] + h[1]) + (h[2] + h[3]) for h in a_hits], axis=0)
    a_tilt = [tilt(basic_centre(4.0 * cell_col + float(k)), y) for k in range(4)]
    parts = [slice(128 * k, 128 * k + 128) for k in range(4)]
    factors = received(recv_ref)
    by_k = [pick_parts(a_hits[k], factors) for k in range(4)]
    d_cell = cell_cols(cell_factors(by_k), whole)
    gamma = pick(b_cell, log_b - jnp.log(d_cell) - tilt(cell_centre(cell_col), y))
    e0, e1, tops = unpack(factors)
    _, ea, a_tops = unpack(by_k)
    d0 = basic_cols(jnp.concatenate(e0, axis=0), whole)
    d1 = basic_cols(jnp.concatenate(e1, axis=0), whole)
    da = basic_cols(jnp.concatenate(ea, axis=0), whole)
    log_b1 = mix([gamma[parts[k]] + b_tilt[k] for k in range(4)], [d0[parts[k]] for k in range(4)])
    gamma1 = log_b1 - mix([b_tilt[k] - tops[k] for k in range(4)], [d1[parts[k]] for k in range(4)])
    back = pick(a_slot, gamma1)
    return [back[parts[k]] + a_tilt[k] - a_tops[k] for k in range(4)], [da[parts[k]] for k in range(4)]


def middle_kernel(place_ref, placement_ref, members_ref, here_ref, recv_ref, whole_ref, log_b_ref):
    log_b_ref[...] = mix(*local_turn(place_ref, placement_ref, members_ref, recv_ref, whole_ref, here_ref[...]))


def last_kernel(place_ref, placement_ref, members_ref, log_b_ref, recv_ref, whole_ref, out_ref, keep_ref):
    v, d = local_turn(place_ref, placement_ref, members_ref, recv_ref, whole_ref, log_b_ref[...])
    for k in range(4):
        keep_ref[k, :, :] = jnp.exp(v[k] + jnp.log(d[k]))
    mine = pl.ds(pl.multiple_of(place_ref[3] * 16, 16), 16)
    for k in range(4):
        out_ref[:, k, :] = keep_ref[k, mine, :]


def call(body, inputs, outs, scratch=(), work=1, space=pltpu.VMEM):
    return pl.pallas_call(
        body,
        out_shape=[jax.ShapeDtypeStruct(s[:2], s[2]) if BF16 in s else jax.ShapeDtypeStruct(s, F32) for s in outs],
        in_specs=[pl.BlockSpec(memory_space=pltpu.SMEM)] + [pl.BlockSpec(memory_space=space)] * (len(inputs) - 1),
        out_specs=[pl.BlockSpec(memory_space=pltpu.VMEM)] * len(outs),
        scratch_shapes=list(scratch),
        compiler_params=pltpu.CompilerParams(vmem_limit_bytes=20 * 2**20),
        cost_estimate=pl.CostEstimate(flops=work * 10**9, bytes_accessed=10**6, transcendentals=0),
    )(*inputs)


def on_device(placement_a, members_b, source_mass, init_log, factors, wholes):
    x, c, z, y = (lax.axis_index(name) for name in ("x", "c", "z", "y"))
    share = z * 4 + y
    place = jnp.stack([c, x * 8 + c * 4 + y, share, x]).astype(jnp.int32)
    index = (place, placement_a.reshape(1, 128), members_b)
    (block,) = call(block_kernel, (place, init_log, source_mass), [(64, 24, 128)],
                    [pltpu.VMEM((16, 4, 128), F32), pltpu.VMEM((16, 256), F32), pltpu.SemaphoreType.DMA((2,))],
                    space=pltpu.HBM)
    own = lax.all_to_all(block, ("x", "z", "y"), 0, 0, tiled=True)
    sum_a, sum_b, factors = call(start_kernel, index + (factors,), [(16, 512), (16, 128), (3840, 128, BF16)])
    other = lax.ppermute(own, "c", [(0, 1), (1, 0)])

    def exchange(rows):
        return lax.all_to_all(rows, ("x", "c", "y"), 0, 0, tiled=True)

    send, table, *rest = call(first_kernel, index + (own, other, sum_a, sum_b, factors),
                              [(32, 16, 128), (128, W), (16, 512), (16, 128), (16, W), (8, W)])
    first = exchange(send)
    send, here = call(second_kernel, index + (first, table, *rest, factors, wholes), [(32, 16, 128), (128, 128)],
                   [pltpu.VMEM((16, W), F32)])
    second = exchange(send)
    (log_b,) = call(middle_kernel, index + (here, first, wholes), [(128, 128)])
    (out,) = call(last_kernel, index + (log_b, second, wholes), [(16, 4, 128)], [pltpu.VMEM((4, 128, 128), F32)])
    return out


def solution(mesh):
    split = Mesh(mesh.devices.reshape(4, 2, 4, 4), ("x", "c", "z", "y"))
    tables = _tables()
    placed = (P(), P(), P(("x", "c"), None), P(("x", "c"), None, ("z", "y"))) + (P(),) * len(tables)
    body = jax.shard_map(
        on_device, mesh=split, in_specs=placed, out_specs=P(("x", "c"), None, ("z", "y")), check_vma=False
    )

    def run(placement_a, members_b, source_mass, init_log):
        return body(placement_a, members_b, source_mass, init_log, *(jnp.asarray(t) for t in tables))

    return run
```

time: 93 us -> 78 us (0.84)
  blocking collectives: 55.8 us -> 38 us
  waiting for transfers between devices: 1.78 us -> 7.09 us
  starting transfers between devices: 2.72 us -> 6.84 us
  Pallas kernels: 27.7 us -> 24 us
  other arithmetic: 1.7 us -> 0.08 us
  local copies, waits for them, and re-layouts: 2.68 us -> 1.6 us
    all_to_all x3 -> x2, blocking collectives: 55.8 us -> 38 us  [the longest x1 25.9 us: on_device(): own = lax.all_to_all(block, ('x', 'z', 'y'), 0, 0, tiled=True)]
    all_to_all x0 -> x1, waiting for transfers between devices: none -> 6.48 us  [exchange(): return lax.all_to_all(rows, ('x', 'c', 'y'), 0, 0, tiled=True)]
    all_to_all x0 -> x1, starting transfers between devices: none -> 4.12 us  [exchange(): return lax.all_to_all(rows, ('x', 'c', 'y'), 0, 0, tiled=True)]
    pallas_call x3 -> x6, Pallas kernels: 27.7 us -> 24 us  [call(): pl.pallas_call(body, out_shape=[jax.ShapeDtypeStruct(s[:2], s[2]) if BF16...]
    unnamed x11 -> x13, local copies, waits for them, and re-layouts: 0.14 us -> 1.6 us
    ppermute x1 -> x0, local copies, waits for them, and re-layouts: 1.42 us -> none  [on_device(): other = lax.ppermute(own, 'c', [(0, 1), (1, 0)])]
    ppermute x1, waiting for transfers between devices: 1.78 us -> 0.61 us  [on_device(): other = lax.ppermute(own, 'c', [(0, 1), (1, 0)])]
  transfers between devices with their start and end apart: 1 -> 2, of which waited for: 1 -> 2; matrix products, arithmetic and copies ran while one was open for 0% -> 0% of each run, Pallas kernels for 0% -> 5%
where the time goes in v2:
time: 78 us; the launch traced here: 77.6 us
  blocking collectives  38 us (49%)
  Pallas kernels  24 us (31%)
  waiting for transfers between devices  7.09 us (9%)
  starting transfers between devices  6.84 us (9%)
  local copies, waits for them, and re-layouts  1.6 us (2%)
    all_to_all x1, blocking collectives, on_device(): own = lax.all_to_all(block, ('x', 'z', 'y'), 0, 0, tiled=True)  25.9 us
    pallas_call x6, Pallas kernels, call(): pl.pallas_call(body, out_shape=[jax.ShapeDtypeStruct(s[:2], s[2]) if BF16...  24 us
    all_to_all x1, blocking collectives, exchange(): return lax.all_to_all(rows, ('x', 'c', 'y'), 0, 0, tiled=True)  12.1 us
    all_to_all x1, waiting for transfers between devices, exchange(): return lax.all_to_all(rows, ('x', 'c', 'y'), 0, 0, tiled=True)  6.48 us
    all_to_all x1, starting transfers between devices, exchange(): return lax.all_to_all(rows, ('x', 'c', 'y'), 0, 0, tiled=True)  4.12 us
    ppermute x1, starting transfers between devices, on_device(): other = lax.ppermute(own, 'c', [(0, 1), (1, 0)])  2.72 us
    unnamed x13, local copies, waits for them, and re-layouts  1.6 us
  transfers between devices with their start and end apart: 2, of which 2 were waited for; matrix products, arithmetic and copies ran while one was open for 0% of the time, Pallas kernels for 5%

profile of v2, /device:TPU:1, one launch (start us, length us, event | category | flops | bytes accessed | tf_op | source)
XLA Modules:
  0.0 77.6 jit_solution(3343235608731318436)
XLA Ops:
  0.0 0.1 pad_add_fusion.place_ref
  0.1 0.0 copy-start.2
  0.1 0.8 copy-done.2
  0.8 0.0 copy-start.3
  0.8 0.7 copy-done.3
  1.6 0.0 copy-start.5
  1.6 0.0 copy-start.1
  1.6 0.0 copy-start.4
  1.6 0.7 shard_map.64
  2.3 25.9 %all_to_all.15.own_ref = f32[64,24,128]{2,1,0:T(8,128)S(1)} all-to-all(f32[64,24,128]{2,1,0:T(8,128)S(1)} %shard_map.64), channel_id=1, replica_groups=mesh['x'=4,'c'=2,'z'=4,'y'=4] {'x','z','y'}, dimensions={0} | all-to-all | bytes 1572864 | tf_op jit(solution)/shard_map/all_to_all | solution.py:466
  28.1 2.7 %collective-permute-start = (f32[64,24,128]{2,1,0:T(8,128)S(1)}, f32[64,24,128]{2,1,0:T(8,128)}, u32[]{:S(2)}, u32[]{:S(2)}) collective-permute-start(f32[64,24,128]{2,1,0:T(8,128)S(1)} %all_to_all.15.own_ref), channel_id=1, source_target_pairs={{0,16},{16,0},{1,17},{17,1},{2,18},{18,2},{3,19},{19,3},{4,20},{20... | collective-permute-start | bytes 2359304 | tf_op jit(solution)/shard_map/ppermute | solution.py:468
  30.9 0.0 copy-done.5
  30.9 0.1 copy.11.members_ref
  31.0 0.0 copy-done.1
  31.0 0.0 copy-done.4
  31.0 1.3 %shard_map.65 = (f32[16,512]{1,0:T(8,128)S(1)}, f32[16,128]{1,0:T(8,128)S(1)}, bf16[3840,128]{1,0:T(8,128)(2,1)S(1)}) custom-call(s32[4]{0:T(128)S(1)} %pad_add_fusion.place_ref, s32[1,128]{1,0:T(1,128)S(1)} %bitcast.5, s32[128,4]{1,0:T(8,128)S(1)} %copy.11.members_ref, bf16[3840,128]{1,0:T(8,128)(2,1)S(1)} %copy-done.4), custom_call_target="tpu_custom_call" | custom-call | flops 1000000000 | bytes 1000000 | tf_op jit(solution)/shard_map/pallas_call | solution.py:447
  32.3 0.0 copy-start
  32.3 0.6 collective-permute-done.other_ref
  32.9 6.5 %shard_map.66 = (f32[32,16,128]{2,1,0:T(8,128)S(1)}, f32[128,2048]{1,0:T(8,128)S(1)}, f32[16,512]{1,0:T(8,128)S(1)}, f32[16,128]{1,0:T(8,128)S(1)}, f32[16,2048]{1,0:T(8,128)S(1)}, /*index=5*/f32[8,2048]{1,0:T(8,128)S(1)}) custom-call(s32[4]{0:T(128)S(1)} %pad_add_fusion.place_ref, s32[1,128]{1,0:T(1,128)S(1)} %bitcast.6, s32[128,4]{1,0:T(8,128)S(1)} %copy.11.members_ref, ...), custom_call_target="tpu_custom_call" | custom-call | flops 1000000000 | bytes 1000000 | tf_op jit(solution)/shard_map/pallas_call | solution.py:447
  39.5 12.1 %all_to_all.16.recv_ref = f32[32,16,128]{2,1,0:T(8,128)S(1)} all-to-all(f32[32,16,128]{2,1,0:T(8,128)S(1)} %get-tuple-element.19), channel_id=1, replica_groups=mesh['x'=4,'c'=2,'z'=4,'y'=4] {'x','c','y'}, dimensions={0} | all-to-all | bytes 524288 | tf_op jit(solution)/shard_map/all_to_all | solution.py:471
  51.5 0.0 copy-done
  51.5 9.9 %shard_map.67 = (f32[32,16,128]{2,1,0:T(8,128)}, f32[128,128]{1,0:T(8,128)S(1)}) custom-call(s32[4]{0:T(128)S(1)} %pad_add_fusion.place_ref, s32[1,128]{1,0:T(1,128)S(1)} %bitcast.7, s32[128,4]{1,0:T(8,128)S(1)} %copy.11.members_ref, f32[32,16,128]{2,1,0:T(8,128)S(1)} %all_to_all.16.recv_ref, f32[128,2048]{1,0:T(8,128)S(1)} %get-tuple-element.20.table_ref, ...), custom_call_target="tpu_custom_call" | custom-call | flops 1000000000 | bytes 1000000 | tf_op jit(solution)/shard_map/pallas_call | solution.py:447
  61.5 4.1 %all-to-all-start.2 = ((f32[32,16,128]{2,1,0:T(8,128)}), f32[32,16,128]{2,1,0:T(8,128)S(1)}, u32[]{:S(2)}, u32[]{:S(2)}) async-start(f32[32,16,128]{2,1,0:T(8,128)} %get-tuple-element.26), calls=%async_computation.2 | async-start | bytes 524288 | tf_op jit(solution)/shard_map/all_to_all | solution.py:471
  65.6 2.4 %shard_map.68.log_b_ref = f32[128,128]{1,0:T(8,128)S(1)} custom-call(s32[4]{0:T(128)S(1)} %pad_add_fusion.place_ref, s32[1,128]{1,0:T(1,128)S(1)} %bitcast.8, s32[128,4]{1,0:T(8,128)S(1)} %copy.11.members_ref, f32[128,128]{1,0:T(8,128)S(1)} %get-tuple-element.25.here_ref, f32[32,16,128]{2,1,0:T(8,128)S(1)} %all_to_all.16.recv_ref, bf16[640,2048]{1,0:T(8,128)(2,1)S(1)} %copy-done), custom_call_target="tpu_custom_call" | custom-call | flops 1000000000 | bytes 1000000 | tf_op jit(solution)/shard_map/pallas_call | solution.py:447
  68.0 6.5 %all-to-all-done.2.recv_ref = f32[32,16,128]{2,1,0:T(8,128)S(1)} async-done(((f32[32,16,128]{2,1,0:T(8,128)}), f32[32,16,128]{2,1,0:T(8,128)S(1)}, u32[]{:S(2)}, u32[]{:S(2)}) %all-to-all-start.2) | async-done | bytes 262176 | tf_op jit(solution)/shard_map/all_to_all | solution.py:471
  74.5 3.1 %shard_map.69 = f32[16,4,128]{2,1,0:T(4,128)} custom-call(s32[4]{0:T(128)S(1)} %pad_add_fusion.place_ref, s32[1,128]{1,0:T(1,128)S(1)} %bitcast.9, s32[128,4]{1,0:T(8,128)S(1)} %copy.11.members_ref, f32[128,128]{1,0:T(8,128)S(1)} %shard_map.68.log_b_ref, f32[32,16,128]{2,1,0:T(8,128)S(1)} %all-to-all-done.2.recv_ref, bf16[640,2048]{1,0:T(8,128)(2,1)S(1)} %copy-done), custom_call_target="tpu_custom_call" | custom-call | flops 1000000000 | bytes 1000000 | tf_op jit(solution)/shard_map/pallas_call | solution.py:447
Async XLA Ops:
  0.1 0.8 copy-start.2
  0.8 0.7 copy-start.3
  1.6 29.3 %copy-start.5 = (s32[128,4]{0,1:T(4,128)S(1)}, s32[128,4]{0,1:T(4,128)}, u32[]{:S(2)}) copy-start(s32[128,4]{0,1:T(4,128)} %param.7) | copy-start | bytes 6148
  1.6 29.4 %copy-start.1 = (s32[128]{0:T(128)S(1)}, s32[128]{0:T(128)}, u32[]{:S(2)}) copy-start(s32[128]{0:T(128)} %param.6) | copy-start | bytes 1540
  1.6 29.4 %copy-start.4 = (bf16[3840,128]{1,0:T(8,128)(2,1)S(1)}, bf16[3840,128]{1,0:T(8,128)(2,1)}, u32[]{:S(2)}) copy-start(bf16[3840,128]{1,0:T(8,128)(2,1)} %constant.25.clone.factor_ref) | copy-start | bytes 2949124
  28.1 4.8 %collective-permute-start = (f32[64,24,128]{2,1,0:T(8,128)S(1)}, f32[64,24,128]{2,1,0:T(8,128)}, u32[]{:S(2)}, u32[]{:S(2)}) collective-permute-start(f32[64,24,128]{2,1,0:T(8,128)S(1)} %all_to_all.15.own_ref), channel_id=1, source_target_pairs={{0,16},{16,0},{1,17},{17,1},{2,18},{18,2},{3,19},{19,3},{4,20},{20... | collective-permute-start | bytes 2359304 | tf_op jit(solution)/shard_map/ppermute | solution.py:468
  32.3 19.2 %copy-start = (bf16[640,2048]{1,0:T(8,128)(2,1)S(1)}, bf16[640,2048]{1,0:T(8,128)(2,1)}, u32[]{:S(2)}) copy-start(bf16[640,2048]{1,0:T(8,128)(2,1)} %constant.26.clone.whole_ref) | copy-start | bytes 7864324
  61.5 13.0 %all-to-all-start.2 = ((f32[32,16,128]{2,1,0:T(8,128)}), f32[32,16,128]{2,1,0:T(8,128)S(1)}, u32[]{:S(2)}, u32[]{:S(2)}) async-start(f32[32,16,128]{2,1,0:T(8,128)} %get-tuple-element.26), calls=%async_computation.2 | async-start | bytes 524288 | tf_op jit(solution)/shard_map/all_to_all | solution.py:471

commit v3 on v2

v3 whole, which is shorter than its diff:
```python
import numpy as np
import ml_dtypes

import jax
import jax.numpy as jnp
from jax import lax
from jax.experimental import pallas as pl
from jax.experimental.pallas import tpu as pltpu
from jax.sharding import Mesh, PartitionSpec as P

F32 = jnp.float32
BF16 = jnp.bfloat16
W = 2048
CENTRE = 128 + 31


def _halves(matrix):
    high = matrix.astype(ml_dtypes.bfloat16)
    low = (matrix - high.astype(np.float64)).astype(ml_dtypes.bfloat16)
    return high, low


def _thrice(matrix):
    high, low = _halves(matrix)
    return np.concatenate([high, high, low], axis=0)


def _tables():
    yh = (np.arange(32) + 0.5) / 32 - 0.5
    ya = (np.arange(64) + 0.5) / 64 - 0.5
    dh = (np.arange(8) - 3.5) / 128
    da = (np.arange(8) - 3.5) / 256
    shifts = [(k - 1.5) / 32 for k in range(4)]

    def whole(shift):
        up = np.exp(400.0 * dh[:, None] * yh[None])
        along = np.exp(400.0 * (da + shift)[:, None] * ya[None])
        return (up[:, None, :, None] * along[None, :, None, :]).reshape(64, W)

    def along(shift):
        part = np.zeros((2, 64, 2, 8, 8))
        for h in range(2):
            part[h, :, h] = np.exp(400.0 * ya[:, None] * (da + shift)[None])[:, None, :]
        return part.reshape(128, 128)

    cells = [along(s) for s in shifts]
    factors = [_thrice(m) for m in cells] + [_thrice(np.concatenate([m.T for m in cells], axis=0))]
    factors += [_thrice(along(0.0)), _thrice(along(0.0).T)]
    wholes = _halves(np.concatenate([whole(s) for s in shifts], axis=0)) + _halves(whole(0.0))
    return np.concatenate(factors, axis=0), np.concatenate(wholes, axis=0)


CELL, BACK, BASIC, BASIC_BACK = 0, 1536, 3072, 3456


def dot(a, b):
    return jnp.dot(a, b, preferred_element_type=F32)


def split2(x):
    high = x.astype(BF16)
    return high, (x - high.astype(F32)).astype(BF16)


def split3(x):
    high = x.astype(BF16)
    rest = x - high.astype(F32)
    mid = rest.astype(BF16)
    return high, mid, (rest - mid.astype(F32)).astype(BF16)


def pick(onehot, x):
    o = onehot.astype(BF16)
    return dot(jnp.concatenate([o, o, o], axis=1), jnp.concatenate(split3(x), axis=0))


def targets(first, count):
    j = first + lax.broadcasted_iota(jnp.int32, (1, count), 1)
    yh = (lax.shift_right_logical(j, 6).astype(F32) + 0.5) / 32.0 - 0.5
    ya = (lax.bitwise_and(j, 63).astype(F32) + 0.5) / 64.0 - 0.5
    return yh, ya


def basic_centre(ids):
    row = jnp.floor(ids / 32.0)
    return (row * 8.0 + 4.0) / 128.0 - 0.5, ((ids - row * 32.0) * 8.0 + 4.0) / 256.0 - 0.5


def cell_centre(cells):
    row = jnp.floor(cells / 8.0)
    return (row * 8.0 + 4.0) / 128.0 - 0.5, ((cells - row * 8.0) * 32.0 + 16.0) / 256.0 - 0.5


def tilt(centre, y):
    return (400.0 * centre[0]) * y[0] + (400.0 * centre[1]) * y[1]


def eye_mask():
    return lax.broadcasted_iota(jnp.int32, (128, 128), 0) == lax.broadcasted_iota(jnp.int32, (128, 128), 1)


def to_col(row):
    return jnp.sum(jnp.where(eye_mask(), jnp.broadcast_to(row, (128, 128)), 0.0), axis=1, keepdims=True)


def to_row(col):
    return jnp.sum(jnp.where(eye_mask(), jnp.broadcast_to(col, (128, 128)), 0.0), axis=0, keepdims=True)


def local_cells(placement_row, core):
    dst = lax.broadcasted_iota(jnp.int32, (128, 128), 0)
    src = lax.broadcasted_iota(jnp.int32, (128, 128), 1)
    side = lax.bitwise_xor(lax.shift_right_logical(dst, 6), core)
    slot = lax.bitwise_and(lax.shift_right_logical(dst, 4), 3) * 32 + side * 16 + lax.bitwise_and(dst, 15)
    col = jnp.sum(jnp.where(slot == src, jnp.broadcast_to(placement_row, (128, 128)), 0.0), axis=1, keepdims=True)
    return col, to_row(col)


def own_ids(member_rows, group):
    lane = lax.broadcasted_iota(jnp.int32, (16, 128), 1)
    sub = lax.broadcasted_iota(jnp.int32, (16, 128), 0)
    k = lax.shift_right_logical(sub, 2)
    rows = jnp.zeros((16, 128), F32)
    for i in range(4):
        rows = jnp.where(k == i, jnp.broadcast_to(member_rows[i], (16, 128)), rows)
    return jnp.sum(jnp.where(lane == 4 * group + lax.bitwise_and(sub, 3), rows, 0.0), axis=1, keepdims=True)


def low_half(shape):
    return lax.broadcasted_iota(jnp.int32, shape, 1) < 64


def swap(x):
    return pltpu.roll(x, 64, 1)


def doubled(x, upper):
    mask = low_half(x.shape)
    return jnp.where(mask, swap(x), x) if upper else jnp.where(mask, x, swap(x))


def segment(x, k):
    y = jnp.where(k >= 2.0, x[:, 256:], x[:, :256])
    return jnp.where((k == 1.0) | (k == 3.0), y[:, 128:], y[:, :128])


def quadrupled(x):
    return jnp.concatenate([doubled(x[:, :128], False), doubled(x[:, :128], True),
                            doubled(x[:, 128:], False), doubled(x[:, 128:], True)], axis=1)


def thrice(x):
    high, low = split2(x)
    return jnp.concatenate([high, low, high], axis=1)


def up_rows():
    lane = lax.broadcasted_iota(jnp.int32, (16, 128), 1)
    row = 2 * lax.broadcasted_iota(jnp.int32, (16, 128), 0) + lax.shift_right_logical(lane, 6)
    yh = (row.astype(F32) + 0.5) / 32.0 - 0.5
    dh = (lax.bitwise_and(lax.shift_right_logical(lane, 3), 7).astype(F32) - 3.5) / 128.0
    up = jnp.exp(400.0 * yh * dh)
    return [up[t : t + 1, :] for t in range(16)]


def sums(u, factor_ref, up, cells):
    n = u.shape[0]
    x = thrice(jnp.concatenate([u[:, 128 * t : 128 * t + 128] for t in range(16)], axis=0))
    out = []
    for first in [CELL + 384 * k for k in range(4)] if cells else [BASIC]:
        p = dot(x, factor_ref[first : first + 384, :])
        parts = [p[n * t : n * t + n] * h for t, h in enumerate(up)]
        while len(parts) > 1:
            parts = [parts[i] + parts[i + 1] for i in range(0, len(parts), 2)]
        out.append(parts[0] + swap(parts[0]))
    return jnp.concatenate(out, axis=1)


def cols(e, factor_ref, up):
    n, groups = e.shape[0], e.shape[1] // 128
    x = jnp.concatenate([e * jnp.concatenate([h] * groups, axis=1) for h in up], axis=0)
    d = dot(thrice(x), factor_ref[BACK : BACK + 1536, :] if groups == 4 else factor_ref[BASIC_BACK : BASIC_BACK + 384, :])
    return jnp.concatenate([d[n * t : n * t + n] for t in range(16)], axis=1)


def halves(e):
    return jnp.concatenate(split2(e), axis=0)


def cell_cols(e, whole):
    n = e.shape[0] // 2
    p = dot(e, whole[:256])
    return p[:n] + p[n:] + dot(e[:n], whole[256:512])


def basic_cols(e, whole):
    n = e.shape[0] // 2
    p = dot(e, whole[512:])
    return p[:n] + p[n:]


def nearness(centre, y):
    return jnp.exp(-200.0 * ((centre[0] - y[0]) ** 2 + (centre[1] - y[1]) ** 2))


def balanced(mass, s):
    return mass * (s[:, CENTRE : CENTRE + 1] / s)


def sweep_a(log_b, mass, d, factor_ref, up, beside):
    b = jnp.exp(log_b - jnp.max(log_b, axis=1, keepdims=True))
    for i in range(3):
        beside(i)
        e = balanced(mass, sums(b / d, factor_ref, up, True))
        d = cols(e, factor_ref, up)
    return e, d


def over_k(x, op):
    y = op(x[:8], x[8:])
    return op(y, pltpu.roll(y, 4, 0))


def twice(x):
    return jnp.concatenate([x, x], axis=0)


def column_part(r, top, d):
    q = r - top
    peak = over_k(q, jnp.maximum)
    return peak + jnp.log(over_k(jnp.exp(q - twice(peak)) * d, jnp.add))


def sweep_b(log_b, mass, r, part, factor_ref, up, beside):
    for i in range(3):
        beside(5 + i)
        v = r + twice(log_b - part)
        top = jnp.max(v, axis=1, keepdims=True)
        e = mass / sums(jnp.exp(v - top), factor_ref, up, False)
        if i < 2:
            part = column_part(r, top, cols(e, factor_ref, up))
    return e, top


def solve_pair(log_b_a, mass_a, mass_b, ids, d, part, factor_ref, up, send_ref, beside=lambda i: None):
    y = targets(0, W)
    k = ids - 4.0 * jnp.floor(ids / 4.0)
    at_cell = cell_centre(jnp.floor(ids / 4.0))
    at_basic = basic_centre(ids)
    e_a, d_a = sweep_a(log_b_a, mass_a, d, factor_ref, up, beside)
    e_first = segment(e_a, k)
    beside(3)
    d_first = cols(e_first, factor_ref, up)
    v = log_b_a - jnp.log(d_a) + (400.0 * (at_basic[1] - at_cell[1])) * y[1]
    peak = over_k(v, jnp.maximum)
    beside(4)
    log_b_b = peak + jnp.log(over_k(jnp.exp(v - twice(peak)) * d_first, jnp.add))
    e_second, top = sweep_b(log_b_b, mass_b, tilt(at_basic, y), part, factor_ref, up, beside)
    rows = jnp.where(low_half((16, 128)), e_first, jnp.log(e_second) - top)
    for i in range(32):
        send_ref[i, :, :] = rows


def member_rows_of(members_ref):
    members = members_ref[...].astype(F32)
    return [to_row(members[:, k : k + 1]) for k in range(4)]


def exchange_ids(members_ref):
    members = members_ref[...].astype(F32)
    slot = lax.broadcasted_iota(jnp.int32, (128, 128), 0)
    lane = lax.broadcasted_iota(jnp.int32, (128, 128), 1)
    k = lax.bitwise_and(lax.shift_right_logical(lane, 2), 3)
    value = jnp.broadcast_to(members[:, 0:1], (128, 128))
    for i in range(1, 4):
        value = jnp.where(k == i, jnp.broadcast_to(members[:, i : i + 1], (128, 128)), value)
    of_lane = 4 * lax.shift_right_logical(lane, 4) + lax.bitwise_and(lane, 3)
    return jnp.concatenate(
        [jnp.sum(jnp.where(slot == of_lane + 32 * t, value, 0.0), axis=0, keepdims=True) for t in range(4)], axis=1)


def near_cells(want, member_rows, cell_row, exchanged, cells_ref, groups_ref, rows_ref, ids_ref):
    hits = [jnp.where(row == want, 1.0, 0.0) for row in member_rows]
    slot = (hits[0] + hits[1]) + (hits[2] + hits[3])
    ids = jnp.concatenate([jnp.sum(slot * row, axis=1, keepdims=True) for row in member_rows], axis=0)
    cell = jnp.floor(ids / 4.0)
    cells = jnp.where(cell_row == cell, 1.0, 0.0)
    cells_ref[...] = cells.astype(BF16)
    for k in range(4):
        groups_ref[256 * k : 256 * k + 256, :] = jnp.where(exchanged == 4.0 * cell + float(k), 1.0, 0.0).astype(BF16)
    ids = jnp.concatenate([ids, want], axis=0)
    rows_ref[...] = jnp.where(exchanged == ids, 1.0, 0.0).astype(BF16)
    ids_ref[...] = jnp.broadcast_to(ids, (320, 128))
    return ids, cells


def start_kernel(place_ref, placement_ref, members_ref, factor_ref, sum_a_ref, sum_b_ref, keep_ref, own_ids_ref, onehot_ref,
                 cell_ref, cells_ref, groups_ref, rows_ref, ids_ref):
    cell_col, cell_row = local_cells(placement_ref[...].astype(F32), place_ref[0])
    member_rows = member_rows_of(members_ref)
    ids = own_ids(member_rows, place_ref[1])
    y = targets(0, W)
    up = up_rows()
    sum_a_ref[...] = sums(nearness(cell_centre(jnp.floor(ids / 4.0)), y), factor_ref, up, True)
    sum_b_ref[...] = sums(nearness(basic_centre(ids), y), factor_ref, up, False)
    keep_ref[...] = factor_ref[...]
    own_ids_ref[...] = jnp.broadcast_to(ids, (16, 128))
    cells = jnp.floor(ids / 4.0)
    onehot_ref[...] = jnp.where(cell_row == cells, 1.0, 0.0)
    cell_ref[...] = jnp.broadcast_to(cell_col, (128, 128))
    want = jnp.concatenate([4.0 * cells + float(k) for k in range(4)], axis=0)
    near_cells(want, member_rows, cell_row, exchange_ids(members_ref), cells_ref, groups_ref, rows_ref, ids_ref)


def first_kernel(place_ref, own_ref, other_ref, sum_a_ref, sum_b_ref, ids_ref, onehot_ref, cell_ref, cells_ref, near_ref,
                 factor_ref, send_ref, here_ref, level_ref, mass_a_ref, mass_b_ref, d_ref, part_ref, table_ref):
    ids, onehot, up = ids_ref[:, :1], onehot_ref[...], up_rows()
    mass = []
    for part in (16, 17):
        rows = jnp.concatenate([own_ref[:, part, :], other_ref[:, part, :]], axis=0)
        mass.append(pick(onehot, rows))
    mass_a = quadrupled(jnp.concatenate(mass, axis=1))
    mass_b = segment(mass_a, ids - 4.0 * jnp.floor(ids / 4.0))
    d = cols(balanced(mass_a, sum_a_ref[...]), factor_ref, up)
    log_b = []
    for t in range(16):
        rows = [ref[x * 16 + t, 0:16, :] for ref in (own_ref, other_ref) for x in range(4)]
        rows = jnp.concatenate(rows, axis=0)
        table_ref[:, 128 * t : 128 * t + 128] = rows
        log_b.append(pick(onehot, rows))
    here_ref[...] = table_ref[:, pl.ds(pl.multiple_of(place_ref[2] * 128, 128), 128)]
    log_b = jnp.concatenate(log_b, axis=1)
    at_basic = basic_centre(ids)
    top = 200.0 * (at_basic[0] * at_basic[0] + at_basic[1] * at_basic[1])
    part = column_part(tilt(at_basic, targets(0, W)), top, cols(mass_b / sum_b_ref[...], factor_ref, up))
    mass_a_ref[...] = mass_a
    mass_b_ref[...] = mass_b
    d_ref[...] = d
    part_ref[...] = part
    near, cell_col = near_ref[0:256, :1], cell_ref[:, :1]

    def level(block):
        at = slice(256 * block, 256 * block + 256)
        level_ref[:, at] = near_level(near, cells_ref[...], table_ref[:, at], cell_col, targets(256 * block, 256))

    solve_pair(log_b, mass_a, mass_b, ids, d, part, factor_ref, up, send_ref, level)


def received(recv_ref):
    return [jnp.concatenate([recv_ref[g, 4 * k : 4 * k + 4, :] for g in range(32)], axis=0) for k in range(4)]


def high_top(x):
    return jnp.max(jnp.where(low_half(x.shape), -jnp.inf, x), axis=1, keepdims=True)


def unpack(f):
    top = -high_top(f)
    return doubled(f, False), jnp.exp(doubled(f, True) + top), top


def a_rows(member_rows, cell_col, k):
    want = 4.0 * cell_col + float(k)
    return jnp.concatenate([jnp.where(row == want, 1.0, 0.0) for row in member_rows], axis=1).astype(BF16)


def packed(f):
    high, low = split2(f)
    return jnp.where(low_half(f.shape), high.astype(F32), swap(low.astype(F32))).astype(BF16)


def cell_halves(by_k):
    mask = low_half(by_k[0].shape)
    high = [jnp.where(mask, by_k[i], swap(by_k[i + 1])) for i in (0, 2)]
    low = [jnp.where(mask, swap(by_k[i]), by_k[i + 1]) for i in (0, 2)]
    return jnp.concatenate([jnp.concatenate(high, axis=1), jnp.concatenate(low, axis=1)], axis=0).astype(BF16)


def mix(v, d):
    peak = jnp.maximum(jnp.maximum(v[0], v[1]), jnp.maximum(v[2], v[3]))
    z = [jnp.exp(a - peak) * b for a, b in zip(v, d)]
    return peak + jnp.log((z[0] + z[1]) + (z[2] + z[3]))


def near_level(ids, cells, log_b, cell_col, y):
    return pick(cells, log_b - tilt(cell_centre(cell_col), y)) + tilt(basic_centre(ids), y)


def gathered(recv_ref, groups_ref, rows_ref):
    f = recv_ref[...].reshape(512, 128)
    by_k = dot(groups_ref[...], packed(f))
    o = rows_ref[...]
    high, mid, low = split3(f)
    e0, e1, top = unpack((dot(o, high) + dot(o, mid)) + dot(o, low))
    by_k = [by_k[256 * k : 256 * k + 256] for k in range(4)]
    return cell_halves(by_k), halves(e0[:256]), halves(e1), top


def near_margins(gather, level, centre, y, whole):
    e_cell, e0, e1, top = gather
    parts = [slice(64 * k, 64 * k + 64) for k in range(4)]
    v = level - jnp.log(cell_cols(e_cell, whole))
    d0 = basic_cols(e0, whole)
    d1 = basic_cols(e1, whole)
    q = tilt(centre, y) - top
    log_b = mix([v[a] for a in parts], [d0[a] for a in parts])
    gamma = log_b - mix([q[a] for a in parts], [d1[a] for a in parts])
    return gamma + q[256:], d1[256:]


def second_kernel(place_ref, own_ids_ref, recv_ref, level_ref, groups_ref, rows_ref, ids_ref, mass_a_ref, mass_b_ref, d_ref,
                  part_ref, factor_ref, whole_ref, send_ref, here_ref):
    here_ref[...] = whole_ref[:, pl.ds(pl.multiple_of(place_ref[2] * 128, 128), 128)]
    gather = gathered(recv_ref, groups_ref, rows_ref)
    centre = basic_centre(ids_ref[:, :1])
    log_b = []
    for block in range(8):
        at = slice(block * 256, block * 256 + 256)
        v, d = near_margins(gather, level_ref[:, at], centre, targets(256 * block, 256), whole_ref[:, at])
        log_b.append(mix([v[16 * k : 16 * k + 16] for k in range(4)], [d[16 * k : 16 * k + 16] for k in range(4)]))
    solve_pair(jnp.concatenate(log_b, axis=1), mass_a_ref[...], mass_b_ref[...], own_ids_ref[:, :1], d_ref[...], part_ref[...],
               factor_ref, up_rows(), send_ref)


def middle_kernel(place_ref, placement_ref, members_ref, log_b_ref, recv_ref, whole_ref, level_ref, cells_ref, groups_ref,
                  rows_ref, ids_ref):
    cell_col, cell_row = local_cells(placement_ref[...].astype(F32), place_ref[0])
    member_rows = member_rows_of(members_ref)
    members = members_ref[...].astype(F32)
    share = place_ref[2]
    y = targets(share * 128, 128)
    whole = whole_ref[...]
    b_ids = [members[:, k : k + 1] for k in range(4)]
    b_cell = jnp.concatenate([jnp.where(cell_row == jnp.floor(i / 4.0), 1.0, 0.0) for i in b_ids], axis=0)
    b_tilt = [tilt(basic_centre(i), y) for i in b_ids]
    a_tilt = [tilt(basic_centre(4.0 * cell_col + float(k)), y) for k in range(4)]
    parts = [slice(128 * k, 128 * k + 128) for k in range(4)]
    every = jnp.concatenate(received(recv_ref), axis=0)
    hits = [a_rows(member_rows, cell_col, k) for k in range(4)]
    rows = packed(every)
    e_cell = cell_halves([dot(h, rows) for h in hits])
    by_k = jnp.concatenate([pick(h, every) for h in hits], axis=0)
    gamma = pick(b_cell, log_b_ref[...] - jnp.log(cell_cols(e_cell, whole)) - tilt(cell_centre(cell_col), y))
    e0, e1, top = unpack(every)
    _, ea, a_top = unpack(by_k)
    d0, d1, da = [basic_cols(halves(e), whole) for e in (e0, e1, ea)]
    log_b1 = mix([gamma[a] + t for a, t in zip(parts, b_tilt)], [d0[a] for a in parts])
    gamma1 = log_b1 - mix([t - top[a] for a, t in zip(parts, b_tilt)], [d1[a] for a in parts])
    log_b = []
    for k in range(4):
        hit = hits[k].astype(F32)
        slot = (hit[:, :128] + hit[:, 128:256]) + (hit[:, 256:384] + hit[:, 384:])
        log_b.append(pick(slot, gamma1) + a_tilt[k] - a_top[parts[k]])
    log_b = mix(log_b, [da[a] for a in parts])
    lane = lax.broadcasted_iota(jnp.int32, (16, 128), 1)
    first = place_ref[3] * 16 + lax.broadcasted_iota(jnp.int32, (16, 128), 0)
    own_cells = jnp.sum(jnp.where(lane == first, jnp.broadcast_to(cell_row, (16, 128)), 0.0), axis=1, keepdims=True)
    want = jnp.concatenate([4.0 * own_cells + float(k) for k in range(4)], axis=0)
    ids, cells = near_cells(want, member_rows, cell_row, exchange_ids(members_ref), cells_ref, groups_ref, rows_ref, ids_ref)
    level_ref[...] = near_level(ids[:256], cells, log_b, cell_col, y)


def last_kernel(place_ref, recv_ref, level_ref, groups_ref, rows_ref, ids_ref, whole_ref, out_ref):
    centre = basic_centre(ids_ref[:, :1])
    v, d = near_margins(gathered(recv_ref, groups_ref, rows_ref), level_ref[...], centre,
                        targets(place_ref[2] * 128, 128), whole_ref[...])
    out = jnp.exp(v + jnp.log(d))
    for k in range(4):
        out_ref[:, k, :] = out[16 * k : 16 * k + 16]


def call(body, inputs, outs, scratch=(), work=1):
    def spec(value):
        return pl.BlockSpec(memory_space=pltpu.SMEM if value.shape == (4,) else pltpu.VMEM)

    return pl.pallas_call(
        body,
        out_shape=[jax.ShapeDtypeStruct(s[:-1], BF16) if s[-1] is BF16 else jax.ShapeDtypeStruct(s, F32) for s in outs],
        in_specs=[spec(value) for value in inputs],
        out_specs=[pl.BlockSpec(memory_space=pltpu.VMEM)] * len(outs),
        scratch_shapes=list(scratch),
        compiler_params=pltpu.CompilerParams(vmem_limit_bytes=24 * 2**20),
        cost_estimate=pl.CostEstimate(flops=work * 10**9, bytes_accessed=10**6, transcendentals=0),
    )(*inputs)


FACTORS = (3840, 128, BF16)
NEAR = [(256, 128, BF16), (1024, 512, BF16), (320, 512, BF16), (320, 128)]


def on_device(placement_a, members_b, source_mass, init_log, factors, wholes):
    x, c, z, y = (lax.axis_index(name) for name in ("x", "c", "z", "y"))
    share = z * 4 + y
    place = jnp.stack([c, x * 8 + c * 4 + y, share, x]).astype(jnp.int32)
    index = (place, placement_a.reshape(1, 128), members_b)
    v = [init_log[:, k, :] for k in range(4)]
    peak = jnp.maximum(jnp.maximum(v[0], v[1]), jnp.maximum(v[2], v[3]))
    e = [jnp.exp(a - peak) for a in v]
    log_b = peak + jnp.log((e[0] + e[1]) + (e[2] + e[3])) + float(np.log(64.0 / W))
    mass = lax.dynamic_slice_in_dim(source_mass, share, 1, 0).reshape(2, 128)
    block = jnp.concatenate([log_b, mass, jnp.zeros((6, 128), F32)], axis=0)
    own = lax.all_to_all(jnp.broadcast_to(block[None], (64, 24, 128)), ("x", "z", "y"), 0, 0, tiled=True)
    sum_a, sum_b, factors, own_ids_, onehot, cell, cells, groups, rows, ids = call(
        start_kernel, index + (factors,), [(16, 512), (16, 128), FACTORS, (16, 128), (16, 128), (128, 128)] + NEAR)
    other = lax.ppermute(own, "c", [(0, 1), (1, 0)])

    def exchange(rows):
        return lax.all_to_all(rows, ("x", "c", "y"), 0, 0, tiled=True)

    send, here, level, *rest = call(
        first_kernel, (place, own, other, sum_a, sum_b, own_ids_, onehot, cell, cells, ids, factors),
        [(32, 16, 128), (128, 128), (256, W), (16, 512), (16, 128), (16, W), (8, W)], [pltpu.VMEM((128, W), F32)])
    first = exchange(send)
    send, whole = call(second_kernel, (place, own_ids_, first, level, groups, rows, ids, *rest, factors, wholes),
                       [(32, 16, 128), (640, 128, BF16)])
    second = exchange(send)
    level, _, groups, rows, ids = call(middle_kernel, index + (here, first, whole), [(256, 128)] + NEAR)
    (out,) = call(last_kernel, (place, second, level, groups, rows, ids, whole), [(16, 4, 128)])
    return out


def solution(mesh):
    split = Mesh(mesh.devices.reshape(4, 2, 4, 4), ("x", "c", "z", "y"))
    tables = _tables()
    placed = (P(), P(), P(("x", "c"), None), P(("x", "c"), None, ("z", "y"))) + (P(),) * len(tables)
    body = jax.shard_map(
        on_device, mesh=split, in_specs=placed, out_specs=P(("x", "c"), None, ("z", "y")), check_vma=False
    )

    def run(placement_a, members_b, source_mass, init_log):
        return body(placement_a, members_b, source_mass, init_log, *(jnp.asarray(t) for t in tables))

    return run
```

time: 78 us -> 74.8 us (0.959)
  waiting for transfers between devices: 7.09 us -> 4.63 us
  Pallas kernels: 24 us -> 23 us
    all_to_all x1, waiting for transfers between devices: 6.48 us -> 4.63 us  [exchange(): return lax.all_to_all(rows, ('x', 'c', 'y'), 0, 0, tiled=True)]
    pallas_call x6 -> x5, Pallas kernels: 24 us -> 23 us  [call(): pl.pallas_call(body, out_shape=[jax.ShapeDtypeStruct(s[:-1], BF16) if s[-...]
    slice x0 -> x1, local copies, waits for them, and re-layouts: none -> 0.94 us  [on_device(): v = [init_log[:, k, :] for k in range(4)]]
    unnamed x13 -> x9, local copies, waits for them, and re-layouts: 1.6 us -> 0.81 us
  transfers between devices with their start and end apart: 2 -> 2, of which waited for: 2 -> 1; matrix products, arithmetic and copies ran while one was open for 0% -> 1% of each run, Pallas kernels for 5% -> 8%
where the time goes in v3:
time: 74.8 us; the launch traced here: 74.5 us
  blocking collectives  37.9 us (51%)
  Pallas kernels  23 us (31%)
  starting transfers between devices  6.84 us (9%)
  waiting for transfers between devices  4.63 us (6%)
  local copies, waits for them, and re-layouts  1.89 us (3%)
    all_to_all x1, blocking collectives, on_device(): lax.all_to_all(jnp.broadcast_to(block[None], (64, 24, 128)), ('x', 'z', '...  25.9 us
    pallas_call x5, Pallas kernels, call(): pl.pallas_call(body, out_shape=[jax.ShapeDtypeStruct(s[:-1], BF16) if s[-...  23 us
    all_to_all x1, blocking collectives, exchange(): return lax.all_to_all(rows, ('x', 'c', 'y'), 0, 0, tiled=True)  12 us
    all_to_all x1, waiting for transfers between devices, exchange(): return lax.all_to_all(rows, ('x', 'c', 'y'), 0, 0, tiled=True)  4.63 us
    all_to_all x1, starting transfers between devices, exchange(): return lax.all_to_all(rows, ('x', 'c', 'y'), 0, 0, tiled=True)  4.12 us
    ppermute x1, starting transfers between devices, on_device(): other = lax.ppermute(own, 'c', [(0, 1), (1, 0)])  2.72 us
  transfers between devices with their start and end apart: 2, of which 1 were waited for; matrix products, arithmetic and copies ran while one was open for 1% of the time, Pallas kernels for 8%

profile of v3, /device:TPU:1, one launch (start us, length us, event | category | flops | bytes accessed | tf_op | source)
XLA Modules:
  0.0 74.5 jit_solution(8674408709692934271)
XLA Ops:
  0.0 0.0 copy-start
  0.0 0.0 copy-start.3
  0.0 0.0 copy-start.2
  0.0 0.9 %fusion.3 = (f32[16,1,128]{2,1,0:T(1,128)S(1)}, f32[16,1,128]{2,1,0:T(1,128)S(1)}, f32[16,1,128]{2,1,0:T(1,128)S(1)}, f32[16,1,128]{2,1,0:T(1,128)S(1)}) fusion(f32[16,4,128]{2,1,0:T(4,128)} %param.9), kind=kLoop, calls=%fused_computation.9 | loop fusion | bytes 65536 | tf_op jit(solution)/shard_map/slice | solution.py:496
  1.0 0.0 copy-done
  1.0 0.1 pad.2.clone
  1.1 0.1 maximum_maximum_fusion
  1.2 0.1 broadcast_in_dim.10
  1.2 25.9 %all_to_all.15.own_ref = f32[64,24,128]{2,1,0:T(8,128)S(1)} all-to-all(f32[64,24,128]{2,1,0:T(8,128)S(1)} %broadcast_in_dim.10), channel_id=1, replica_groups=mesh['x'=4,'c'=2,'z'=4,'y'=4] {'x','z','y'}, dimensions={0} | all-to-all | bytes 1572864 | tf_op jit(solution)/shard_map/all_to_all | solution.py:502
  27.1 2.7 %collective-permute-start = (f32[64,24,128]{2,1,0:T(8,128)S(1)}, f32[64,24,128]{2,1,0:T(8,128)S(1)}, u32[]{:S(2)}, u32[]{:S(2)}) collective-permute-start(f32[64,24,128]{2,1,0:T(8,128)S(1)} %all_to_all.15.own_ref), channel_id=1, source_target_pairs={{0,16},{16,0},{1,17},{17,1},{2,18},{18,2},{3,19},{19,3},{4,20},{20... | collective-permute-start | bytes 2359304 | tf_op jit(solution)/shard_map/ppermute | solution.py:505
  29.8 0.8 %copy.7.members_ref = s32[128,4]{1,0:T(8,128)S(1)} copy(s32[128,4]{0,1:T(4,128)} %param.7) | data formatting | bytes 4096 | tf_op args[1]
  30.6 0.1 pad_add_fusion.place_ref
  30.7 0.0 copy-done.3
  30.7 0.0 copy-done.2
  30.7 1.5 %shard_map.64 = (f32[16,512]{1,0:T(8,128)S(1)}, f32[16,128]{1,0:T(8,128)S(1)}, bf16[3840,128]{1,0:T(8,128)(2,1)S(1)}, f32[16,128]{1,0:T(8,128)S(1)}, f32[16,128]...) custom-call(s32[4]{0:T(128)S(1)} %pad_add_fusion.place_ref, ...), custom_call_target="tpu_custom_call" | custom-call | flops 1000000000 | bytes 1000000 | tf_op jit(solution)/shard_map/pallas_call | solution.py:476
  32.2 0.0 copy-start.1
  32.2 0.0 collective-permute-done.other_ref
  32.2 6.0 %shard_map.65 = (f32[32,16,128]{2,1,0:T(8,128)S(1)}, f32[128,128]{1,0:T(8,128)S(1)}, f32[256,2048]{1,0:T(8,128)S(1)}, f32[16,512]{1,0:T(8,128)S(1)}, f32[16,128]...) custom-call(s32[4]{0:T(128)S(1)} %pad_add_fusion.place_ref, f32[64,24,128]{2,1,0:T(8,128)S(1)} %all_to_all.15.own_ref, ...), custom_call_target="tpu_custom_call" | custom-call | flops 1000000000 | bytes 1000000 | tf_op jit(solution)/shard_map/pallas_call | solution.py:476
  38.2 12.0 %all_to_all.16.recv_ref = f32[32,16,128]{2,1,0:T(8,128)S(1)} all-to-all(f32[32,16,128]{2,1,0:T(8,128)S(1)} %get-tuple-element.36), channel_id=1, replica_groups=mesh['x'=4,'c'=2,'z'=4,'y'=4] {'x','c','y'}, dimensions={0} | all-to-all | bytes 524288 | tf_op jit(solution)/shard_map/all_to_all | solution.py:508
  50.2 0.0 copy-done.1
  50.2 8.6 %shard_map.66 = (f32[32,16,128]{2,1,0:T(8,128)}, bf16[640,128]{1,0:T(8,128)(2,1)S(1)}) custom-call(s32[4]{0:T(128)S(1)} %pad_add_fusion.place_ref, f32[16,128]{1,0:T(8,128)S(1)} %get-tuple-element.28.ids_ref.own_ids_ref, f32[32,16,128]{2,1,0:T(8,128)S(1)} %all_to_all.16.recv_ref, f32[256,2048]{1,0:T(8,128)S(1)} %get-tuple-element.37.level_ref, ...), custom_call_target="tpu_custom_call" | custom-call | flops 1000000000 | bytes 1000000 | tf_op jit(solution)/shard_map/pallas_call | solution.py:476
  58.8 4.1 %all-to-all-start.2 = ((f32[32,16,128]{2,1,0:T(8,128)}), f32[32,16,128]{2,1,0:T(8,128)S(1)}, u32[]{:S(2)}, u32[]{:S(2)}) async-start(f32[32,16,128]{2,1,0:T(8,128)} %get-tuple-element.44), calls=%async_computation.2 | async-start | bytes 524288 | tf_op jit(solution)/shard_map/all_to_all | solution.py:508
  63.0 4.3 %shard_map.67 = (f32[256,128]{1,0:T(8,128)S(1)}, bf16[256,128]{1,0:T(8,128)(2,1)}, bf16[1024,512]{1,0:T(8,128)(2,1)S(1)}, bf16[320,512]{1,0:T(8,128)(2,1)S(1)}, f32[320,128]{1,0:T(8,128)S(1)}) custom-call(s32[4]{0:T(128)S(1)} %pad_add_fusion.place_ref, s32[1,128]{1,0:T(1,128)S(1)} %bitcast.17, s32[128,4]{1,0:T(8,128)S(1)} %copy.7.members_ref, ...), custom_call_target="tpu_custom_call" | custom-call | flops 1000000000 | bytes 1000000 | tf_op jit(solution)/shard_map/pallas_call | solution.py:476
  67.2 4.6 %all-to-all-done.2.recv_ref = f32[32,16,128]{2,1,0:T(8,128)S(1)} async-done(((f32[32,16,128]{2,1,0:T(8,128)}), f32[32,16,128]{2,1,0:T(8,128)S(1)}, u32[]{:S(2)}, u32[]{:S(2)}) %all-to-all-start.2) | async-done | bytes 262176 | tf_op jit(solution)/shard_map/all_to_all | solution.py:508
  71.9 2.6 %shard_map.68 = f32[16,4,128]{2,1,0:T(4,128)} custom-call(s32[4]{0:T(128)S(1)} %pad_add_fusion.place_ref, f32[32,16,128]{2,1,0:T(8,128)S(1)} %all-to-all-done.2.recv_ref, f32[256,128]{1,0:T(8,128)S(1)} %get-tuple-element.47.level_ref, bf16[1024,512]{1,0:T(8,128)(2,1)S(1)} %get-tuple-element.48.groups_ref, bf16[320,512]{1,0:T(8,128)(2,1)S(1)} %get-tuple-element.49.rows_ref, ...), custom_call_target="tpu_custom_call" | custom-call | flops 1000000000 | bytes 1000000 | tf_op jit(solution)/shard_map/pallas_call | solution.py:476
  (3 shorter events, 0.0 us)
Async XLA Ops:
  0.0 1.0 %copy-start = (f32[16,256]{1,0:T(8,128)S(1)}, f32[16,256]{1,0:T(8,128)}, u32[]{:S(2)}) copy-start(f32[16,256]{1,0:T(8,128)} %param.8) | copy-start | bytes 49156
  0.0 30.7 %copy-start.3 = (bf16[3840,128]{1,0:T(8,128)(2,1)S(1)}, bf16[3840,128]{1,0:T(8,128)(2,1)}, u32[]{:S(2)}) copy-start(bf16[3840,128]{1,0:T(8,128)(2,1)} %constant.33.clone.factor_ref) | copy-start | bytes 2949124
  0.0 30.7 %copy-start.2 = (s32[128]{0:T(128)S(1)}, s32[128]{0:T(128)}, u32[]{:S(2)}) copy-start(s32[128]{0:T(128)} %param.6) | copy-start | bytes 1540
  27.1 5.1 %collective-permute-start = (f32[64,24,128]{2,1,0:T(8,128)S(1)}, f32[64,24,128]{2,1,0:T(8,128)S(1)}, u32[]{:S(2)}, u32[]{:S(2)}) collective-permute-start(f32[64,24,128]{2,1,0:T(8,128)S(1)} %all_to_all.15.own_ref), channel_id=1, source_target_pairs={{0,16},{16,0},{1,17},{17,1},{2,18},{18,2},{3,19},{19,3},{4,20},{20... | collective-permute-start | bytes 2359304 | tf_op jit(solution)/shard_map/ppermute | solution.py:505
  32.2 18.1 %copy-start.1 = (bf16[640,2048]{1,0:T(8,128)(2,1)S(1)}, bf16[640,2048]{1,0:T(8,128)(2,1)}, u32[]{:S(2)}) copy-start(bf16[640,2048]{1,0:T(8,128)(2,1)} %constant.34.clone.whole_ref) | copy-start | bytes 7864324
  58.8 13.0 %all-to-all-start.2 = ((f32[32,16,128]{2,1,0:T(8,128)}), f32[32,16,128]{2,1,0:T(8,128)S(1)}, u32[]{:S(2)}, u32[]{:S(2)}) async-start(f32[32,16,128]{2,1,0:T(8,128)} %get-tuple-element.44), calls=%async_computation.2 | async-start | bytes 524288 | tf_op jit(solution)/shard_map/all_to_all | solution.py:508

commit v4 on v3

--- a/solution.py
+++ b/solution.py
@@ -11,7 +11,7 @@
 F32 = jnp.float32
 BF16 = jnp.bfloat16
 W = 2048
-CENTRE = 128 + 31
+CENTRE = (slice(48, 64), slice(15, 16))
 
 
 def _halves(matrix):
@@ -43,14 +43,27 @@
             part[h, :, h] = np.exp(400.0 * ya[:, None] * (da + shift)[None])[:, None, :]
         return part.reshape(128, 128)
 
-    cells = [along(s) for s in shifts]
-    factors = [_thrice(m) for m in cells] + [_thrice(np.concatenate([m.T for m in cells], axis=0))]
-    factors += [_thrice(along(0.0)), _thrice(along(0.0).T)]
+    cell = np.concatenate([np.exp(400.0 * ya[:, None] * (da + s)[None]) for s in shifts], axis=1)
+    high, low = _halves(np.concatenate([cell.T, cell.T], axis=1))
+    order = np.zeros((8, 4, 8, 8, 4, 4, 8), ml_dtypes.bfloat16)
+    for i, k, r in np.ndindex(8, 4, 8):
+        order[i, k, i, r, :, k, r] = 1
+    factors = [
+        _thrice(np.tile(cell, (2, 4))),
+        np.concatenate([high, high, low, np.zeros_like(low)], axis=0),
+        _thrice(along(0.0)),
+        _thrice(along(0.0).T),
+        order.reshape(2048, 128),
+    ]
     wholes = _halves(np.concatenate([whole(s) for s in shifts], axis=0)) + _halves(whole(0.0))
-    return np.concatenate(factors, axis=0), np.concatenate(wholes, axis=0)
-
-
-CELL, BACK, BASIC, BASIC_BACK = 0, 1536, 3072, 3456
+    up = np.exp(400.0 * yh.reshape(16, 2, 1) * dh[None, None])
+    of_row = np.repeat(up.transpose(0, 2, 1).reshape(128, 1, 2), 64, axis=2)
+    of_pixel = np.repeat(up.reshape(16, 1, 16), 8, axis=2)
+    ups = np.repeat(np.concatenate([of_row, of_pixel], axis=0), 8, axis=1).reshape(1152, 128)
+    return np.concatenate(factors, axis=0), np.concatenate(wholes, axis=0), ups.astype(np.float32)
+
+
+CELL, BACK, BASIC, BASIC_BACK, ORDER = 0, 384, 512, 896, 1280
 
 
 def dot(a, b):
@@ -154,33 +167,57 @@
     return jnp.concatenate([high, low, high], axis=1)
 
 
-def up_rows():
-    lane = lax.broadcasted_iota(jnp.int32, (16, 128), 1)
-    row = 2 * lax.broadcasted_iota(jnp.int32, (16, 128), 0) + lax.shift_right_logical(lane, 6)
-    yh = (row.astype(F32) + 0.5) / 32.0 - 0.5
-    dh = (lax.bitwise_and(lax.shift_right_logical(lane, 3), 7).astype(F32) - 3.5) / 128.0
-    up = jnp.exp(400.0 * yh * dh)
-    return [up[t : t + 1, :] for t in range(16)]
-
-
-def sums(u, factor_ref, up, cells):
-    n = u.shape[0]
+def up_of(up_ref, i):
+    h = up_ref[8 * i : 8 * i + 8, :]
+    return jnp.concatenate([h, h], axis=0)
+
+
+def total(parts):
+    while len(parts) > 1:
+        parts = [parts[i] + parts[i + 1] for i in range(0, len(parts), 2)]
+    return parts[0]
+
+
+def cell_sums(u, factor_ref, up_ref):
+    v = [None] * 8
+    for t in range(16):
+        part = u[:, 128 * t : 128 * t + 128]
+        for i in range(8):
+            term = part * up_of(up_ref, 8 * t + i)
+            v[i] = term if t == 0 else v[i] + term
+    return dot(thrice(jnp.concatenate(v, axis=0)), factor_ref[CELL : CELL + 384, :])
+
+
+def cell_back(e, factor_ref, up_ref):
+    high = e.astype(BF16).astype(F32)
+    lane = lax.broadcasted_iota(jnp.int32, e.shape, 1)
+    x = jnp.where(lax.shift_right_logical(lane, 5) == 1, e - high, high).astype(BF16)
+    z = dot(x, factor_ref[BACK : BACK + 128, :])
+    z = [z[16 * i : 16 * i + 16] for i in range(8)]
+    return jnp.concatenate(
+        [total([z[i] * up_of(up_ref, 8 * t + i) for i in range(8)]) for t in range(16)], axis=1)
+
+
+def ordered(mass, factor_ref):
+    x = jnp.concatenate(split3(mass), axis=0)
+    out = []
+    for i in range(8):
+        p = dot(x, factor_ref[ORDER + 256 * i : ORDER + 256 * i + 256, :])
+        out.append((p[:16] + p[16:32]) + p[32:])
+    return jnp.concatenate(out, axis=0)
+
+
+def sums(u, factor_ref, up_ref):
     x = thrice(jnp.concatenate([u[:, 128 * t : 128 * t + 128] for t in range(16)], axis=0))
-    out = []
-    for first in [CELL + 384 * k for k in range(4)] if cells else [BASIC]:
-        p = dot(x, factor_ref[first : first + 384, :])
-        parts = [p[n * t : n * t + n] * h for t, h in enumerate(up)]
-        while len(parts) > 1:
-            parts = [parts[i] + parts[i + 1] for i in range(0, len(parts), 2)]
-        out.append(parts[0] + swap(parts[0]))
-    return jnp.concatenate(out, axis=1)
-
-
-def cols(e, factor_ref, up):
-    n, groups = e.shape[0], e.shape[1] // 128
-    x = jnp.concatenate([e * jnp.concatenate([h] * groups, axis=1) for h in up], axis=0)
-    d = dot(thrice(x), factor_ref[BACK : BACK + 1536, :] if groups == 4 else factor_ref[BASIC_BACK : BASIC_BACK + 384, :])
-    return jnp.concatenate([d[n * t : n * t + n] for t in range(16)], axis=1)
+    p = dot(x, factor_ref[BASIC : BASIC + 384, :])
+    s = total([p[16 * t : 16 * t + 16] * up_of(up_ref, 128 + t) for t in range(16)])
+    return s + swap(s)
+
+
+def cols(e, factor_ref, up_ref):
+    x = jnp.concatenate([e * up_of(up_ref, 128 + t) for t in range(16)], axis=0)
+    d = dot(thrice(x), factor_ref[BASIC_BACK : BASIC_BACK + 384, :])
+    return jnp.concatenate([d[16 * t : 16 * t + 16] for t in range(16)], axis=1)
 
 
 def halves(e):
@@ -204,16 +241,17 @@
 
 
 def balanced(mass, s):
-    return mass * (s[:, CENTRE : CENTRE + 1] / s)
-
-
-def sweep_a(log_b, mass, d, factor_ref, up, beside):
+    return mass * (jnp.concatenate([s[CENTRE]] * 8, axis=0) / s)
+
+
+def sweep_a(log_b, mass, d, factor_ref, up_ref, beside):
     b = jnp.exp(log_b - jnp.max(log_b, axis=1, keepdims=True))
     for i in range(3):
         beside(i)
-        e = balanced(mass, sums(b / d, factor_ref, up, True))
-        d = cols(e, factor_ref, up)
-    return e, d
+        u = b / d
+        s = cell_sums(u, factor_ref, up_ref)
+        d = cell_back(balanced(mass, s), factor_ref, up_ref)
+    return u, s[CENTRE], d
 
 
 def over_k(x, op):
@@ -231,31 +269,31 @@
     return peak + jnp.log(over_k(jnp.exp(q - twice(peak)) * d, jnp.add))
 
 
-def sweep_b(log_b, mass, r, part, factor_ref, up, beside):
+def sweep_b(log_b, mass, r, part, factor_ref, up_ref, beside):
     for i in range(3):
         beside(5 + i)
         v = r + twice(log_b - part)
         top = jnp.max(v, axis=1, keepdims=True)
-        e = mass / sums(jnp.exp(v - top), factor_ref, up, False)
+        e = mass / sums(jnp.exp(v - top), factor_ref, up_ref)
         if i < 2:
-            part = column_part(r, top, cols(e, factor_ref, up))
+            part = column_part(r, top, cols(e, factor_ref, up_ref))
     return e, top
 
 
-def solve_pair(log_b_a, mass_a, mass_b, ids, d, part, factor_ref, up, send_ref, beside=lambda i: None):
+def solve_pair(log_b_a, mass_a, mass_b, ids, d, part, factor_ref, up_ref, send_ref, beside=lambda i: None):
     y = targets(0, W)
-    k = ids - 4.0 * jnp.floor(ids / 4.0)
     at_cell = cell_centre(jnp.floor(ids / 4.0))
     at_basic = basic_centre(ids)
-    e_a, d_a = sweep_a(log_b_a, mass_a, d, factor_ref, up, beside)
-    e_first = segment(e_a, k)
+    shift = (400.0 * (at_basic[1] - at_cell[1])) * y[1]
+    u, centre, d_a = sweep_a(log_b_a, mass_a, d, factor_ref, up_ref, beside)
+    e_first = mass_b * (centre / sums(u * jnp.exp(shift), factor_ref, up_ref))
     beside(3)
-    d_first = cols(e_first, factor_ref, up)
-    v = log_b_a - jnp.log(d_a) + (400.0 * (at_basic[1] - at_cell[1])) * y[1]
+    d_first = cols(e_first, factor_ref, up_ref)
+    v = log_b_a - jnp.log(d_a) + shift
     peak = over_k(v, jnp.maximum)
     beside(4)
     log_b_b = peak + jnp.log(over_k(jnp.exp(v - twice(peak)) * d_first, jnp.add))
-    e_second, top = sweep_b(log_b_b, mass_b, tilt(at_basic, y), part, factor_ref, up, beside)
+    e_second, top = sweep_b(log_b_b, mass_b, tilt(at_basic, y), part, factor_ref, up_ref, beside)
     rows = jnp.where(low_half((16, 128)), e_first, jnp.log(e_second) - top)
     for i in range(32):
         send_ref[i, :, :] = rows
@@ -294,16 +332,16 @@
     return ids, cells
 
 
-def start_kernel(place_ref, placement_ref, members_ref, factor_ref, sum_a_ref, sum_b_ref, keep_ref, own_ids_ref, onehot_ref,
+def start_kernel(place_ref, placement_ref, members_ref, factor_ref, up_ref, sum_a_ref, sum_b_ref, keep_ref, keep_up_ref, own_ids_ref, onehot_ref,
                  cell_ref, cells_ref, groups_ref, rows_ref, ids_ref):
     cell_col, cell_row = local_cells(placement_ref[...].astype(F32), place_ref[0])
     member_rows = member_rows_of(members_ref)
     ids = own_ids(member_rows, place_ref[1])
     y = targets(0, W)
-    up = up_rows()
-    sum_a_ref[...] = sums(nearness(cell_centre(jnp.floor(ids / 4.0)), y), factor_ref, up, True)
-    sum_b_ref[...] = sums(nearness(basic_centre(ids), y), factor_ref, up, False)
+    sum_a_ref[...] = cell_sums(nearness(cell_centre(jnp.floor(ids / 4.0)), y), factor_ref, up_ref)
+    sum_b_ref[...] = sums(nearness(basic_centre(ids), y), factor_ref, up_ref)
     keep_ref[...] = factor_ref[...]
+    keep_up_ref[...] = up_ref[...]
     own_ids_ref[...] = jnp.broadcast_to(ids, (16, 128))
     cells = jnp.floor(ids / 4.0)
     onehot_ref[...] = jnp.where(cell_row == cells, 1.0, 0.0)
@@ -313,15 +351,16 @@
 
 
 def first_kernel(place_ref, own_ref, other_ref, sum_a_ref, sum_b_ref, ids_ref, onehot_ref, cell_ref, cells_ref, near_ref,
-                 factor_ref, send_ref, here_ref, level_ref, mass_a_ref, mass_b_ref, d_ref, part_ref, table_ref):
-    ids, onehot, up = ids_ref[:, :1], onehot_ref[...], up_rows()
+                 factor_ref, up_ref, send_ref, here_ref, level_ref, mass_a_ref, mass_b_ref, d_ref, part_ref, table_ref):
+    ids, onehot = ids_ref[:, :1], onehot_ref[...]
     mass = []
     for part in (16, 17):
         rows = jnp.concatenate([own_ref[:, part, :], other_ref[:, part, :]], axis=0)
         mass.append(pick(onehot, rows))
-    mass_a = quadrupled(jnp.concatenate(mass, axis=1))
-    mass_b = segment(mass_a, ids - 4.0 * jnp.floor(ids / 4.0))
-    d = cols(balanced(mass_a, sum_a_ref[...]), factor_ref, up)
+    mass = jnp.concatenate(mass, axis=1)
+    mass_a = ordered(mass, factor_ref)
+    mass_b = segment(quadrupled(mass), ids - 4.0 * jnp.floor(ids / 4.0))
+    d = cell_back(balanced(mass_a, sum_a_ref[...]), factor_ref, up_ref)
     log_b = []
     for t in range(16):
         rows = [ref[x * 16 + t, 0:16, :] for ref in (own_ref, other_ref) for x in range(4)]
@@ -332,7 +371,7 @@
     log_b = jnp.concatenate(log_b, axis=1)
     at_basic = basic_centre(ids)
     top = 200.0 * (at_basic[0] * at_basic[0] + at_basic[1] * at_basic[1])
-    part = column_part(tilt(at_basic, targets(0, W)), top, cols(mass_b / sum_b_ref[...], factor_ref, up))
+    part = column_part(tilt(at_basic, targets(0, W)), top, cols(mass_b / sum_b_ref[...], factor_ref, up_ref))
     mass_a_ref[...] = mass_a
     mass_b_ref[...] = mass_b
     d_ref[...] = d
@@ -343,7 +382,7 @@
         at = slice(256 * block, 256 * block + 256)
         level_ref[:, at] = near_level(near, cells_ref[...], table_ref[:, at], cell_col, targets(256 * block, 256))
 
-    solve_pair(log_b, mass_a, mass_b, ids, d, part, factor_ref, up, send_ref, level)
+    solve_pair(log_b, mass_a, mass_b, ids, d, part, factor_ref, up_ref, send_ref, level)
 
 
 def received(recv_ref):
@@ -409,7 +448,7 @@
 
 
 def second_kernel(place_ref, own_ids_ref, recv_ref, level_ref, groups_ref, rows_ref, ids_ref, mass_a_ref, mass_b_ref, d_ref,
-                  part_ref, factor_ref, whole_ref, send_ref, here_ref):
+                  part_ref, factor_ref, up_ref, whole_ref, send_ref, here_ref):
     here_ref[...] = whole_ref[:, pl.ds(pl.multiple_of(place_ref[2] * 128, 128), 128)]
     gather = gathered(recv_ref, groups_ref, rows_ref)
     centre = basic_centre(ids_ref[:, :1])
@@ -419,7 +458,7 @@
         v, d = near_margins(gather, level_ref[:, at], centre, targets(256 * block, 256), whole_ref[:, at])
         log_b.append(mix([v[16 * k : 16 * k + 16] for k in range(4)], [d[16 * k : 16 * k + 16] for k in range(4)]))
     solve_pair(jnp.concatenate(log_b, axis=1), mass_a_ref[...], mass_b_ref[...], own_ids_ref[:, :1], d_ref[...], part_ref[...],
-               factor_ref, up_rows(), send_ref)
+               factor_ref, up_ref, send_ref)
 
 
 def middle_kernel(place_ref, placement_ref, members_ref, log_b_ref, recv_ref, whole_ref, level_ref, cells_ref, groups_ref,
@@ -484,11 +523,11 @@
     )(*inputs)
 
 
-FACTORS = (3840, 128, BF16)
+FACTORS = [(3328, 128, BF16), (1152, 128)]
 NEAR = [(256, 128, BF16), (1024, 512, BF16), (320, 512, BF16), (320, 128)]
 
 
-def on_device(placement_a, members_b, source_mass, init_log, factors, wholes):
+def on_device(placement_a, members_b, source_mass, init_log, factors, wholes, ups):
     x, c, z, y = (lax.axis_index(name) for name in ("x", "c", "z", "y"))
     share = z * 4 + y
     place = jnp.stack([c, x * 8 + c * 4 + y, share, x]).astype(jnp.int32)
@@ -500,18 +539,18 @@
     mass = lax.dynamic_slice_in_dim(source_mass, share, 1, 0).reshape(2, 128)
     block = jnp.concatenate([log_b, mass, jnp.zeros((6, 128), F32)], axis=0)
     own = lax.all_to_all(jnp.broadcast_to(block[None], (64, 24, 128)), ("x", "z", "y"), 0, 0, tiled=True)
-    sum_a, sum_b, factors, own_ids_, onehot, cell, cells, groups, rows, ids = call(
-        start_kernel, index + (factors,), [(16, 512), (16, 128), FACTORS, (16, 128), (16, 128), (128, 128)] + NEAR)
+    sum_a, sum_b, factors, ups, held, onehot, cell, cells, groups, rows, ids = call(
+        start_kernel, index + (factors, ups), [(128, 128), (16, 128)] + FACTORS + [(16, 128), (16, 128), (128, 128)] + NEAR)
     other = lax.ppermute(own, "c", [(0, 1), (1, 0)])
 
     def exchange(rows):
         return lax.all_to_all(rows, ("x", "c", "y"), 0, 0, tiled=True)
 
     send, here, level, *rest = call(
-        first_kernel, (place, own, other, sum_a, sum_b, own_ids_, onehot, cell, cells, ids, factors),
-        [(32, 16, 128), (128, 128), (256, W), (16, 512), (16, 128), (16, W), (8, W)], [pltpu.VMEM((128, W), F32)])
+        first_kernel, (place, own, other, sum_a, sum_b, held, onehot, cell, cells, ids, factors, ups),
+        [(32, 16, 128), (128, 128), (256, W), (128, 128), (16, 128), (16, W), (8, W)], [pltpu.VMEM((128, W), F32)])
     first = exchange(send)
-    send, whole = call(second_kernel, (place, own_ids_, first, level, groups, rows, ids, *rest, factors, wholes),
+    send, whole = call(second_kernel, (place, held, first, level, groups, rows, ids, *rest, factors, ups, wholes),
                        [(32, 16, 128), (640, 128, BF16)])
     second = exchange(send)
     level, _, groups, rows, ids = call(middle_kernel, index + (here, first, whole), [(256, 128)] + NEAR)

time: 74.8 us -> 73.4 us (0.981)
  Pallas kernels: 23 us -> 21.6 us
    pallas_call x5, Pallas kernels: 23 us -> 21.6 us  [call(): pl.pallas_call(body, out_shape=[jax.ShapeDtypeStruct(s[:-1], BF16) if s[-...]
where the time goes in v4:
time: 73.4 us; the launch traced here: 73.2 us
  blocking collectives  37.9 us (52%)
  Pallas kernels  21.6 us (29%)
  starting transfers between devices  6.86 us (9%)
  waiting for transfers between devices  4.62 us (6%)
  local copies, waits for them, and re-layouts  1.91 us (3%)
    all_to_all x1, blocking collectives, on_device(): lax.all_to_all(jnp.broadcast_to(block[None], (64, 24, 128)), ('x', 'z', '...  25.9 us
    pallas_call x5, Pallas kernels, call(): pl.pallas_call(body, out_shape=[jax.ShapeDtypeStruct(s[:-1], BF16) if s[-...  21.6 us
    all_to_all x1, blocking collectives, exchange(): return lax.all_to_all(rows, ('x', 'c', 'y'), 0, 0, tiled=True)  12 us
    all_to_all x1, waiting for transfers between devices, exchange(): return lax.all_to_all(rows, ('x', 'c', 'y'), 0, 0, tiled=True)  4.61 us
    all_to_all x1, starting transfers between devices, exchange(): return lax.all_to_all(rows, ('x', 'c', 'y'), 0, 0, tiled=True)  4.13 us
    ppermute x1, starting transfers between devices, on_device(): other = lax.ppermute(own, 'c', [(0, 1), (1, 0)])  2.72 us
  transfers between devices with their start and end apart: 2, of which 1 were waited for; matrix products, arithmetic and copies ran while one was open for 1% of the time, Pallas kernels for 8%

profile of v4, /device:TPU:1, one launch (start us, length us, event | category | flops | bytes accessed | tf_op | source)
XLA Modules:
  0.0 73.2 jit_solution(8878014216088101476)
XLA Ops:
  0.0 0.0 copy-start
  0.0 0.0 copy-start.4
  0.0 0.0 copy-start.3
  0.0 0.0 copy-start.2
  0.0 1.0 %fusion.3 = (f32[16,1,128]{2,1,0:T(1,128)S(1)}, f32[16,1,128]{2,1,0:T(1,128)S(1)}, f32[16,1,128]{2,1,0:T(1,128)S(1)}, f32[16,1,128]{2,1,0:T(1,128)S(1)}) fusion(f32[16,4,128]{2,1,0:T(4,128)} %param.10), kind=kLoop, calls=%fused_computation.9 | loop fusion | bytes 65536 | tf_op jit(solution)/shard_map/slice | solution.py:535
  1.0 0.0 copy-done
  1.0 0.1 pad.2.clone
  1.1 0.1 maximum_maximum_fusion
  1.2 0.1 broadcast_in_dim.10
  1.3 25.9 %all_to_all.15.own_ref = f32[64,24,128]{2,1,0:T(8,128)S(1)} all-to-all(f32[64,24,128]{2,1,0:T(8,128)S(1)} %broadcast_in_dim.10), channel_id=1, replica_groups=mesh['x'=4,'c'=2,'z'=4,'y'=4] {'x','z','y'}, dimensions={0} | all-to-all | bytes 1572864 | tf_op jit(solution)/shard_map/all_to_all | solution.py:541
  27.1 2.7 %collective-permute-start = (f32[64,24,128]{2,1,0:T(8,128)S(1)}, f32[64,24,128]{2,1,0:T(8,128)S(1)}, u32[]{:S(2)}, u32[]{:S(2)}) collective-permute-start(f32[64,24,128]{2,1,0:T(8,128)S(1)} %all_to_all.15.own_ref), channel_id=1, source_target_pairs={{0,16},{16,0},{1,17},{17,1},{2,18},{18,2},{3,19},{19,3},{4,20},{20... | collective-permute-start | bytes 2359304 | tf_op jit(solution)/shard_map/ppermute | solution.py:544
  29.8 0.8 %copy.8.members_ref = s32[128,4]{1,0:T(8,128)S(1)} copy(s32[128,4]{0,1:T(4,128)} %param.8) | data formatting | bytes 4096 | tf_op args[1]
  30.6 0.1 pad_add_fusion.place_ref
  30.7 0.0 copy-done.4
  30.7 0.0 copy-done.3
  30.7 0.0 copy-done.2
  30.7 1.5 %shard_map.73 = (f32[128,128]{1,0:T(8,128)S(1)}, f32[16,128]{1,0:T(8,128)S(1)}, bf16[3328,128]{1,0:T(8,128)(2,1)S(1)}, f32[1152,128]{1,0:T(8,128)S(1)}, f32[16,1...) custom-call(s32[4]{0:T(128)S(1)} %pad_add_fusion.place_ref, ...), custom_call_target="tpu_custom_call" | custom-call | flops 1000000000 | bytes 1000000 | tf_op jit(solution)/shard_map/pallas_call | solution.py:515
  32.2 0.0 copy-start.1
  32.3 0.0 collective-permute-done.other_ref
  32.3 5.3 %shard_map.74 = (f32[32,16,128]{2,1,0:T(8,128)S(1)}, f32[128,128]{1,0:T(8,128)S(1)}, f32[256,2048]{1,0:T(8,128)S(1)}, f32[128,128]{1,0:T(8,128)S(1)}, f32[16,128...) custom-call(s32[4]{0:T(128)S(1)} %pad_add_fusion.place_ref, f32[64,24,128]{2,1,0:T(8,128)S(1)} %all_to_all.15.own_ref, ...), custom_call_target="tpu_custom_call" | custom-call | flops 1000000000 | bytes 1000000 | tf_op jit(solution)/shard_map/pallas_call | solution.py:515
  37.5 12.0 %all_to_all.16.recv_ref = f32[32,16,128]{2,1,0:T(8,128)S(1)} all-to-all(f32[32,16,128]{2,1,0:T(8,128)S(1)} %get-tuple-element.38), channel_id=1, replica_groups=mesh['x'=4,'c'=2,'z'=4,'y'=4] {'x','c','y'}, dimensions={0} | all-to-all | bytes 524288 | tf_op jit(solution)/shard_map/all_to_all | solution.py:547
  49.5 0.0 copy-done.1
  49.5 7.9 %shard_map.75 = (f32[32,16,128]{2,1,0:T(8,128)}, bf16[640,128]{1,0:T(8,128)(2,1)S(1)}) custom-call(s32[4]{0:T(128)S(1)} %pad_add_fusion.place_ref, f32[16,128]{1,0:T(8,128)S(1)} %get-tuple-element.29.ids_ref.own_ids_ref, f32[32,16,128]{2,1,0:T(8,128)S(1)} %all_to_all.16.recv_ref, f32[256,2048]{1,0:T(8,128)S(1)} %get-tuple-element.39.level_ref, ...), custom_call_target="tpu_custom_call" | custom-call | flops 1000000000 | bytes 1000000 | tf_op jit(solution)/shard_map/pallas_call | solution.py:515
  57.5 4.1 %all-to-all-start.2 = ((f32[32,16,128]{2,1,0:T(8,128)}), f32[32,16,128]{2,1,0:T(8,128)S(1)}, u32[]{:S(2)}, u32[]{:S(2)}) async-start(f32[32,16,128]{2,1,0:T(8,128)} %get-tuple-element.46), calls=%async_computation.2 | async-start | bytes 524288 | tf_op jit(solution)/shard_map/all_to_all | solution.py:547
  61.6 4.3 %shard_map.76 = (f32[256,128]{1,0:T(8,128)S(1)}, bf16[256,128]{1,0:T(8,128)(2,1)}, bf16[1024,512]{1,0:T(8,128)(2,1)S(1)}, bf16[320,512]{1,0:T(8,128)(2,1)S(1)}, f32[320,128]{1,0:T(8,128)S(1)}) custom-call(s32[4]{0:T(128)S(1)} %pad_add_fusion.place_ref, s32[1,128]{1,0:T(1,128)S(1)} %bitcast.17, s32[128,4]{1,0:T(8,128)S(1)} %copy.8.members_ref, ...), custom_call_target="tpu_custom_call" | custom-call | flops 1000000000 | bytes 1000000 | tf_op jit(solution)/shard_map/pallas_call | solution.py:515
  65.9 4.6 %all-to-all-done.2.recv_ref = f32[32,16,128]{2,1,0:T(8,128)S(1)} async-done(((f32[32,16,128]{2,1,0:T(8,128)}), f32[32,16,128]{2,1,0:T(8,128)S(1)}, u32[]{:S(2)}, u32[]{:S(2)}) %all-to-all-start.2) | async-done | bytes 262176 | tf_op jit(solution)/shard_map/all_to_all | solution.py:547
  70.5 2.6 %shard_map.77 = f32[16,4,128]{2,1,0:T(4,128)} custom-call(s32[4]{0:T(128)S(1)} %pad_add_fusion.place_ref, f32[32,16,128]{2,1,0:T(8,128)S(1)} %all-to-all-done.2.recv_ref, f32[256,128]{1,0:T(8,128)S(1)} %get-tuple-element.49.level_ref, bf16[1024,512]{1,0:T(8,128)(2,1)S(1)} %get-tuple-element.50.groups_ref, bf16[320,512]{1,0:T(8,128)(2,1)S(1)} %get-tuple-element.51.rows_ref, ...), custom_call_target="tpu_custom_call" | custom-call | flops 1000000000 | bytes 1000000 | tf_op jit(solution)/shard_map/pallas_call | solution.py:515
  (3 shorter events, 0.0 us)
Async XLA Ops:
  0.0 1.0 %copy-start = (f32[16,256]{1,0:T(8,128)S(1)}, f32[16,256]{1,0:T(8,128)}, u32[]{:S(2)}) copy-start(f32[16,256]{1,0:T(8,128)} %param.9) | copy-start | bytes 49156
  0.0 30.7 %copy-start.4 = (f32[1152,128]{1,0:T(8,128)S(1)}, f32[1152,128]{1,0:T(8,128)}, u32[]{:S(2)}) copy-start(f32[1152,128]{1,0:T(8,128)} %constant.37.clone.up_ref) | copy-start | bytes 1769476
  0.0 30.7 %copy-start.3 = (bf16[3328,128]{1,0:T(8,128)(2,1)S(1)}, bf16[3328,128]{1,0:T(8,128)(2,1)}, u32[]{:S(2)}) copy-start(bf16[3328,128]{1,0:T(8,128)(2,1)} %constant.35.clone.factor_ref) | copy-start | bytes 2555908
  0.0 30.7 %copy-start.2 = (s32[128]{0:T(128)S(1)}, s32[128]{0:T(128)}, u32[]{:S(2)}) copy-start(s32[128]{0:T(128)} %param.7) | copy-start | bytes 1540
  27.1 5.1 %collective-permute-start = (f32[64,24,128]{2,1,0:T(8,128)S(1)}, f32[64,24,128]{2,1,0:T(8,128)S(1)}, u32[]{:S(2)}, u32[]{:S(2)}) collective-permute-start(f32[64,24,128]{2,1,0:T(8,128)S(1)} %all_to_all.15.own_ref), channel_id=1, source_target_pairs={{0,16},{16,0},{1,17},{17,1},{2,18},{18,2},{3,19},{19,3},{4,20},{20... | collective-permute-start | bytes 2359304 | tf_op jit(solution)/shard_map/ppermute | solution.py:544
  32.2 17.3 %copy-start.1 = (bf16[640,2048]{1,0:T(8,128)(2,1)S(1)}, bf16[640,2048]{1,0:T(8,128)(2,1)}, u32[]{:S(2)}) copy-start(bf16[640,2048]{1,0:T(8,128)(2,1)} %constant.36.clone.whole_ref) | copy-start | bytes 7864324
  57.5 13.0 %all-to-all-start.2 = ((f32[32,16,128]{2,1,0:T(8,128)}), f32[32,16,128]{2,1,0:T(8,128)S(1)}, u32[]{:S(2)}, u32[]{:S(2)}) async-start(f32[32,16,128]{2,1,0:T(8,128)} %get-tuple-element.46), calls=%async_computation.2 | async-start | bytes 524288 | tf_op jit(solution)/shard_map/all_to_all | solution.py:547

commit v5 on v4

--- a/solution.py
+++ b/solution.py
@@ -55,7 +55,8 @@
         _thrice(along(0.0).T),
         order.reshape(2048, 128),
     ]
-    wholes = _halves(np.concatenate([whole(s) for s in shifts], axis=0)) + _halves(whole(0.0))
+    high, low = _halves(whole(0.0))
+    wholes = _halves(np.concatenate([whole(s) for s in shifts], axis=0)) + (high, high, low, np.zeros_like(low))
     up = np.exp(400.0 * yh.reshape(16, 2, 1) * dh[None, None])
     of_row = np.repeat(up.transpose(0, 2, 1).reshape(128, 1, 2), 64, axis=2)
     of_pixel = np.repeat(up.reshape(16, 1, 16), 8, axis=2)
@@ -220,8 +221,9 @@
     return jnp.concatenate([d[16 * t : 16 * t + 16] for t in range(16)], axis=1)
 
 
-def halves(e):
-    return jnp.concatenate(split2(e), axis=0)
+def wide(e):
+    high = e.astype(BF16).astype(F32)
+    return jnp.concatenate([jnp.where(low_half(e.shape), high, e - high), high], axis=1).astype(BF16)
 
 
 def cell_cols(e, whole):
@@ -231,9 +233,7 @@
 
 
 def basic_cols(e, whole):
-    n = e.shape[0] // 2
-    p = dot(e, whole[512:])
-    return p[:n] + p[n:]
+    return dot(e, whole[512:])
 
 
 def nearness(centre, y):
@@ -301,17 +301,17 @@
 
 def member_rows_of(members_ref):
     members = members_ref[...].astype(F32)
-    return [to_row(members[:, k : k + 1]) for k in range(4)]
-
-
-def exchange_ids(members_ref):
-    members = members_ref[...].astype(F32)
+    return [members[k : k + 1, :] for k in range(4)]
+
+
+def exchange_ids(member_rows):
+    members = [to_col(row) for row in member_rows]
     slot = lax.broadcasted_iota(jnp.int32, (128, 128), 0)
     lane = lax.broadcasted_iota(jnp.int32, (128, 128), 1)
     k = lax.bitwise_and(lax.shift_right_logical(lane, 2), 3)
-    value = jnp.broadcast_to(members[:, 0:1], (128, 128))
+    value = jnp.broadcast_to(members[0], (128, 128))
     for i in range(1, 4):
-        value = jnp.where(k == i, jnp.broadcast_to(members[:, i : i + 1], (128, 128)), value)
+        value = jnp.where(k == i, jnp.broadcast_to(members[i], (128, 128)), value)
     of_lane = 4 * lax.shift_right_logical(lane, 4) + lax.bitwise_and(lane, 3)
     return jnp.concatenate(
         [jnp.sum(jnp.where(slot == of_lane + 32 * t, value, 0.0), axis=0, keepdims=True) for t in range(4)], axis=1)
@@ -332,22 +332,28 @@
     return ids, cells
 
 
-def start_kernel(place_ref, placement_ref, members_ref, factor_ref, up_ref, sum_a_ref, sum_b_ref, keep_ref, keep_up_ref, own_ids_ref, onehot_ref,
-                 cell_ref, cells_ref, groups_ref, rows_ref, ids_ref):
+def start_kernel(place_ref, placement_hbm, members_hbm, factor_hbm, up_hbm, sum_a_ref, sum_b_ref, factor_ref, up_ref, own_ids_ref, onehot_ref,
+                 cell_ref, cells_ref, groups_ref, rows_ref, ids_ref, placement_ref, members_ref, sems):
+    pairs = ((placement_hbm, placement_ref), (members_hbm, members_ref), (factor_hbm, factor_ref), (up_hbm, up_ref))
+    copies = [pltpu.make_async_copy(*pair, sems.at[i]) for i, pair in enumerate(pairs)]
+    for copy in copies:
+        copy.start()
+    for copy in copies[:2]:
+        copy.wait()
     cell_col, cell_row = local_cells(placement_ref[...].astype(F32), place_ref[0])
     member_rows = member_rows_of(members_ref)
     ids = own_ids(member_rows, place_ref[1])
-    y = targets(0, W)
-    sum_a_ref[...] = cell_sums(nearness(cell_centre(jnp.floor(ids / 4.0)), y), factor_ref, up_ref)
-    sum_b_ref[...] = sums(nearness(basic_centre(ids), y), factor_ref, up_ref)
-    keep_ref[...] = factor_ref[...]
-    keep_up_ref[...] = up_ref[...]
     own_ids_ref[...] = jnp.broadcast_to(ids, (16, 128))
     cells = jnp.floor(ids / 4.0)
     onehot_ref[...] = jnp.where(cell_row == cells, 1.0, 0.0)
     cell_ref[...] = jnp.broadcast_to(cell_col, (128, 128))
     want = jnp.concatenate([4.0 * cells + float(k) for k in range(4)], axis=0)
-    near_cells(want, member_rows, cell_row, exchange_ids(members_ref), cells_ref, groups_ref, rows_ref, ids_ref)
+    near_cells(want, member_rows, cell_row, exchange_ids(member_rows), cells_ref, groups_ref, rows_ref, ids_ref)
+    for copy in copies[2:]:
+        copy.wait()
+    y = targets(0, W)
+    sum_a_ref[...] = cell_sums(nearness(cell_centre(jnp.floor(ids / 4.0)), y), factor_ref, up_ref)
+    sum_b_ref[...] = sums(nearness(basic_centre(ids), y), factor_ref, up_ref)
 
 
 def first_kernel(place_ref, own_ref, other_ref, sum_a_ref, sum_b_ref, ids_ref, onehot_ref, cell_ref, cells_ref, near_ref,
@@ -355,7 +361,8 @@
     ids, onehot = ids_ref[:, :1], onehot_ref[...]
     mass = []
     for part in (16, 17):
-        rows = jnp.concatenate([own_ref[:, part, :], other_ref[:, part, :]], axis=0)
+        at = pl.ds(part, 64, stride=18)
+        rows = jnp.concatenate([own_ref[at, :], other_ref[at, :]], axis=0)
         mass.append(pick(onehot, rows))
     mass = jnp.concatenate(mass, axis=1)
     mass_a = ordered(mass, factor_ref)
@@ -363,7 +370,8 @@
     d = cell_back(balanced(mass_a, sum_a_ref[...]), factor_ref, up_ref)
     log_b = []
     for t in range(16):
-        rows = [ref[x * 16 + t, 0:16, :] for ref in (own_ref, other_ref) for x in range(4)]
+        starts = [18 * (16 * x + t) for x in range(4)]
+        rows = [ref[i : i + 16, :] for ref in (own_ref, other_ref) for i in starts]
         rows = jnp.concatenate(rows, axis=0)
         table_ref[:, 128 * t : 128 * t + 128] = rows
         log_b.append(pick(onehot, rows))
@@ -430,9 +438,10 @@
     by_k = dot(groups_ref[...], packed(f))
     o = rows_ref[...]
     high, mid, low = split3(f)
-    e0, e1, top = unpack((dot(o, high) + dot(o, mid)) + dot(o, low))
+    two = dot(o, jnp.concatenate([high, mid], axis=1))
+    e0, e1, top = unpack((two[:, :128] + two[:, 128:]) + dot(o, low))
     by_k = [by_k[256 * k : 256 * k + 256] for k in range(4)]
-    return cell_halves(by_k), halves(e0[:256]), halves(e1), top
+    return cell_halves(by_k), wide(e0[:256]), wide(e1), top
 
 
 def near_margins(gather, level, centre, y, whole):
@@ -465,11 +474,10 @@
                   rows_ref, ids_ref):
     cell_col, cell_row = local_cells(placement_ref[...].astype(F32), place_ref[0])
     member_rows = member_rows_of(members_ref)
-    members = members_ref[...].astype(F32)
     share = place_ref[2]
     y = targets(share * 128, 128)
     whole = whole_ref[...]
-    b_ids = [members[:, k : k + 1] for k in range(4)]
+    b_ids = [to_col(row) for row in member_rows]
     b_cell = jnp.concatenate([jnp.where(cell_row == jnp.floor(i / 4.0), 1.0, 0.0) for i in b_ids], axis=0)
     b_tilt = [tilt(basic_centre(i), y) for i in b_ids]
     a_tilt = [tilt(basic_centre(4.0 * cell_col + float(k)), y) for k in range(4)]
@@ -482,7 +490,7 @@
     gamma = pick(b_cell, log_b_ref[...] - jnp.log(cell_cols(e_cell, whole)) - tilt(cell_centre(cell_col), y))
     e0, e1, top = unpack(every)
     _, ea, a_top = unpack(by_k)
-    d0, d1, da = [basic_cols(halves(e), whole) for e in (e0, e1, ea)]
+    d0, d1, da = [basic_cols(wide(e), whole) for e in (e0, e1, ea)]
     log_b1 = mix([gamma[a] + t for a, t in zip(parts, b_tilt)], [d0[a] for a in parts])
     gamma1 = log_b1 - mix([t - top[a] for a, t in zip(parts, b_tilt)], [d1[a] for a in parts])
     log_b = []
@@ -495,7 +503,7 @@
     first = place_ref[3] * 16 + lax.broadcasted_iota(jnp.int32, (16, 128), 0)
     own_cells = jnp.sum(jnp.where(lane == first, jnp.broadcast_to(cell_row, (16, 128)), 0.0), axis=1, keepdims=True)
     want = jnp.concatenate([4.0 * own_cells + float(k) for k in range(4)], axis=0)
-    ids, cells = near_cells(want, member_rows, cell_row, exchange_ids(members_ref), cells_ref, groups_ref, rows_ref, ids_ref)
+    ids, cells = near_cells(want, member_rows, cell_row, exchange_ids(member_rows), cells_ref, groups_ref, rows_ref, ids_ref)
     level_ref[...] = near_level(ids[:256], cells, log_b, cell_col, y)
 
 
@@ -508,14 +516,17 @@
         out_ref[:, k, :] = out[16 * k : 16 * k + 16]
 
 
-def call(body, inputs, outs, scratch=(), work=1):
+def call(body, inputs, outs, scratch=(), work=1, far=0):
+    near = len(inputs) - far
+    inputs = inputs[:near] + tuple(pltpu.with_memory_space_constraint(v, pltpu.HBM) for v in inputs[near:])
+
     def spec(value):
         return pl.BlockSpec(memory_space=pltpu.SMEM if value.shape == (4,) else pltpu.VMEM)
 
     return pl.pallas_call(
         body,
         out_shape=[jax.ShapeDtypeStruct(s[:-1], BF16) if s[-1] is BF16 else jax.ShapeDtypeStruct(s, F32) for s in outs],
-        in_specs=[spec(value) for value in inputs],
+        in_specs=[spec(value) for value in inputs[:near]] + [pl.BlockSpec(memory_space=pltpu.HBM)] * far,
         out_specs=[pl.BlockSpec(memory_space=pltpu.VMEM)] * len(outs),
         scratch_shapes=list(scratch),
         compiler_params=pltpu.CompilerParams(vmem_limit_bytes=24 * 2**20),
@@ -531,17 +542,19 @@
     x, c, z, y = (lax.axis_index(name) for name in ("x", "c", "z", "y"))
     share = z * 4 + y
     place = jnp.stack([c, x * 8 + c * 4 + y, share, x]).astype(jnp.int32)
-    index = (place, placement_a.reshape(1, 128), members_b)
+    index = (place, placement_a.reshape(1, 128), members_b.T)
     v = [init_log[:, k, :] for k in range(4)]
     peak = jnp.maximum(jnp.maximum(v[0], v[1]), jnp.maximum(v[2], v[3]))
     e = [jnp.exp(a - peak) for a in v]
     log_b = peak + jnp.log((e[0] + e[1]) + (e[2] + e[3])) + float(np.log(64.0 / W))
     mass = lax.dynamic_slice_in_dim(source_mass, share, 1, 0).reshape(2, 128)
-    block = jnp.concatenate([log_b, mass, jnp.zeros((6, 128), F32)], axis=0)
-    own = lax.all_to_all(jnp.broadcast_to(block[None], (64, 24, 128)), ("x", "z", "y"), 0, 0, tiled=True)
+    block = jnp.concatenate([log_b, mass], axis=0).reshape(9, 2, 128)
+    own = lax.all_to_all(jnp.broadcast_to(block[None], (64, 9, 2, 128)), ("x", "z", "y"), 0, 0, tiled=True)
     sum_a, sum_b, factors, ups, held, onehot, cell, cells, groups, rows, ids = call(
-        start_kernel, index + (factors, ups), [(128, 128), (16, 128)] + FACTORS + [(16, 128), (16, 128), (128, 128)] + NEAR)
-    other = lax.ppermute(own, "c", [(0, 1), (1, 0)])
+        start_kernel, index + (factors, ups), [(128, 128), (16, 128)] + FACTORS + [(16, 128), (16, 128), (128, 128)] + NEAR,
+        [pltpu.VMEM((1, 128), jnp.int32), pltpu.VMEM((4, 128), jnp.int32), pltpu.SemaphoreType.DMA((4,))], far=4)
+    other = lax.ppermute(own, "c", [(0, 1), (1, 0)]).reshape(1152, 128)
+    own = own.reshape(1152, 128)
 
     def exchange(rows):
         return lax.all_to_all(rows, ("x", "c", "y"), 0, 0, tiled=True)
@@ -551,7 +564,7 @@
         [(32, 16, 128), (128, 128), (256, W), (128, 128), (16, 128), (16, W), (8, W)], [pltpu.VMEM((128, W), F32)])
     first = exchange(send)
     send, whole = call(second_kernel, (place, held, first, level, groups, rows, ids, *rest, factors, ups, wholes),
-                       [(32, 16, 128), (640, 128, BF16)])
+                       [(32, 16, 128), (768, 128, BF16)])
     second = exchange(send)
     level, _, groups, rows, ids = call(middle_kernel, index + (here, first, whole), [(256, 128)] + NEAR)
     (out,) = call(last_kernel, (place, second, level, groups, rows, ids, whole), [(16, 4, 128)])

time: 73.4 us -> 71.3 us (0.971)
  blocking collectives: 37.9 us -> 36.1 us
  local copies, waits for them, and re-layouts: 1.91 us -> 1.13 us
    all_to_all x1, blocking collectives: 25.9 us -> 24 us  [on_device(): lax.all_to_all(jnp.broadcast_to(block[None], (64, 9, 2, 128)), ('x', 'z',...]
    unnamed x11 -> x8, local copies, waits for them, and re-layouts: 0.81 us -> 0.02 us
  transfers between devices with their start and end apart: 2 -> 2, of which waited for: 1 -> 1; matrix products, arithmetic and copies ran while one was open for 1% -> 0% of each run, Pallas kernels for 8% -> 9%
where the time goes in v5:
time: 71.3 us; the launch traced here: 70.9 us
  blocking collectives  36.1 us (51%)
  Pallas kernels  21.9 us (31%)
  starting transfers between devices  6.66 us (9%)
  waiting for transfers between devices  5.02 us (7%)
  local copies, waits for them, and re-layouts  1.13 us (2%)
    all_to_all x1, blocking collectives, on_device(): lax.all_to_all(jnp.broadcast_to(block[None], (64, 9, 2, 128)), ('x', 'z',...  24 us
    pallas_call x5, Pallas kernels, call(): pl.pallas_call(body, out_shape=[jax.ShapeDtypeStruct(s[:-1], BF16) if s[-...  21.9 us
    all_to_all x1, blocking collectives, exchange(): return lax.all_to_all(rows, ('x', 'c', 'y'), 0, 0, tiled=True)  12 us
    all_to_all x1, waiting for transfers between devices, exchange(): return lax.all_to_all(rows, ('x', 'c', 'y'), 0, 0, tiled=True)  5.02 us
    all_to_all x1, starting transfers between devices, exchange(): return lax.all_to_all(rows, ('x', 'c', 'y'), 0, 0, tiled=True)  4.12 us
    ppermute x1, starting transfers between devices, on_device(): other = lax.ppermute(own, 'c', [(0, 1), (1, 0)]).reshape(1152, 128)  2.54 us
  transfers between devices with their start and end apart: 2, of which 1 were waited for; matrix products, arithmetic and copies ran while one was open for 0% of the time, Pallas kernels for 9%

profile of v5, /device:TPU:1, one launch (start us, length us, event | category | flops | bytes accessed | tf_op | source)
XLA Modules:
  0.0 70.9 jit_solution(15013939283881092707)
XLA Ops:
  0.0 0.0 copy-start
  0.0 0.9 %fusion.3 = (f32[16,1,128]{2,1,0:T(1,128)S(1)}, f32[16,1,128]{2,1,0:T(1,128)S(1)}, f32[16,1,128]{2,1,0:T(1,128)S(1)}, f32[16,1,128]{2,1,0:T(1,128)S(1)}) fusion(f32[16,4,128]{2,1,0:T(4,128)} %param.10), kind=kLoop, calls=%fused_computation.9 | loop fusion | bytes 65536 | tf_op jit(solution)/shard_map/slice | solution.py:546
  0.9 0.0 copy-done
  1.0 0.2 broadcast_in_dim.8
  1.2 24.0 %all_to_all.15 = f32[64,9,2,128]{3,2,1,0:T(2,128)S(1)} all-to-all(f32[64,9,2,128]{3,2,1,0:T(2,128)S(1)} %broadcast_in_dim.8), channel_id=1, replica_groups=mesh['x'=4,'c'=2,'z'=4,'y'=4] {'x','z','y'}, dimensions={0} | all-to-all | bytes 1179648 | tf_op jit(solution)/shard_map/all_to_all | solution.py:552
  25.2 2.5 %collective-permute-start = (f32[64,9,2,128]{3,2,1,0:T(2,128)S(1)}, f32[64,9,2,128]{3,2,1,0:T(2,128)S(1)}, u32[]{:S(2)}, u32[]{:S(2)}) collective-permute-start(f32[64,9,2,128]{3,2,1,0:T(2,128)S(1)} %all_to_all.15), channel_id=1, source_target_pairs={{0,16},{16,0},{1,17},{17,1},{2,18},{18,2},{3,19},{19,3},{4,20},{20... | collective-permute-start | bytes 1769480 | tf_op jit(solution)/shard_map/ppermute | solution.py:556
  27.8 0.1 pad_add_fusion.place_ref
  27.8 0.0 copy-start.1
  27.8 2.6 %shard_map.73 = (f32[128,128]{1,0:T(8,128)S(1)}, f32[16,128]{1,0:T(8,128)S(1)}, bf16[3328,128]{1,0:T(8,128)(2,1)S(1)}, f32[1152,128]{1,0:T(8,128)S(1)}, f32[16,1...) custom-call(s32[4]{0:T(128)S(1)} %pad_add_fusion.place_ref, ...), custom_call_target="tpu_custom_call" | custom-call | flops 1000000000 | bytes 1000000 | tf_op jit(solution)/shard_map/pallas_call | solution.py:526
  30.5 0.0 collective-permute-done
  30.5 5.2 %shard_map.74 = (f32[32,16,128]{2,1,0:T(8,128)S(1)}, f32[128,128]{1,0:T(8,128)S(1)}, f32[256,2048]{1,0:T(8,128)S(1)}, f32[128,128]{1,0:T(8,128)S(1)}, f32[16,128...) custom-call(s32[4]{0:T(128)S(1)} %pad_add_fusion.place_ref, f32[1152,128]{1,0:T(8,128)S(1)} %bitcast.19, ...), custom_call_target="tpu_custom_call" | custom-call | flops 1000000000 | bytes 1000000 | tf_op jit(solution)/shard_map/pallas_call | solution.py:526
  35.7 12.0 %all_to_all.16.recv_ref = f32[32,16,128]{2,1,0:T(8,128)S(1)} all-to-all(f32[32,16,128]{2,1,0:T(8,128)S(1)} %get-tuple-element.38), channel_id=1, replica_groups=mesh['x'=4,'c'=2,'z'=4,'y'=4] {'x','c','y'}, dimensions={0} | all-to-all | bytes 524288 | tf_op jit(solution)/shard_map/all_to_all | solution.py:560
  47.7 0.0 copy-done.1
  47.7 0.0 copy-start.2
  47.7 0.0 copy-start.3
  47.7 7.8 %shard_map.75 = (f32[32,16,128]{2,1,0:T(8,128)}, bf16[768,128]{1,0:T(8,128)(2,1)S(1)}) custom-call(s32[4]{0:T(128)S(1)} %pad_add_fusion.place_ref, f32[16,128]{1,0:T(8,128)S(1)} %get-tuple-element.29.ids_ref.own_ids_ref, f32[32,16,128]{2,1,0:T(8,128)S(1)} %all_to_all.16.recv_ref, f32[256,2048]{1,0:T(8,128)S(1)} %get-tuple-element.39.level_ref, ...), custom_call_target="tpu_custom_call" | custom-call | flops 1000000000 | bytes 1000000 | tf_op jit(solution)/shard_map/pallas_call | solution.py:526
  55.5 4.1 %all-to-all-start.2 = ((f32[32,16,128]{2,1,0:T(8,128)}), f32[32,16,128]{2,1,0:T(8,128)S(1)}, u32[]{:S(2)}, u32[]{:S(2)}) async-start(f32[32,16,128]{2,1,0:T(8,128)} %get-tuple-element.46), calls=%async_computation.2 | async-start | bytes 524288 | tf_op jit(solution)/shard_map/all_to_all | solution.py:560
  59.6 0.0 copy-done.2
  59.6 0.0 copy-done.3
  59.7 3.9 %shard_map.76 = (f32[256,128]{1,0:T(8,128)S(1)}, bf16[256,128]{1,0:T(8,128)(2,1)}, bf16[1024,512]{1,0:T(8,128)(2,1)S(1)}, bf16[320,512]{1,0:T(8,128)(2,1)S(1)}, f32[320,128]{1,0:T(8,128)S(1)}) custom-call(s32[4]{0:T(128)S(1)} %pad_add_fusion.place_ref, s32[1,128]{1,0:T(1,128)S(1)} %bitcast.24, s32[4,128]{1,0:T(4,128)S(1)} %bitcast.22, ...), custom_call_target="tpu_custom_call" | custom-call | flops 1000000000 | bytes 1000000 | tf_op jit(solution)/shard_map/pallas_call | solution.py:526
  63.5 5.0 %all-to-all-done.2.recv_ref = f32[32,16,128]{2,1,0:T(8,128)S(1)} async-done(((f32[32,16,128]{2,1,0:T(8,128)}), f32[32,16,128]{2,1,0:T(8,128)S(1)}, u32[]{:S(2)}, u32[]{:S(2)}) %all-to-all-start.2) | async-done | bytes 262176 | tf_op jit(solution)/shard_map/all_to_all | solution.py:560
  68.5 2.4 %shard_map.77 = f32[16,4,128]{2,1,0:T(4,128)} custom-call(s32[4]{0:T(128)S(1)} %pad_add_fusion.place_ref, f32[32,16,128]{2,1,0:T(8,128)S(1)} %all-to-all-done.2.recv_ref, f32[256,128]{1,0:T(8,128)S(1)} %get-tuple-element.49.level_ref, bf16[1024,512]{1,0:T(8,128)(2,1)S(1)} %get-tuple-element.50.groups_ref, bf16[320,512]{1,0:T(8,128)(2,1)S(1)} %get-tuple-element.51.rows_ref, ...), custom_call_target="tpu_custom_call" | custom-call | flops 1000000000 | bytes 1000000 | tf_op jit(solution)/shard_map/pallas_call | solution.py:526
  (4 shorter events, 0.1 us)
Async XLA Ops:
  0.0 0.9 %copy-start = (f32[16,256]{1,0:T(8,128)S(1)}, f32[16,256]{1,0:T(8,128)}, u32[]{:S(2)}) copy-start(f32[16,256]{1,0:T(8,128)} %param.9) | copy-start | bytes 49156
  25.2 5.2 %collective-permute-start = (f32[64,9,2,128]{3,2,1,0:T(2,128)S(1)}, f32[64,9,2,128]{3,2,1,0:T(2,128)S(1)}, u32[]{:S(2)}, u32[]{:S(2)}) collective-permute-start(f32[64,9,2,128]{3,2,1,0:T(2,128)S(1)} %all_to_all.15), channel_id=1, source_target_pairs={{0,16},{16,0},{1,17},{17,1},{2,18},{18,2},{3,19},{19,3},{4,20},{20... | collective-permute-start | bytes 1769480 | tf_op jit(solution)/shard_map/ppermute | solution.py:556
  27.8 19.9 %copy-start.1 = (bf16[768,2048]{1,0:T(8,128)(2,1)S(1)}, bf16[768,2048]{1,0:T(8,128)(2,1)}, u32[]{:S(2)}) copy-start(bf16[768,2048]{1,0:T(8,128)(2,1)} %constant.34.clone.whole_ref) | copy-start | bytes 9437188
  47.7 11.9 %copy-start.2 = (s32[128,4]{0,1:T(4,128)S(1)}, s32[128,4]{0,1:T(4,128)}, u32[]{:S(2)}) copy-start(s32[128,4]{0,1:T(4,128)} %param.8) | copy-start | bytes 6148
  47.7 11.9 %copy-start.3 = (s32[128]{0:T(128)S(1)}, s32[128]{0:T(128)}, u32[]{:S(2)}) copy-start(s32[128]{0:T(128)} %param.7) | copy-start | bytes 1540
  55.5 13.0 %all-to-all-start.2 = ((f32[32,16,128]{2,1,0:T(8,128)}), f32[32,16,128]{2,1,0:T(8,128)S(1)}, u32[]{:S(2)}, u32[]{:S(2)}) async-start(f32[32,16,128]{2,1,0:T(8,128)} %get-tuple-element.46), calls=%async_computation.2 | async-start | bytes 524288 | tf_op jit(solution)/shard_map/all_to_all | solution.py:560

commit v6 on v5

--- a/solution.py
+++ b/solution.py
@@ -45,6 +45,9 @@
 
     cell = np.concatenate([np.exp(400.0 * ya[:, None] * (da + s)[None]) for s in shifts], axis=1)
     high, low = _halves(np.concatenate([cell.T, cell.T], axis=1))
+    one = np.exp(400.0 * ya[:, None] * da[None])
+    turned = _halves(np.concatenate([one.T, one.T], axis=1))
+    turned = (turned[0],) + turned + (np.zeros_like(turned[0]),)
     order = np.zeros((8, 4, 8, 8, 4, 4, 8), ml_dtypes.bfloat16)
     for i, k, r in np.ndindex(8, 4, 8):
         order[i, k, i, r, :, k, r] = 1
@@ -54,6 +57,8 @@
         _thrice(along(0.0)),
         _thrice(along(0.0).T),
         order.reshape(2048, 128),
+        _thrice(np.tile(one, (2, 16))),
+        np.concatenate([np.concatenate([m, np.zeros((24, 128), m.dtype)], axis=0) for m in turned], axis=0),
     ]
     high, low = _halves(whole(0.0))
     wholes = _halves(np.concatenate([whole(s) for s in shifts], axis=0)) + (high, high, low, np.zeros_like(low))
@@ -64,7 +69,7 @@
     return np.concatenate(factors, axis=0), np.concatenate(wholes, axis=0), ups.astype(np.float32)
 
 
-CELL, BACK, BASIC, BASIC_BACK, ORDER = 0, 384, 512, 896, 1280
+CELL, BACK, BASIC, BASIC_BACK, ORDER, ONE, ONE_BACK = 0, 384, 512, 896, 1280, 3328, 3712
 
 
 def dot(a, b):
@@ -179,21 +184,21 @@
     return parts[0]
 
 
-def cell_sums(u, factor_ref, up_ref):
+def cell_sums(u, factor_ref, up_ref, first=CELL):
     v = [None] * 8
     for t in range(16):
         part = u[:, 128 * t : 128 * t + 128]
         for i in range(8):
             term = part * up_of(up_ref, 8 * t + i)
             v[i] = term if t == 0 else v[i] + term
-    return dot(thrice(jnp.concatenate(v, axis=0)), factor_ref[CELL : CELL + 384, :])
-
-
-def cell_back(e, factor_ref, up_ref):
+    return dot(thrice(jnp.concatenate(v, axis=0)), factor_ref[first : first + 384, :])
+
+
+def cell_back(e, factor_ref, up_ref, first=BACK):
     high = e.astype(BF16).astype(F32)
     lane = lax.broadcasted_iota(jnp.int32, e.shape, 1)
     x = jnp.where(lax.shift_right_logical(lane, 5) == 1, e - high, high).astype(BF16)
-    z = dot(x, factor_ref[BACK : BACK + 128, :])
+    z = dot(x, factor_ref[first : first + 128, :])
     z = [z[16 * i : 16 * i + 16] for i in range(8)]
     return jnp.concatenate(
         [total([z[i] * up_of(up_ref, 8 * t + i) for i in range(8)]) for t in range(16)], axis=1)
@@ -269,31 +274,33 @@
     return peak + jnp.log(over_k(jnp.exp(q - twice(peak)) * d, jnp.add))
 
 
-def sweep_b(log_b, mass, r, part, factor_ref, up_ref, beside):
+def sweep_b(log_b, masses, r, part, factor_ref, up_ref, beside):
     for i in range(3):
         beside(5 + i)
         v = r + twice(log_b - part)
         top = jnp.max(v, axis=1, keepdims=True)
-        e = mass / sums(jnp.exp(v - top), factor_ref, up_ref)
+        t = jnp.exp(v - top)
         if i < 2:
-            part = column_part(r, top, cols(e, factor_ref, up_ref))
+            e = masses[0] / cell_sums(t, factor_ref, up_ref, ONE)
+            part = column_part(r, top, cell_back(e, factor_ref, up_ref, ONE_BACK))
+    e = masses[1] / sums(t, factor_ref, up_ref)
     return e, top
 
 
-def solve_pair(log_b_a, mass_a, mass_b, ids, d, part, factor_ref, up_ref, send_ref, beside=lambda i: None):
+def solve_pair(log_b_a, mass_a, masses_b, ids, d, part, factor_ref, up_ref, send_ref, beside=lambda i: None):
     y = targets(0, W)
     at_cell = cell_centre(jnp.floor(ids / 4.0))
     at_basic = basic_centre(ids)
     shift = (400.0 * (at_basic[1] - at_cell[1])) * y[1]
     u, centre, d_a = sweep_a(log_b_a, mass_a, d, factor_ref, up_ref, beside)
-    e_first = mass_b * (centre / sums(u * jnp.exp(shift), factor_ref, up_ref))
+    e_first = masses_b[1] * (centre / sums(u * jnp.exp(shift), factor_ref, up_ref))
     beside(3)
     d_first = cols(e_first, factor_ref, up_ref)
     v = log_b_a - jnp.log(d_a) + shift
     peak = over_k(v, jnp.maximum)
     beside(4)
     log_b_b = peak + jnp.log(over_k(jnp.exp(v - twice(peak)) * d_first, jnp.add))
-    e_second, top = sweep_b(log_b_b, mass_b, tilt(at_basic, y), part, factor_ref, up_ref, beside)
+    e_second, top = sweep_b(log_b_b, masses_b, tilt(at_basic, y), part, factor_ref, up_ref, beside)
     rows = jnp.where(low_half((16, 128)), e_first, jnp.log(e_second) - top)
     for i in range(32):
         send_ref[i, :, :] = rows
@@ -357,7 +364,9 @@
 
 
 def first_kernel(place_ref, own_ref, other_ref, sum_a_ref, sum_b_ref, ids_ref, onehot_ref, cell_ref, cells_ref, near_ref,
-                 factor_ref, up_ref, send_ref, here_ref, level_ref, mass_a_ref, mass_b_ref, d_ref, part_ref, table_ref):
+                 factor_ref, up_ref, whole_hbm, send_ref, here_ref, level_ref, mass_a_ref, mass_b_ref, mass_one_ref, d_ref, part_ref, whole_ref, table_ref, sems):
+    copy = pltpu.make_async_copy(whole_hbm, whole_ref, sems.at[0])
+    copy.start()
     ids, onehot = ids_ref[:, :1], onehot_ref[...]
     mass = []
     for part in (16, 17):
@@ -366,7 +375,12 @@
         mass.append(pick(onehot, rows))
     mass = jnp.concatenate(mass, axis=1)
     mass_a = ordered(mass, factor_ref)
-    mass_b = segment(quadrupled(mass), ids - 4.0 * jnp.floor(ids / 4.0))
+    k = ids - 4.0 * jnp.floor(ids / 4.0)
+    mass_b = segment(quadrupled(mass), k)
+    lane_k = lax.bitwise_and(lax.shift_right_logical(lax.broadcasted_iota(jnp.int32, (128, 128), 1), 3), 3).astype(F32)
+    mass_one = jnp.where(lane_k == jnp.concatenate([k] * 8, axis=0), mass_a, 0.0)
+    mass_one = mass_one + pltpu.roll(mass_one, 8, 1)
+    mass_one = mass_one + pltpu.roll(mass_one, 16, 1)
     d = cell_back(balanced(mass_a, sum_a_ref[...]), factor_ref, up_ref)
     log_b = []
     for t in range(16):
@@ -382,6 +396,7 @@
     part = column_part(tilt(at_basic, targets(0, W)), top, cols(mass_b / sum_b_ref[...], factor_ref, up_ref))
     mass_a_ref[...] = mass_a
     mass_b_ref[...] = mass_b
+    mass_one_ref[...] = mass_one
     d_ref[...] = d
     part_ref[...] = part
     near, cell_col = near_ref[0:256, :1], cell_ref[:, :1]
@@ -390,7 +405,8 @@
         at = slice(256 * block, 256 * block + 256)
         level_ref[:, at] = near_level(near, cells_ref[...], table_ref[:, at], cell_col, targets(256 * block, 256))
 
-    solve_pair(log_b, mass_a, mass_b, ids, d, part, factor_ref, up_ref, send_ref, level)
+    solve_pair(log_b, mass_a, (mass_one, mass_b), ids, d, part, factor_ref, up_ref, send_ref, level)
+    copy.wait()
 
 
 def received(recv_ref):
@@ -456,7 +472,7 @@
     return gamma + q[256:], d1[256:]
 
 
-def second_kernel(place_ref, own_ids_ref, recv_ref, level_ref, groups_ref, rows_ref, ids_ref, mass_a_ref, mass_b_ref, d_ref,
+def second_kernel(place_ref, own_ids_ref, recv_ref, level_ref, groups_ref, rows_ref, ids_ref, mass_a_ref, mass_b_ref, mass_one_ref, d_ref,
                   part_ref, factor_ref, up_ref, whole_ref, send_ref, here_ref):
     here_ref[...] = whole_ref[:, pl.ds(pl.multiple_of(place_ref[2] * 128, 128), 128)]
     gather = gathered(recv_ref, groups_ref, rows_ref)
@@ -466,7 +482,7 @@
         at = slice(block * 256, block * 256 + 256)
         v, d = near_margins(gather, level_ref[:, at], centre, targets(256 * block, 256), whole_ref[:, at])
         log_b.append(mix([v[16 * k : 16 * k + 16] for k in range(4)], [d[16 * k : 16 * k + 16] for k in range(4)]))
-    solve_pair(jnp.concatenate(log_b, axis=1), mass_a_ref[...], mass_b_ref[...], own_ids_ref[:, :1], d_ref[...], part_ref[...],
+    solve_pair(jnp.concatenate(log_b, axis=1), mass_a_ref[...], (mass_one_ref[...], mass_b_ref[...]), own_ids_ref[:, :1], d_ref[...], part_ref[...],
                factor_ref, up_ref, send_ref)
 
 
@@ -534,7 +550,7 @@
     )(*inputs)
 
 
-FACTORS = [(3328, 128, BF16), (1152, 128)]
+FACTORS = [(3840, 128, BF16), (1152, 128)]
 NEAR = [(256, 128, BF16), (1024, 512, BF16), (320, 512, BF16), (320, 128)]
 
 
@@ -559,9 +575,10 @@
     def exchange(rows):
         return lax.all_to_all(rows, ("x", "c", "y"), 0, 0, tiled=True)
 
-    send, here, level, *rest = call(
-        first_kernel, (place, own, other, sum_a, sum_b, held, onehot, cell, cells, ids, factors, ups),
-        [(32, 16, 128), (128, 128), (256, W), (128, 128), (16, 128), (16, W), (8, W)], [pltpu.VMEM((128, W), F32)])
+    send, here, level, *rest, wholes = call(
+        first_kernel, (place, own, other, sum_a, sum_b, held, onehot, cell, cells, ids, factors, ups, wholes),
+        [(32, 16, 128), (128, 128), (256, W), (128, 128), (16, 128), (128, 128), (16, W), (8, W), (768, W, BF16)],
+        [pltpu.VMEM((128, W), F32), pltpu.SemaphoreType.DMA((1,))], far=1)
     first = exchange(send)
     send, whole = call(second_kernel, (place, held, first, level, groups, rows, ids, *rest, factors, ups, wholes),
                        [(32, 16, 128), (768, 128, BF16)])

time: 71.3 us -> 70.7 us (level)
  no operation moved by 1% of the time
where the time goes in v6:
time: 70.7 us; the launch traced here: 70.4 us
  blocking collectives  36.1 us (51%)
  Pallas kernels  21.3 us (30%)
  starting transfers between devices  6.66 us (9%)
  waiting for transfers between devices  5.01 us (7%)
  local copies, waits for them, and re-layouts  1.13 us (2%)
    all_to_all x1, blocking collectives, on_device(): lax.all_to_all(jnp.broadcast_to(block[None], (64, 9, 2, 128)), ('x', 'z',...  24 us
    pallas_call x5, Pallas kernels, call(): pl.pallas_call(body, out_shape=[jax.ShapeDtypeStruct(s[:-1], BF16) if s[-...  21.3 us
    all_to_all x1, blocking collectives, exchange(): return lax.all_to_all(rows, ('x', 'c', 'y'), 0, 0, tiled=True)  12 us
    all_to_all x1, waiting for transfers between devices, exchange(): return lax.all_to_all(rows, ('x', 'c', 'y'), 0, 0, tiled=True)  5 us
    all_to_all x1, starting transfers between devices, exchange(): return lax.all_to_all(rows, ('x', 'c', 'y'), 0, 0, tiled=True)  4.13 us
    ppermute x1, starting transfers between devices, on_device(): other = lax.ppermute(own, 'c', [(0, 1), (1, 0)]).reshape(1152, 128)  2.54 us
  transfers between devices with their start and end apart: 2, of which 1 were waited for; matrix products, arithmetic and copies ran while one was open for 0% of the time, Pallas kernels for 9%

profile of v6, /device:TPU:1, one launch (start us, length us, event | category | flops | bytes accessed | tf_op | source)
XLA Modules:
  0.0 70.4 jit_solution(6915732175534736344)
XLA Ops:
  0.0 0.0 copy-start
  0.0 0.9 %fusion.3 = (f32[16,1,128]{2,1,0:T(1,128)S(1)}, f32[16,1,128]{2,1,0:T(1,128)S(1)}, f32[16,1,128]{2,1,0:T(1,128)S(1)}, f32[16,1,128]{2,1,0:T(1,128)S(1)}) fusion(f32[16,4,128]{2,1,0:T(4,128)} %param.10), kind=kLoop, calls=%fused_computation.9 | loop fusion | bytes 65536 | tf_op jit(solution)/shard_map/slice | solution.py:562
  0.9 0.0 copy-done
  1.0 0.2 broadcast_in_dim.8
  1.2 24.0 %all_to_all.15 = f32[64,9,2,128]{3,2,1,0:T(2,128)S(1)} all-to-all(f32[64,9,2,128]{3,2,1,0:T(2,128)S(1)} %broadcast_in_dim.8), channel_id=1, replica_groups=mesh['x'=4,'c'=2,'z'=4,'y'=4] {'x','z','y'}, dimensions={0} | all-to-all | bytes 1179648 | tf_op jit(solution)/shard_map/all_to_all | solution.py:568
  25.2 2.5 %collective-permute-start = (f32[64,9,2,128]{3,2,1,0:T(2,128)S(1)}, f32[64,9,2,128]{3,2,1,0:T(2,128)S(1)}, u32[]{:S(2)}, u32[]{:S(2)}) collective-permute-start(f32[64,9,2,128]{3,2,1,0:T(2,128)S(1)} %all_to_all.15), channel_id=1, source_target_pairs={{0,16},{16,0},{1,17},{17,1},{2,18},{18,2},{3,19},{19,3},{4,20},{20... | collective-permute-start | bytes 1769480 | tf_op jit(solution)/shard_map/ppermute | solution.py:572
  27.8 0.1 pad_add_fusion.place_ref
  27.8 2.4 %shard_map.73 = (f32[128,128]{1,0:T(8,128)S(1)}, f32[16,128]{1,0:T(8,128)S(1)}, bf16[3840,128]{1,0:T(8,128)(2,1)S(1)}, f32[1152,128]{1,0:T(8,128)S(1)}, f32[16,1...) custom-call(s32[4]{0:T(128)S(1)} %pad_add_fusion.place_ref, ...), custom_call_target="tpu_custom_call" | custom-call | flops 1000000000 | bytes 1000000 | tf_op jit(solution)/shard_map/pallas_call | solution.py:542
  30.2 0.0 collective-permute-done
  30.3 5.1 %shard_map.74 = (f32[32,16,128]{2,1,0:T(8,128)S(1)}, f32[128,128]{1,0:T(8,128)S(1)}, f32[256,2048]{1,0:T(8,128)S(1)}, f32[128,128]{1,0:T(8,128)S(1)}, f32[16,128...) custom-call(s32[4]{0:T(128)S(1)} %pad_add_fusion.place_ref, ...), custom_call_target="tpu_custom_call" | custom-call | flops 1000000000 | bytes 1000000 | tf_op jit(solution)/shard_map/pallas_call | solution.py:542
  35.3 12.0 %all_to_all.16.recv_ref = f32[32,16,128]{2,1,0:T(8,128)S(1)} all-to-all(f32[32,16,128]{2,1,0:T(8,128)S(1)} %get-tuple-element.40), channel_id=1, replica_groups=mesh['x'=4,'c'=2,'z'=4,'y'=4] {'x','c','y'}, dimensions={0} | all-to-all | bytes 524288 | tf_op jit(solution)/shard_map/all_to_all | solution.py:576
  47.4 0.0 copy-start.1
  47.4 0.0 copy-start.2
  47.4 7.6 %shard_map.75 = (f32[32,16,128]{2,1,0:T(8,128)}, bf16[768,128]{1,0:T(8,128)(2,1)S(1)}) custom-call(s32[4]{0:T(128)S(1)} %pad_add_fusion.place_ref, f32[16,128]{1,0:T(8,128)S(1)} %get-tuple-element.31.ids_ref.own_ids_ref, f32[32,16,128]{2,1,0:T(8,128)S(1)} %all_to_all.16.recv_ref, f32[256,2048]{1,0:T(8,128)S(1)} %get-tuple-element.41.level_ref, ...), custom_call_target="tpu_custom_call" | custom-call | flops 1000000000 | bytes 1000000 | tf_op jit(solution)/shard_map/pallas_call | solution.py:542
  55.0 4.1 %all-to-all-start.2 = ((f32[32,16,128]{2,1,0:T(8,128)}), f32[32,16,128]{2,1,0:T(8,128)S(1)}, u32[]{:S(2)}, u32[]{:S(2)}) async-start(f32[32,16,128]{2,1,0:T(8,128)} %get-tuple-element.50), calls=%async_computation.2 | async-start | bytes 524288 | tf_op jit(solution)/shard_map/all_to_all | solution.py:576
  59.1 0.0 copy-done.1
  59.1 0.0 copy-done.2
  59.1 3.9 %shard_map.76 = (f32[256,128]{1,0:T(8,128)S(1)}, bf16[256,128]{1,0:T(8,128)(2,1)}, bf16[1024,512]{1,0:T(8,128)(2,1)S(1)}, bf16[320,512]{1,0:T(8,128)(2,1)S(1)}, f32[320,128]{1,0:T(8,128)S(1)}) custom-call(s32[4]{0:T(128)S(1)} %pad_add_fusion.place_ref, s32[1,128]{1,0:T(1,128)S(1)} %bitcast.24, s32[4,128]{1,0:T(4,128)S(1)} %bitcast.22, ...), custom_call_target="tpu_custom_call" | custom-call | flops 1000000000 | bytes 1000000 | tf_op jit(solution)/shard_map/pallas_call | solution.py:542
  63.0 5.0 %all-to-all-done.2.recv_ref = f32[32,16,128]{2,1,0:T(8,128)S(1)} async-done(((f32[32,16,128]{2,1,0:T(8,128)}), f32[32,16,128]{2,1,0:T(8,128)S(1)}, u32[]{:S(2)}, u32[]{:S(2)}) %all-to-all-start.2) | async-done | bytes 262176 | tf_op jit(solution)/shard_map/all_to_all | solution.py:576
  68.0 2.4 %shard_map.77 = f32[16,4,128]{2,1,0:T(4,128)} custom-call(s32[4]{0:T(128)S(1)} %pad_add_fusion.place_ref, f32[32,16,128]{2,1,0:T(8,128)S(1)} %all-to-all-done.2.recv_ref, f32[256,128]{1,0:T(8,128)S(1)} %get-tuple-element.53.level_ref, bf16[1024,512]{1,0:T(8,128)(2,1)S(1)} %get-tuple-element.54.groups_ref, bf16[320,512]{1,0:T(8,128)(2,1)S(1)} %get-tuple-element.55.rows_ref, ...), custom_call_target="tpu_custom_call" | custom-call | flops 1000000000 | bytes 1000000 | tf_op jit(solution)/shard_map/pallas_call | solution.py:542
  (4 shorter events, 0.1 us)
Async XLA Ops:
  0.0 0.9 %copy-start = (f32[16,256]{1,0:T(8,128)S(1)}, f32[16,256]{1,0:T(8,128)}, u32[]{:S(2)}) copy-start(f32[16,256]{1,0:T(8,128)} %param.9) | copy-start | bytes 49156
  25.2 5.0 %collective-permute-start = (f32[64,9,2,128]{3,2,1,0:T(2,128)S(1)}, f32[64,9,2,128]{3,2,1,0:T(2,128)S(1)}, u32[]{:S(2)}, u32[]{:S(2)}) collective-permute-start(f32[64,9,2,128]{3,2,1,0:T(2,128)S(1)} %all_to_all.15), channel_id=1, source_target_pairs={{0,16},{16,0},{1,17},{17,1},{2,18},{18,2},{3,19},{19,3},{4,20},{20... | collective-permute-start | bytes 1769480 | tf_op jit(solution)/shard_map/ppermute | solution.py:572
  47.4 11.7 %copy-start.1 = (s32[128,4]{0,1:T(4,128)S(1)}, s32[128,4]{0,1:T(4,128)}, u32[]{:S(2)}) copy-start(s32[128,4]{0,1:T(4,128)} %param.8) | copy-start | bytes 6148
  47.4 11.7 %copy-start.2 = (s32[128]{0:T(128)S(1)}, s32[128]{0:T(128)}, u32[]{:S(2)}) copy-start(s32[128]{0:T(128)} %param.7) | copy-start | bytes 1540
  55.0 13.0 %all-to-all-start.2 = ((f32[32,16,128]{2,1,0:T(8,128)}), f32[32,16,128]{2,1,0:T(8,128)S(1)}, u32[]{:S(2)}, u32[]{:S(2)}) async-start(f32[32,16,128]{2,1,0:T(8,128)} %get-tuple-element.50), calls=%async_computation.2 | async-start | bytes 524288 | tf_op jit(solution)/shard_map/all_to_all | solution.py:576

commit v7 on v6

--- a/solution.py
+++ b/solution.py
@@ -36,12 +36,6 @@
         up = np.exp(400.0 * dh[:, None] * yh[None])
         along = np.exp(400.0 * (da + shift)[:, None] * ya[None])
         return (up[:, None, :, None] * along[None, :, None, :]).reshape(64, W)
-
-    def along(shift):
-        part = np.zeros((2, 64, 2, 8, 8))
-        for h in range(2):
-            part[h, :, h] = np.exp(400.0 * ya[:, None] * (da + shift)[None])[:, None, :]
-        return part.reshape(128, 128)
 
     cell = np.concatenate([np.exp(400.0 * ya[:, None] * (da + s)[None]) for s in shifts], axis=1)
     high, low = _halves(np.concatenate([cell.T, cell.T], axis=1))
@@ -54,8 +48,6 @@
     factors = [
         _thrice(np.tile(cell, (2, 4))),
         np.concatenate([high, high, low, np.zeros_like(low)], axis=0),
-        _thrice(along(0.0)),
-        _thrice(along(0.0).T),
         order.reshape(2048, 128),
         _thrice(np.tile(one, (2, 16))),
         np.concatenate([np.concatenate([m, np.zeros((24, 128), m.dtype)], axis=0) for m in turned], axis=0),
@@ -64,12 +56,11 @@
     wholes = _halves(np.concatenate([whole(s) for s in shifts], axis=0)) + (high, high, low, np.zeros_like(low))
     up = np.exp(400.0 * yh.reshape(16, 2, 1) * dh[None, None])
     of_row = np.repeat(up.transpose(0, 2, 1).reshape(128, 1, 2), 64, axis=2)
-    of_pixel = np.repeat(up.reshape(16, 1, 16), 8, axis=2)
-    ups = np.repeat(np.concatenate([of_row, of_pixel], axis=0), 8, axis=1).reshape(1152, 128)
+    ups = np.repeat(of_row, 8, axis=1).reshape(1024, 128)
     return np.concatenate(factors, axis=0), np.concatenate(wholes, axis=0), ups.astype(np.float32)
 
 
-CELL, BACK, BASIC, BASIC_BACK, ORDER, ONE, ONE_BACK = 0, 384, 512, 896, 1280, 3328, 3712
+CELL, BACK, ORDER, ONE, ONE_BACK = 0, 384, 512, 2560, 2944
 
 
 def dot(a, b):
@@ -158,16 +149,6 @@
     return jnp.where(mask, swap(x), x) if upper else jnp.where(mask, x, swap(x))
 
 
-def segment(x, k):
-    y = jnp.where(k >= 2.0, x[:, 256:], x[:, :256])
-    return jnp.where((k == 1.0) | (k == 3.0), y[:, 128:], y[:, :128])
-
-
-def quadrupled(x):
-    return jnp.concatenate([doubled(x[:, :128], False), doubled(x[:, :128], True),
-                            doubled(x[:, 128:], False), doubled(x[:, 128:], True)], axis=1)
-
-
 def thrice(x):
     high, low = split2(x)
     return jnp.concatenate([high, low, high], axis=1)
@@ -213,17 +194,12 @@
     return jnp.concatenate(out, axis=0)
 
 
-def sums(u, factor_ref, up_ref):
-    x = thrice(jnp.concatenate([u[:, 128 * t : 128 * t + 128] for t in range(16)], axis=0))
-    p = dot(x, factor_ref[BASIC : BASIC + 384, :])
-    s = total([p[16 * t : 16 * t + 16] * up_of(up_ref, 128 + t) for t in range(16)])
-    return s + swap(s)
-
-
-def cols(e, factor_ref, up_ref):
-    x = jnp.concatenate([e * up_of(up_ref, 128 + t) for t in range(16)], axis=0)
-    d = dot(thrice(x), factor_ref[BASIC_BACK : BASIC_BACK + 384, :])
-    return jnp.concatenate([d[16 * t : 16 * t + 16] for t in range(16)], axis=1)
+def spread(e):
+    row = lax.bitwise_and(lax.shift_right_logical(lax.broadcasted_iota(jnp.int32, (16, 128), 1), 3), 7)
+    out = e[:16]
+    for i in range(1, 8):
+        out = jnp.where(row == i, e[16 * i : 16 * i + 16], out)
+    return out
 
 
 def wide(e):
@@ -274,34 +250,33 @@
     return peak + jnp.log(over_k(jnp.exp(q - twice(peak)) * d, jnp.add))
 
 
-def sweep_b(log_b, masses, r, part, factor_ref, up_ref, beside):
+def sweep_b(log_b, mass, r, part, factor_ref, up_ref, beside):
     for i in range(3):
         beside(5 + i)
         v = r + twice(log_b - part)
         top = jnp.max(v, axis=1, keepdims=True)
-        t = jnp.exp(v - top)
+        e = mass / cell_sums(jnp.exp(v - top), factor_ref, up_ref, ONE)
         if i < 2:
-            e = masses[0] / cell_sums(t, factor_ref, up_ref, ONE)
             part = column_part(r, top, cell_back(e, factor_ref, up_ref, ONE_BACK))
-    e = masses[1] / sums(t, factor_ref, up_ref)
     return e, top
 
 
-def solve_pair(log_b_a, mass_a, masses_b, ids, d, part, factor_ref, up_ref, send_ref, beside=lambda i: None):
+def solve_pair(log_b_a, mass_a, mass_b, ids, d, part, factor_ref, up_ref, send_ref, beside=lambda i: None):
     y = targets(0, W)
     at_cell = cell_centre(jnp.floor(ids / 4.0))
     at_basic = basic_centre(ids)
     shift = (400.0 * (at_basic[1] - at_cell[1])) * y[1]
     u, centre, d_a = sweep_a(log_b_a, mass_a, d, factor_ref, up_ref, beside)
-    e_first = masses_b[1] * (centre / sums(u * jnp.exp(shift), factor_ref, up_ref))
+    s = cell_sums(u * jnp.exp(shift), factor_ref, up_ref, ONE)
+    e_first = mass_b * (jnp.concatenate([centre] * 8, axis=0) / s)
     beside(3)
-    d_first = cols(e_first, factor_ref, up_ref)
+    d_first = cell_back(e_first, factor_ref, up_ref, ONE_BACK)
     v = log_b_a - jnp.log(d_a) + shift
     peak = over_k(v, jnp.maximum)
     beside(4)
     log_b_b = peak + jnp.log(over_k(jnp.exp(v - twice(peak)) * d_first, jnp.add))
-    e_second, top = sweep_b(log_b_b, masses_b, tilt(at_basic, y), part, factor_ref, up_ref, beside)
-    rows = jnp.where(low_half((16, 128)), e_first, jnp.log(e_second) - top)
+    e_second, top = sweep_b(log_b_b, mass_b, tilt(at_basic, y), part, factor_ref, up_ref, beside)
+    rows = jnp.where(low_half((16, 128)), spread(e_first), jnp.log(spread(e_second)) - top)
     for i in range(32):
         send_ref[i, :, :] = rows
 
@@ -341,7 +316,8 @@
 
 def start_kernel(place_ref, placement_hbm, members_hbm, factor_hbm, up_hbm, sum_a_ref, sum_b_ref, factor_ref, up_ref, own_ids_ref, onehot_ref,
                  cell_ref, cells_ref, groups_ref, rows_ref, ids_ref, placement_ref, members_ref, sems):
-    pairs = ((placement_hbm, placement_ref), (members_hbm, members_ref), (factor_hbm, factor_ref), (up_hbm, up_ref))
+    pairs = [(placement_hbm, placement_ref), (members_hbm, members_ref), (up_hbm, up_ref)]
+    pairs += [(factor_hbm.at[at, :], factor_ref.at[at, :]) for at in (pl.ds(0, ORDER), pl.ds(ONE, 512), pl.ds(ORDER, ONE - ORDER))]
     copies = [pltpu.make_async_copy(*pair, sems.at[i]) for i, pair in enumerate(pairs)]
     for copy in copies:
         copy.start()
@@ -356,15 +332,16 @@
     cell_ref[...] = jnp.broadcast_to(cell_col, (128, 128))
     want = jnp.concatenate([4.0 * cells + float(k) for k in range(4)], axis=0)
     near_cells(want, member_rows, cell_row, exchange_ids(member_rows), cells_ref, groups_ref, rows_ref, ids_ref)
-    for copy in copies[2:]:
+    for copy in copies[2:5]:
         copy.wait()
     y = targets(0, W)
     sum_a_ref[...] = cell_sums(nearness(cell_centre(jnp.floor(ids / 4.0)), y), factor_ref, up_ref)
-    sum_b_ref[...] = sums(nearness(basic_centre(ids), y), factor_ref, up_ref)
+    sum_b_ref[...] = cell_sums(nearness(basic_centre(ids), y), factor_ref, up_ref, ONE)
+    copies[5].wait()
 
 
 def first_kernel(place_ref, own_ref, other_ref, sum_a_ref, sum_b_ref, ids_ref, onehot_ref, cell_ref, cells_ref, near_ref,
-                 factor_ref, up_ref, whole_hbm, send_ref, here_ref, level_ref, mass_a_ref, mass_b_ref, mass_one_ref, d_ref, part_ref, whole_ref, table_ref, sems):
+                 factor_ref, up_ref, whole_hbm, send_ref, here_ref, level_ref, mass_a_ref, mass_b_ref, d_ref, part_ref, whole_ref, table_ref, sems):
     copy = pltpu.make_async_copy(whole_hbm, whole_ref, sems.at[0])
     copy.start()
     ids, onehot = ids_ref[:, :1], onehot_ref[...]
@@ -376,11 +353,10 @@
     mass = jnp.concatenate(mass, axis=1)
     mass_a = ordered(mass, factor_ref)
     k = ids - 4.0 * jnp.floor(ids / 4.0)
-    mass_b = segment(quadrupled(mass), k)
     lane_k = lax.bitwise_and(lax.shift_right_logical(lax.broadcasted_iota(jnp.int32, (128, 128), 1), 3), 3).astype(F32)
-    mass_one = jnp.where(lane_k == jnp.concatenate([k] * 8, axis=0), mass_a, 0.0)
-    mass_one = mass_one + pltpu.roll(mass_one, 8, 1)
-    mass_one = mass_one + pltpu.roll(mass_one, 16, 1)
+    mass_b = jnp.where(lane_k == jnp.concatenate([k] * 8, axis=0), mass_a, 0.0)
+    mass_b = mass_b + pltpu.roll(mass_b, 8, 1)
+    mass_b = mass_b + pltpu.roll(mass_b, 16, 1)
     d = cell_back(balanced(mass_a, sum_a_ref[...]), factor_ref, up_ref)
     log_b = []
     for t in range(16):
@@ -393,10 +369,9 @@
     log_b = jnp.concatenate(log_b, axis=1)
     at_basic = basic_centre(ids)
     top = 200.0 * (at_basic[0] * at_basic[0] + at_basic[1] * at_basic[1])
-    part = column_part(tilt(at_basic, targets(0, W)), top, cols(mass_b / sum_b_ref[...], factor_ref, up_ref))
+    part = column_part(tilt(at_basic, targets(0, W)), top, cell_back(mass_b / sum_b_ref[...], factor_ref, up_ref, ONE_BACK))
     mass_a_ref[...] = mass_a
     mass_b_ref[...] = mass_b
-    mass_one_ref[...] = mass_one
     d_ref[...] = d
     part_ref[...] = part
     near, cell_col = near_ref[0:256, :1], cell_ref[:, :1]
@@ -405,7 +380,7 @@
         at = slice(256 * block, 256 * block + 256)
         level_ref[:, at] = near_level(near, cells_ref[...], table_ref[:, at], cell_col, targets(256 * block, 256))
 
-    solve_pair(log_b, mass_a, (mass_one, mass_b), ids, d, part, factor_ref, up_ref, send_ref, level)
+    solve_pair(log_b, mass_a, mass_b, ids, d, part, factor_ref, up_ref, send_ref, level)
     copy.wait()
 
 
@@ -472,7 +447,7 @@
     return gamma + q[256:], d1[256:]
 
 
-def second_kernel(place_ref, own_ids_ref, recv_ref, level_ref, groups_ref, rows_ref, ids_ref, mass_a_ref, mass_b_ref, mass_one_ref, d_ref,
+def second_kernel(place_ref, own_ids_ref, recv_ref, level_ref, groups_ref, rows_ref, ids_ref, mass_a_ref, mass_b_ref, d_ref,
                   part_ref, factor_ref, up_ref, whole_ref, send_ref, here_ref):
     here_ref[...] = whole_ref[:, pl.ds(pl.multiple_of(place_ref[2] * 128, 128), 128)]
     gather = gathered(recv_ref, groups_ref, rows_ref)
@@ -482,7 +457,7 @@
         at = slice(block * 256, block * 256 + 256)
         v, d = near_margins(gather, level_ref[:, at], centre, targets(256 * block, 256), whole_ref[:, at])
         log_b.append(mix([v[16 * k : 16 * k + 16] for k in range(4)], [d[16 * k : 16 * k + 16] for k in range(4)]))
-    solve_pair(jnp.concatenate(log_b, axis=1), mass_a_ref[...], (mass_one_ref[...], mass_b_ref[...]), own_ids_ref[:, :1], d_ref[...], part_ref[...],
+    solve_pair(jnp.concatenate(log_b, axis=1), mass_a_ref[...], mass_b_ref[...], own_ids_ref[:, :1], d_ref[...], part_ref[...],
                factor_ref, up_ref, send_ref)
 
 
@@ -550,7 +525,7 @@
     )(*inputs)
 
 
-FACTORS = [(3840, 128, BF16), (1152, 128)]
+FACTORS = [(3072, 128, BF16), (1024, 128)]
 NEAR = [(256, 128, BF16), (1024, 512, BF16), (320, 512, BF16), (320, 128)]
 
 
@@ -567,8 +542,8 @@
     block = jnp.concatenate([log_b, mass], axis=0).reshape(9, 2, 128)
     own = lax.all_to_all(jnp.broadcast_to(block[None], (64, 9, 2, 128)), ("x", "z", "y"), 0, 0, tiled=True)
     sum_a, sum_b, factors, ups, held, onehot, cell, cells, groups, rows, ids = call(
-        start_kernel, index + (factors, ups), [(128, 128), (16, 128)] + FACTORS + [(16, 128), (16, 128), (128, 128)] + NEAR,
-        [pltpu.VMEM((1, 128), jnp.int32), pltpu.VMEM((4, 128), jnp.int32), pltpu.SemaphoreType.DMA((4,))], far=4)
+        start_kernel, index + (factors, ups), [(128, 128), (128, 128)] + FACTORS + [(16, 128), (16, 128), (128, 128)] + NEAR,
+        [pltpu.VMEM((1, 128), jnp.int32), pltpu.VMEM((4, 128), jnp.int32), pltpu.SemaphoreType.DMA((6,))], far=4)
     other = lax.ppermute(own, "c", [(0, 1), (1, 0)]).reshape(1152, 128)
     own = own.reshape(1152, 128)
 
@@ -577,7 +552,7 @@
 
     send, here, level, *rest, wholes = call(
         first_kernel, (place, own, other, sum_a, sum_b, held, onehot, cell, cells, ids, factors, ups, wholes),
-        [(32, 16, 128), (128, 128), (256, W), (128, 128), (16, 128), (128, 128), (16, W), (8, W), (768, W, BF16)],
+        [(32, 16, 128), (128, 128), (256, W), (128, 128), (128, 128), (16, W), (8, W), (768, W, BF16)],
         [pltpu.VMEM((128, W), F32), pltpu.SemaphoreType.DMA((1,))], far=1)
     first = exchange(send)
     send, whole = call(second_kernel, (place, held, first, level, groups, rows, ids, *rest, factors, ups, wholes),

time: 70.7 us -> 70.5 us (level)
  no operation moved by 1% of the time
where the time goes in v7:
time: 70.5 us; the launch traced here: 70.1 us
  blocking collectives  36.1 us (51%)
  Pallas kernels  21.1 us (30%)
  starting transfers between devices  6.66 us (9%)
  waiting for transfers between devices  5.01 us (7%)
  local copies, waits for them, and re-layouts  1.13 us (2%)
    all_to_all x1, blocking collectives, on_device(): lax.all_to_all(jnp.broadcast_to(block[None], (64, 9, 2, 128)), ('x', 'z',...  24 us
    pallas_call x5, Pallas kernels, call(): pl.pallas_call(body, out_shape=[jax.ShapeDtypeStruct(s[:-1], BF16) if s[-...  21.1 us
    all_to_all x1, blocking collectives, exchange(): return lax.all_to_all(rows, ('x', 'c', 'y'), 0, 0, tiled=True)  12 us
    all_to_all x1, waiting for transfers between devices, exchange(): return lax.all_to_all(rows, ('x', 'c', 'y'), 0, 0, tiled=True)  5.01 us
    all_to_all x1, starting transfers between devices, exchange(): return lax.all_to_all(rows, ('x', 'c', 'y'), 0, 0, tiled=True)  4.13 us
    ppermute x1, starting transfers between devices, on_device(): other = lax.ppermute(own, 'c', [(0, 1), (1, 0)]).reshape(1152, 128)  2.54 us
  transfers between devices with their start and end apart: 2, of which 1 were waited for; matrix products, arithmetic and copies ran while one was open for 0% of the time, Pallas kernels for 9%

profile of v7, /device:TPU:1, one launch (start us, length us, event | category | flops | bytes accessed | tf_op | source)
XLA Modules:
  0.0 70.1 jit_solution(8442663329901943645)
XLA Ops:
  0.0 0.0 copy-start
  0.0 0.9 %fusion.3 = (f32[16,1,128]{2,1,0:T(1,128)S(1)}, f32[16,1,128]{2,1,0:T(1,128)S(1)}, f32[16,1,128]{2,1,0:T(1,128)S(1)}, f32[16,1,128]{2,1,0:T(1,128)S(1)}) fusion(f32[16,4,128]{2,1,0:T(4,128)} %param.10), kind=kLoop, calls=%fused_computation.9 | loop fusion | bytes 65536 | tf_op jit(solution)/shard_map/slice | solution.py:537
  0.9 0.0 copy-done
  1.0 0.2 broadcast_in_dim.8
  1.2 24.0 %all_to_all.15 = f32[64,9,2,128]{3,2,1,0:T(2,128)S(1)} all-to-all(f32[64,9,2,128]{3,2,1,0:T(2,128)S(1)} %broadcast_in_dim.8), channel_id=1, replica_groups=mesh['x'=4,'c'=2,'z'=4,'y'=4] {'x','z','y'}, dimensions={0} | all-to-all | bytes 1179648 | tf_op jit(solution)/shard_map/all_to_all | solution.py:543
  25.2 2.5 %collective-permute-start = (f32[64,9,2,128]{3,2,1,0:T(2,128)S(1)}, f32[64,9,2,128]{3,2,1,0:T(2,128)S(1)}, u32[]{:S(2)}, u32[]{:S(2)}) collective-permute-start(f32[64,9,2,128]{3,2,1,0:T(2,128)S(1)} %all_to_all.15), channel_id=1, source_target_pairs={{0,16},{16,0},{1,17},{17,1},{2,18},{18,2},{3,19},{19,3},{4,20},{20... | collective-permute-start | bytes 1769480 | tf_op jit(solution)/shard_map/ppermute | solution.py:547
  27.8 0.1 pad_add_fusion.place_ref
  27.8 2.3 %shard_map.73 = (f32[128,128]{1,0:T(8,128)S(1)}, f32[128,128]{1,0:T(8,128)S(1)}, bf16[3072,128]{1,0:T(8,128)(2,1)S(1)}, f32[1024,128]{1,0:T(8,128)S(1)}, f32[16,...) custom-call(s32[4]{0:T(128)S(1)} %pad_add_fusion.place_ref, ...), custom_call_target="tpu_custom_call" | custom-call | flops 1000000000 | bytes 1000000 | tf_op jit(solution)/shard_map/pallas_call | solution.py:517
  30.2 0.0 collective-permute-done
  30.2 5.1 %shard_map.74 = (f32[32,16,128]{2,1,0:T(8,128)S(1)}, f32[128,128]{1,0:T(8,128)S(1)}, f32[256,2048]{1,0:T(8,128)S(1)}, f32[128,128]{1,0:T(8,128)S(1)}, f32[128,12...) custom-call(s32[4]{0:T(128)S(1)} %pad_add_fusion.place_ref, ...), custom_call_target="tpu_custom_call" | custom-call | flops 1000000000 | bytes 1000000 | tf_op jit(solution)/shard_map/pallas_call | solution.py:517
  35.3 12.0 %all_to_all.16.recv_ref = f32[32,16,128]{2,1,0:T(8,128)S(1)} all-to-all(f32[32,16,128]{2,1,0:T(8,128)S(1)} %get-tuple-element.39), channel_id=1, replica_groups=mesh['x'=4,'c'=2,'z'=4,'y'=4] {'x','c','y'}, dimensions={0} | all-to-all | bytes 524288 | tf_op jit(solution)/shard_map/all_to_all | solution.py:551
  47.3 0.0 copy-start.1
  47.3 0.0 copy-start.2
  47.3 7.4 %shard_map.75 = (f32[32,16,128]{2,1,0:T(8,128)}, bf16[768,128]{1,0:T(8,128)(2,1)S(1)}) custom-call(s32[4]{0:T(128)S(1)} %pad_add_fusion.place_ref, f32[16,128]{1,0:T(8,128)S(1)} %get-tuple-element.30.ids_ref.own_ids_ref, f32[32,16,128]{2,1,0:T(8,128)S(1)} %all_to_all.16.recv_ref, f32[256,2048]{1,0:T(8,128)S(1)} %get-tuple-element.40.level_ref, ...), custom_call_target="tpu_custom_call" | custom-call | flops 1000000000 | bytes 1000000 | tf_op jit(solution)/shard_map/pallas_call | solution.py:517
  54.7 4.1 %all-to-all-start.2 = ((f32[32,16,128]{2,1,0:T(8,128)}), f32[32,16,128]{2,1,0:T(8,128)S(1)}, u32[]{:S(2)}, u32[]{:S(2)}) async-start(f32[32,16,128]{2,1,0:T(8,128)} %get-tuple-element.48), calls=%async_computation.2 | async-start | bytes 524288 | tf_op jit(solution)/shard_map/all_to_all | solution.py:551
  58.8 0.0 copy-done.1
  58.8 0.0 copy-done.2
  58.9 3.9 %shard_map.76 = (f32[256,128]{1,0:T(8,128)S(1)}, bf16[256,128]{1,0:T(8,128)(2,1)}, bf16[1024,512]{1,0:T(8,128)(2,1)S(1)}, bf16[320,512]{1,0:T(8,128)(2,1)S(1)}, f32[320,128]{1,0:T(8,128)S(1)}) custom-call(s32[4]{0:T(128)S(1)} %pad_add_fusion.place_ref, s32[1,128]{1,0:T(1,128)S(1)} %bitcast.24, s32[4,128]{1,0:T(4,128)S(1)} %bitcast.22, ...), custom_call_target="tpu_custom_call" | custom-call | flops 1000000000 | bytes 1000000 | tf_op jit(solution)/shard_map/pallas_call | solution.py:517
  62.7 5.0 %all-to-all-done.2.recv_ref = f32[32,16,128]{2,1,0:T(8,128)S(1)} async-done(((f32[32,16,128]{2,1,0:T(8,128)}), f32[32,16,128]{2,1,0:T(8,128)S(1)}, u32[]{:S(2)}, u32[]{:S(2)}) %all-to-all-start.2) | async-done | bytes 262176 | tf_op jit(solution)/shard_map/all_to_all | solution.py:551
  67.7 2.4 %shard_map.77 = f32[16,4,128]{2,1,0:T(4,128)} custom-call(s32[4]{0:T(128)S(1)} %pad_add_fusion.place_ref, f32[32,16,128]{2,1,0:T(8,128)S(1)} %all-to-all-done.2.recv_ref, f32[256,128]{1,0:T(8,128)S(1)} %get-tuple-element.51.level_ref, bf16[1024,512]{1,0:T(8,128)(2,1)S(1)} %get-tuple-element.52.groups_ref, bf16[320,512]{1,0:T(8,128)(2,1)S(1)} %get-tuple-element.53.rows_ref, ...), custom_call_target="tpu_custom_call" | custom-call | flops 1000000000 | bytes 1000000 | tf_op jit(solution)/shard_map/pallas_call | solution.py:517
  (4 shorter events, 0.1 us)
Async XLA Ops:
  0.0 0.9 %copy-start = (f32[16,256]{1,0:T(8,128)S(1)}, f32[16,256]{1,0:T(8,128)}, u32[]{:S(2)}) copy-start(f32[16,256]{1,0:T(8,128)} %param.9) | copy-start | bytes 49156
  25.2 5.0 %collective-permute-start = (f32[64,9,2,128]{3,2,1,0:T(2,128)S(1)}, f32[64,9,2,128]{3,2,1,0:T(2,128)S(1)}, u32[]{:S(2)}, u32[]{:S(2)}) collective-permute-start(f32[64,9,2,128]{3,2,1,0:T(2,128)S(1)} %all_to_all.15), channel_id=1, source_target_pairs={{0,16},{16,0},{1,17},{17,1},{2,18},{18,2},{3,19},{19,3},{4,20},{20... | collective-permute-start | bytes 1769480 | tf_op jit(solution)/shard_map/ppermute | solution.py:547
  47.3 11.5 %copy-start.1 = (s32[128,4]{0,1:T(4,128)S(1)}, s32[128,4]{0,1:T(4,128)}, u32[]{:S(2)}) copy-start(s32[128,4]{0,1:T(4,128)} %param.8) | copy-start | bytes 6148
  47.3 11.6 %copy-start.2 = (s32[128]{0:T(128)S(1)}, s32[128]{0:T(128)}, u32[]{:S(2)}) copy-start(s32[128]{0:T(128)} %param.7) | copy-start | bytes 1540
  54.7 13.0 %all-to-all-start.2 = ((f32[32,16,128]{2,1,0:T(8,128)}), f32[32,16,128]{2,1,0:T(8,128)S(1)}, u32[]{:S(2)}, u32[]{:S(2)}) async-start(f32[32,16,128]{2,1,0:T(8,128)} %get-tuple-element.48), calls=%async_computation.2 | async-start | bytes 524288 | tf_op jit(solution)/shard_map/all_to_all | solution.py:551

commit v8 on v7

--- a/solution.py
+++ b/solution.py
@@ -380,7 +380,7 @@
         at = slice(256 * block, 256 * block + 256)
         level_ref[:, at] = near_level(near, cells_ref[...], table_ref[:, at], cell_col, targets(256 * block, 256))
 
-    solve_pair(log_b, mass_a, mass_b, ids, d, part, factor_ref, up_ref, send_ref, level)
+    solve_pair(log_b, mass_a, mass_b, ids, d, part, factor_ref, up_ref, send_ref, lambda i: [level(b) for b in LEVELS[i]])
     copy.wait()
 
 
@@ -525,6 +525,7 @@
     )(*inputs)
 
 
+LEVELS = ((0, 1), (2, 3), (4, 5), (6,), (7,), (), (), ())
 FACTORS = [(3072, 128, BF16), (1024, 128)]
 NEAR = [(256, 128, BF16), (1024, 512, BF16), (320, 512, BF16), (320, 128)]
 

time: 70.5 us -> 70.1 us (level)
  no operation moved by 1% of the time
where the time goes in v8:
time: 70.1 us; the launch traced here: 69.8 us
  blocking collectives  36 us (51%)
  Pallas kernels  20.7 us (30%)
  starting transfers between devices  6.66 us (10%)
  waiting for transfers between devices  5.01 us (7%)
  local copies, waits for them, and re-layouts  1.13 us (2%)
    all_to_all x1, blocking collectives, on_device(): lax.all_to_all(jnp.broadcast_to(block[None], (64, 9, 2, 128)), ('x', 'z',...  24 us
    pallas_call x5, Pallas kernels, call(): pl.pallas_call(body, out_shape=[jax.ShapeDtypeStruct(s[:-1], BF16) if s[-...  20.7 us
    all_to_all x1, blocking collectives, exchange(): return lax.all_to_all(rows, ('x', 'c', 'y'), 0, 0, tiled=True)  12 us
    all_to_all x1, waiting for transfers between devices, exchange(): return lax.all_to_all(rows, ('x', 'c', 'y'), 0, 0, tiled=True)  5.01 us
    all_to_all x1, starting transfers between devices, exchange(): return lax.all_to_all(rows, ('x', 'c', 'y'), 0, 0, tiled=True)  4.13 us
    ppermute x1, starting transfers between devices, on_device(): other = lax.ppermute(own, 'c', [(0, 1), (1, 0)]).reshape(1152, 128)  2.54 us
  transfers between devices with their start and end apart: 2, of which 1 were waited for; matrix products, arithmetic and copies ran while one was open for 0% of the time, Pallas kernels for 9%

profile of v8, /device:TPU:1, one launch (start us, length us, event | category | flops | bytes accessed | tf_op | source)
XLA Modules:
  0.0 69.8 jit_solution(9917785495714858261)
XLA Ops:
  0.0 0.0 copy-start
  0.0 0.9 %fusion.3 = (f32[16,1,128]{2,1,0:T(1,128)S(1)}, f32[16,1,128]{2,1,0:T(1,128)S(1)}, f32[16,1,128]{2,1,0:T(1,128)S(1)}, f32[16,1,128]{2,1,0:T(1,128)S(1)}) fusion(f32[16,4,128]{2,1,0:T(4,128)} %param.10), kind=kLoop, calls=%fused_computation.9 | loop fusion | bytes 65536 | tf_op jit(solution)/shard_map/slice | solution.py:538
  0.9 0.0 copy-done
  1.0 0.2 broadcast_in_dim.8
  1.2 24.0 %all_to_all.15 = f32[64,9,2,128]{3,2,1,0:T(2,128)S(1)} all-to-all(f32[64,9,2,128]{3,2,1,0:T(2,128)S(1)} %broadcast_in_dim.8), channel_id=1, replica_groups=mesh['x'=4,'c'=2,'z'=4,'y'=4] {'x','z','y'}, dimensions={0} | all-to-all | bytes 1179648 | tf_op jit(solution)/shard_map/all_to_all | solution.py:544
  25.2 2.5 %collective-permute-start = (f32[64,9,2,128]{3,2,1,0:T(2,128)S(1)}, f32[64,9,2,128]{3,2,1,0:T(2,128)S(1)}, u32[]{:S(2)}, u32[]{:S(2)}) collective-permute-start(f32[64,9,2,128]{3,2,1,0:T(2,128)S(1)} %all_to_all.15), channel_id=1, source_target_pairs={{0,16},{16,0},{1,17},{17,1},{2,18},{18,2},{3,19},{19,3},{4,20},{20... | collective-permute-start | bytes 1769480 | tf_op jit(solution)/shard_map/ppermute | solution.py:548
  27.8 0.1 pad_add_fusion.place_ref
  27.8 2.3 %shard_map.73 = (f32[128,128]{1,0:T(8,128)S(1)}, f32[128,128]{1,0:T(8,128)S(1)}, bf16[3072,128]{1,0:T(8,128)(2,1)S(1)}, f32[1024,128]{1,0:T(8,128)S(1)}, f32[16,...) custom-call(s32[4]{0:T(128)S(1)} %pad_add_fusion.place_ref, ...), custom_call_target="tpu_custom_call" | custom-call | flops 1000000000 | bytes 1000000 | tf_op jit(solution)/shard_map/pallas_call | solution.py:517
  30.2 0.0 collective-permute-done
  30.2 4.7 %shard_map.74 = (f32[32,16,128]{2,1,0:T(8,128)S(1)}, f32[128,128]{1,0:T(8,128)S(1)}, f32[256,2048]{1,0:T(8,128)S(1)}, f32[128,128]{1,0:T(8,128)S(1)}, f32[128,12...) custom-call(s32[4]{0:T(128)S(1)} %pad_add_fusion.place_ref, ...), custom_call_target="tpu_custom_call" | custom-call | flops 1000000000 | bytes 1000000 | tf_op jit(solution)/shard_map/pallas_call | solution.py:517
  34.9 12.0 %all_to_all.16.recv_ref = f32[32,16,128]{2,1,0:T(8,128)S(1)} all-to-all(f32[32,16,128]{2,1,0:T(8,128)S(1)} %get-tuple-element.39), channel_id=1, replica_groups=mesh['x'=4,'c'=2,'z'=4,'y'=4] {'x','c','y'}, dimensions={0} | all-to-all | bytes 524288 | tf_op jit(solution)/shard_map/all_to_all | solution.py:552
  47.0 0.0 copy-start.1
  47.0 0.0 copy-start.2
  47.0 7.4 %shard_map.75 = (f32[32,16,128]{2,1,0:T(8,128)}, bf16[768,128]{1,0:T(8,128)(2,1)S(1)}) custom-call(s32[4]{0:T(128)S(1)} %pad_add_fusion.place_ref, f32[16,128]{1,0:T(8,128)S(1)} %get-tuple-element.30.ids_ref.own_ids_ref, f32[32,16,128]{2,1,0:T(8,128)S(1)} %all_to_all.16.recv_ref, f32[256,2048]{1,0:T(8,128)S(1)} %get-tuple-element.40.level_ref, ...), custom_call_target="tpu_custom_call" | custom-call | flops 1000000000 | bytes 1000000 | tf_op jit(solution)/shard_map/pallas_call | solution.py:517
  54.4 4.1 %all-to-all-start.2 = ((f32[32,16,128]{2,1,0:T(8,128)}), f32[32,16,128]{2,1,0:T(8,128)S(1)}, u32[]{:S(2)}, u32[]{:S(2)}) async-start(f32[32,16,128]{2,1,0:T(8,128)} %get-tuple-element.48), calls=%async_computation.2 | async-start | bytes 524288 | tf_op jit(solution)/shard_map/all_to_all | solution.py:552
  58.5 0.0 copy-done.1
  58.5 0.0 copy-done.2
  58.5 3.9 %shard_map.76 = (f32[256,128]{1,0:T(8,128)S(1)}, bf16[256,128]{1,0:T(8,128)(2,1)}, bf16[1024,512]{1,0:T(8,128)(2,1)S(1)}, bf16[320,512]{1,0:T(8,128)(2,1)S(1)}, f32[320,128]{1,0:T(8,128)S(1)}) custom-call(s32[4]{0:T(128)S(1)} %pad_add_fusion.place_ref, s32[1,128]{1,0:T(1,128)S(1)} %bitcast.24, s32[4,128]{1,0:T(4,128)S(1)} %bitcast.22, ...), custom_call_target="tpu_custom_call" | custom-call | flops 1000000000 | bytes 1000000 | tf_op jit(solution)/shard_map/pallas_call | solution.py:517
  62.4 5.0 %all-to-all-done.2.recv_ref = f32[32,16,128]{2,1,0:T(8,128)S(1)} async-done(((f32[32,16,128]{2,1,0:T(8,128)}), f32[32,16,128]{2,1,0:T(8,128)S(1)}, u32[]{:S(2)}, u32[]{:S(2)}) %all-to-all-start.2) | async-done | bytes 262176 | tf_op jit(solution)/shard_map/all_to_all | solution.py:552
  67.4 2.4 %shard_map.77 = f32[16,4,128]{2,1,0:T(4,128)} custom-call(s32[4]{0:T(128)S(1)} %pad_add_fusion.place_ref, f32[32,16,128]{2,1,0:T(8,128)S(1)} %all-to-all-done.2.recv_ref, f32[256,128]{1,0:T(8,128)S(1)} %get-tuple-element.51.level_ref, bf16[1024,512]{1,0:T(8,128)(2,1)S(1)} %get-tuple-element.52.groups_ref, bf16[320,512]{1,0:T(8,128)(2,1)S(1)} %get-tuple-element.53.rows_ref, ...), custom_call_target="tpu_custom_call" | custom-call | flops 1000000000 | bytes 1000000 | tf_op jit(solution)/shard_map/pallas_call | solution.py:517
  (4 shorter events, 0.1 us)
Async XLA Ops:
  0.0 0.9 %copy-start = (f32[16,256]{1,0:T(8,128)S(1)}, f32[16,256]{1,0:T(8,128)}, u32[]{:S(2)}) copy-start(f32[16,256]{1,0:T(8,128)} %param.9) | copy-start | bytes 49156
  25.2 5.0 %collective-permute-start = (f32[64,9,2,128]{3,2,1,0:T(2,128)S(1)}, f32[64,9,2,128]{3,2,1,0:T(2,128)S(1)}, u32[]{:S(2)}, u32[]{:S(2)}) collective-permute-start(f32[64,9,2,128]{3,2,1,0:T(2,128)S(1)} %all_to_all.15), channel_id=1, source_target_pairs={{0,16},{16,0},{1,17},{17,1},{2,18},{18,2},{3,19},{19,3},{4,20},{20... | collective-permute-start | bytes 1769480 | tf_op jit(solution)/shard_map/ppermute | solution.py:548
  47.0 11.5 %copy-start.1 = (s32[128,4]{0,1:T(4,128)S(1)}, s32[128,4]{0,1:T(4,128)}, u32[]{:S(2)}) copy-start(s32[128,4]{0,1:T(4,128)} %param.8) | copy-start | bytes 6148
  47.0 11.6 %copy-start.2 = (s32[128]{0:T(128)S(1)}, s32[128]{0:T(128)}, u32[]{:S(2)}) copy-start(s32[128]{0:T(128)} %param.7) | copy-start | bytes 1540
  54.4 13.0 %all-to-all-start.2 = ((f32[32,16,128]{2,1,0:T(8,128)}), f32[32,16,128]{2,1,0:T(8,128)S(1)}, u32[]{:S(2)}, u32[]{:S(2)}) async-start(f32[32,16,128]{2,1,0:T(8,128)} %get-tuple-element.48), calls=%async_computation.2 | async-start | bytes 524288 | tf_op jit(solution)/shard_map/all_to_all | solution.py:552

commit v9 on v8

--- a/solution.py
+++ b/solution.py
@@ -426,11 +426,11 @@
 
 def gathered(recv_ref, groups_ref, rows_ref):
     f = recv_ref[...].reshape(512, 128)
-    by_k = dot(groups_ref[...], packed(f))
     o = rows_ref[...]
     high, mid, low = split3(f)
-    two = dot(o, jnp.concatenate([high, mid], axis=1))
-    e0, e1, top = unpack((two[:, :128] + two[:, 128:]) + dot(o, low))
+    three = dot(o, jnp.concatenate([high, mid, low], axis=1))
+    e0, e1, top = unpack((three[:, :128] + three[:, 128:256]) + three[:, 256:])
+    by_k = dot(groups_ref[...], packed(f))
     by_k = [by_k[256 * k : 256 * k + 256] for k in range(4)]
     return cell_halves(by_k), wide(e0[:256]), wide(e1), top
 

time: 70.1 us -> 70.5 us (level)
  no operation moved by 1% of the time
where the time goes in v9:
time: 70.5 us; the launch traced here: 70.2 us
  blocking collectives  36 us (51%)
  Pallas kernels  21.1 us (30%)
  starting transfers between devices  6.66 us (9%)
  waiting for transfers between devices  5.01 us (7%)
  local copies, waits for them, and re-layouts  1.13 us (2%)
    all_to_all x1, blocking collectives, on_device(): lax.all_to_all(jnp.broadcast_to(block[None], (64, 9, 2, 128)), ('x', 'z',...  24 us
    pallas_call x5, Pallas kernels, call(): pl.pallas_call(body, out_shape=[jax.ShapeDtypeStruct(s[:-1], BF16) if s[-...  21.1 us
    all_to_all x1, blocking collectives, exchange(): return lax.all_to_all(rows, ('x', 'c', 'y'), 0, 0, tiled=True)  12 us
    all_to_all x1, waiting for transfers between devices, exchange(): return lax.all_to_all(rows, ('x', 'c', 'y'), 0, 0, tiled=True)  5.01 us
    all_to_all x1, starting transfers between devices, exchange(): return lax.all_to_all(rows, ('x', 'c', 'y'), 0, 0, tiled=True)  4.12 us
    ppermute x1, starting transfers between devices, on_device(): other = lax.ppermute(own, 'c', [(0, 1), (1, 0)]).reshape(1152, 128)  2.54 us
  transfers between devices with their start and end apart: 2, of which 1 were waited for; matrix products, arithmetic and copies ran while one was open for 0% of the time, Pallas kernels for 9%

profile of v9, /device:TPU:1, one launch (start us, length us, event | category | flops | bytes accessed | tf_op | source)
XLA Modules:
  0.0 70.2 jit_solution(3081784789639293943)
XLA Ops:
  0.0 0.0 copy-start
  0.0 0.9 %fusion.3 = (f32[16,1,128]{2,1,0:T(1,128)S(1)}, f32[16,1,128]{2,1,0:T(1,128)S(1)}, f32[16,1,128]{2,1,0:T(1,128)S(1)}, f32[16,1,128]{2,1,0:T(1,128)S(1)}) fusion(f32[16,4,128]{2,1,0:T(4,128)} %param.10), kind=kLoop, calls=%fused_computation.9 | loop fusion | bytes 65536 | tf_op jit(solution)/shard_map/slice | solution.py:538
  0.9 0.0 copy-done
  1.0 0.2 broadcast_in_dim.8
  1.2 24.0 %all_to_all.15 = f32[64,9,2,128]{3,2,1,0:T(2,128)S(1)} all-to-all(f32[64,9,2,128]{3,2,1,0:T(2,128)S(1)} %broadcast_in_dim.8), channel_id=1, replica_groups=mesh['x'=4,'c'=2,'z'=4,'y'=4] {'x','z','y'}, dimensions={0} | all-to-all | bytes 1179648 | tf_op jit(solution)/shard_map/all_to_all | solution.py:544
  25.2 2.5 %collective-permute-start = (f32[64,9,2,128]{3,2,1,0:T(2,128)S(1)}, f32[64,9,2,128]{3,2,1,0:T(2,128)S(1)}, u32[]{:S(2)}, u32[]{:S(2)}) collective-permute-start(f32[64,9,2,128]{3,2,1,0:T(2,128)S(1)} %all_to_all.15), channel_id=1, source_target_pairs={{0,16},{16,0},{1,17},{17,1},{2,18},{18,2},{3,19},{19,3},{4,20},{20... | collective-permute-start | bytes 1769480 | tf_op jit(solution)/shard_map/ppermute | solution.py:548
  27.8 0.1 pad_add_fusion.place_ref
  27.8 2.3 %shard_map.73 = (f32[128,128]{1,0:T(8,128)S(1)}, f32[128,128]{1,0:T(8,128)S(1)}, bf16[3072,128]{1,0:T(8,128)(2,1)S(1)}, f32[1024,128]{1,0:T(8,128)S(1)}, f32[16,...) custom-call(s32[4]{0:T(128)S(1)} %pad_add_fusion.place_ref, ...), custom_call_target="tpu_custom_call" | custom-call | flops 1000000000 | bytes 1000000 | tf_op jit(solution)/shard_map/pallas_call | solution.py:517
  30.2 0.0 collective-permute-done
  30.2 4.7 %shard_map.74 = (f32[32,16,128]{2,1,0:T(8,128)S(1)}, f32[128,128]{1,0:T(8,128)S(1)}, f32[256,2048]{1,0:T(8,128)S(1)}, f32[128,128]{1,0:T(8,128)S(1)}, f32[128,12...) custom-call(s32[4]{0:T(128)S(1)} %pad_add_fusion.place_ref, ...), custom_call_target="tpu_custom_call" | custom-call | flops 1000000000 | bytes 1000000 | tf_op jit(solution)/shard_map/pallas_call | solution.py:517
  34.9 12.0 %all_to_all.16.recv_ref = f32[32,16,128]{2,1,0:T(8,128)S(1)} all-to-all(f32[32,16,128]{2,1,0:T(8,128)S(1)} %get-tuple-element.39), channel_id=1, replica_groups=mesh['x'=4,'c'=2,'z'=4,'y'=4] {'x','c','y'}, dimensions={0} | all-to-all | bytes 524288 | tf_op jit(solution)/shard_map/all_to_all | solution.py:552
  47.0 0.0 copy-start.1
  47.0 0.0 copy-start.2
  47.0 7.7 %shard_map.75 = (f32[32,16,128]{2,1,0:T(8,128)}, bf16[768,128]{1,0:T(8,128)(2,1)S(1)}) custom-call(s32[4]{0:T(128)S(1)} %pad_add_fusion.place_ref, f32[16,128]{1,0:T(8,128)S(1)} %get-tuple-element.30.ids_ref.own_ids_ref, f32[32,16,128]{2,1,0:T(8,128)S(1)} %all_to_all.16.recv_ref, f32[256,2048]{1,0:T(8,128)S(1)} %get-tuple-element.40.level_ref, ...), custom_call_target="tpu_custom_call" | custom-call | flops 1000000000 | bytes 1000000 | tf_op jit(solution)/shard_map/pallas_call | solution.py:517
  54.7 4.1 %all-to-all-start.2 = ((f32[32,16,128]{2,1,0:T(8,128)}), f32[32,16,128]{2,1,0:T(8,128)S(1)}, u32[]{:S(2)}, u32[]{:S(2)}) async-start(f32[32,16,128]{2,1,0:T(8,128)} %get-tuple-element.48), calls=%async_computation.2 | async-start | bytes 524288 | tf_op jit(solution)/shard_map/all_to_all | solution.py:552
  58.8 0.0 copy-done.1
  58.8 0.0 copy-done.2
  58.8 3.9 %shard_map.76 = (f32[256,128]{1,0:T(8,128)S(1)}, bf16[256,128]{1,0:T(8,128)(2,1)}, bf16[1024,512]{1,0:T(8,128)(2,1)S(1)}, bf16[320,512]{1,0:T(8,128)(2,1)S(1)}, f32[320,128]{1,0:T(8,128)S(1)}) custom-call(s32[4]{0:T(128)S(1)} %pad_add_fusion.place_ref, s32[1,128]{1,0:T(1,128)S(1)} %bitcast.24, s32[4,128]{1,0:T(4,128)S(1)} %bitcast.22, ...), custom_call_target="tpu_custom_call" | custom-call | flops 1000000000 | bytes 1000000 | tf_op jit(solution)/shard_map/pallas_call | solution.py:517
  62.7 5.0 %all-to-all-done.2.recv_ref = f32[32,16,128]{2,1,0:T(8,128)S(1)} async-done(((f32[32,16,128]{2,1,0:T(8,128)}), f32[32,16,128]{2,1,0:T(8,128)S(1)}, u32[]{:S(2)}, u32[]{:S(2)}) %all-to-all-start.2) | async-done | bytes 262176 | tf_op jit(solution)/shard_map/all_to_all | solution.py:552
  67.7 2.5 %shard_map.77 = f32[16,4,128]{2,1,0:T(4,128)} custom-call(s32[4]{0:T(128)S(1)} %pad_add_fusion.place_ref, f32[32,16,128]{2,1,0:T(8,128)S(1)} %all-to-all-done.2.recv_ref, f32[256,128]{1,0:T(8,128)S(1)} %get-tuple-element.51.level_ref, bf16[1024,512]{1,0:T(8,128)(2,1)S(1)} %get-tuple-element.52.groups_ref, bf16[320,512]{1,0:T(8,128)(2,1)S(1)} %get-tuple-element.53.rows_ref, ...), custom_call_target="tpu_custom_call" | custom-call | flops 1000000000 | bytes 1000000 | tf_op jit(solution)/shard_map/pallas_call | solution.py:517
  (4 shorter events, 0.1 us)
Async XLA Ops:
  0.0 0.9 %copy-start = (f32[16,256]{1,0:T(8,128)S(1)}, f32[16,256]{1,0:T(8,128)}, u32[]{:S(2)}) copy-start(f32[16,256]{1,0:T(8,128)} %param.9) | copy-start | bytes 49156
  25.2 5.0 %collective-permute-start = (f32[64,9,2,128]{3,2,1,0:T(2,128)S(1)}, f32[64,9,2,128]{3,2,1,0:T(2,128)S(1)}, u32[]{:S(2)}, u32[]{:S(2)}) collective-permute-start(f32[64,9,2,128]{3,2,1,0:T(2,128)S(1)} %all_to_all.15), channel_id=1, source_target_pairs={{0,16},{16,0},{1,17},{17,1},{2,18},{18,2},{3,19},{19,3},{4,20},{20... | collective-permute-start | bytes 1769480 | tf_op jit(solution)/shard_map/ppermute | solution.py:548
  47.0 11.8 %copy-start.1 = (s32[128,4]{0,1:T(4,128)S(1)}, s32[128,4]{0,1:T(4,128)}, u32[]{:S(2)}) copy-start(s32[128,4]{0,1:T(4,128)} %param.8) | copy-start | bytes 6148
  47.0 11.8 %copy-start.2 = (s32[128]{0:T(128)S(1)}, s32[128]{0:T(128)}, u32[]{:S(2)}) copy-start(s32[128]{0:T(128)} %param.7) | copy-start | bytes 1540
  54.7 13.0 %all-to-all-start.2 = ((f32[32,16,128]{2,1,0:T(8,128)}), f32[32,16,128]{2,1,0:T(8,128)S(1)}, u32[]{:S(2)}, u32[]{:S(2)}) async-start(f32[32,16,128]{2,1,0:T(8,128)} %get-tuple-element.48), calls=%async_computation.2 | async-start | bytes 524288 | tf_op jit(solution)/shard_map/all_to_all | solution.py:552

commit v10 on v9

--- a/solution.py
+++ b/solution.py
@@ -502,7 +502,7 @@
     centre = basic_centre(ids_ref[:, :1])
     v, d = near_margins(gathered(recv_ref, groups_ref, rows_ref), level_ref[...], centre,
                         targets(place_ref[2] * 128, 128), whole_ref[...])
-    out = jnp.exp(v + jnp.log(d))
+    out = jnp.exp(v) * d
     for k in range(4):
         out_ref[:, k, :] = out[16 * k : 16 * k + 16]
 

time: 70.5 us -> 70.5 us (level)
  no operation moved by 1% of the time
where the time goes in v10:
time: 70.5 us; the launch traced here: 70.1 us
  blocking collectives  36 us (51%)
  Pallas kernels  21.1 us (30%)
  starting transfers between devices  6.66 us (9%)
  waiting for transfers between devices  5.01 us (7%)
  local copies, waits for them, and re-layouts  1.13 us (2%)
    all_to_all x1, blocking collectives, on_device(): lax.all_to_all(jnp.broadcast_to(block[None], (64, 9, 2, 128)), ('x', 'z',...  24 us
    pallas_call x5, Pallas kernels, call(): pl.pallas_call(body, out_shape=[jax.ShapeDtypeStruct(s[:-1], BF16) if s[-...  21.1 us
    all_to_all x1, blocking collectives, exchange(): return lax.all_to_all(rows, ('x', 'c', 'y'), 0, 0, tiled=True)  12 us
    all_to_all x1, waiting for transfers between devices, exchange(): return lax.all_to_all(rows, ('x', 'c', 'y'), 0, 0, tiled=True)  5.01 us
    all_to_all x1, starting transfers between devices, exchange(): return lax.all_to_all(rows, ('x', 'c', 'y'), 0, 0, tiled=True)  4.12 us
    ppermute x1, starting transfers between devices, on_device(): other = lax.ppermute(own, 'c', [(0, 1), (1, 0)]).reshape(1152, 128)  2.54 us
  transfers between devices with their start and end apart: 2, of which 1 were waited for; matrix products, arithmetic and copies ran while one was open for 0% of the time, Pallas kernels for 9%

profile of v10, /device:TPU:1, one launch (start us, length us, event | category | flops | bytes accessed | tf_op | source)
XLA Modules:
  0.0 70.1 jit_solution(13878053695139145798)
XLA Ops:
  0.0 0.0 copy-start
  0.0 0.9 %fusion.3 = (f32[16,1,128]{2,1,0:T(1,128)S(1)}, f32[16,1,128]{2,1,0:T(1,128)S(1)}, f32[16,1,128]{2,1,0:T(1,128)S(1)}, f32[16,1,128]{2,1,0:T(1,128)S(1)}) fusion(f32[16,4,128]{2,1,0:T(4,128)} %param.10), kind=kLoop, calls=%fused_computation.9 | loop fusion | bytes 65536 | tf_op jit(solution)/shard_map/slice | solution.py:538
  0.9 0.0 copy-done
  1.0 0.2 broadcast_in_dim.8
  1.2 24.0 %all_to_all.15 = f32[64,9,2,128]{3,2,1,0:T(2,128)S(1)} all-to-all(f32[64,9,2,128]{3,2,1,0:T(2,128)S(1)} %broadcast_in_dim.8), channel_id=1, replica_groups=mesh['x'=4,'c'=2,'z'=4,'y'=4] {'x','z','y'}, dimensions={0} | all-to-all | bytes 1179648 | tf_op jit(solution)/shard_map/all_to_all | solution.py:544
  25.2 2.5 %collective-permute-start = (f32[64,9,2,128]{3,2,1,0:T(2,128)S(1)}, f32[64,9,2,128]{3,2,1,0:T(2,128)S(1)}, u32[]{:S(2)}, u32[]{:S(2)}) collective-permute-start(f32[64,9,2,128]{3,2,1,0:T(2,128)S(1)} %all_to_all.15), channel_id=1, source_target_pairs={{0,16},{16,0},{1,17},{17,1},{2,18},{18,2},{3,19},{19,3},{4,20},{20... | collective-permute-start | bytes 1769480 | tf_op jit(solution)/shard_map/ppermute | solution.py:548
  27.8 0.1 pad_add_fusion.place_ref
  27.8 2.3 %shard_map.73 = (f32[128,128]{1,0:T(8,128)S(1)}, f32[128,128]{1,0:T(8,128)S(1)}, bf16[3072,128]{1,0:T(8,128)(2,1)S(1)}, f32[1024,128]{1,0:T(8,128)S(1)}, f32[16,...) custom-call(s32[4]{0:T(128)S(1)} %pad_add_fusion.place_ref, ...), custom_call_target="tpu_custom_call" | custom-call | flops 1000000000 | bytes 1000000 | tf_op jit(solution)/shard_map/pallas_call | solution.py:517
  30.2 0.0 collective-permute-done
  30.2 4.7 %shard_map.74 = (f32[32,16,128]{2,1,0:T(8,128)S(1)}, f32[128,128]{1,0:T(8,128)S(1)}, f32[256,2048]{1,0:T(8,128)S(1)}, f32[128,128]{1,0:T(8,128)S(1)}, f32[128,12...) custom-call(s32[4]{0:T(128)S(1)} %pad_add_fusion.place_ref, ...), custom_call_target="tpu_custom_call" | custom-call | flops 1000000000 | bytes 1000000 | tf_op jit(solution)/shard_map/pallas_call | solution.py:517
  34.9 12.0 %all_to_all.16.recv_ref = f32[32,16,128]{2,1,0:T(8,128)S(1)} all-to-all(f32[32,16,128]{2,1,0:T(8,128)S(1)} %get-tuple-element.39), channel_id=1, replica_groups=mesh['x'=4,'c'=2,'z'=4,'y'=4] {'x','c','y'}, dimensions={0} | all-to-all | bytes 524288 | tf_op jit(solution)/shard_map/all_to_all | solution.py:552
  47.0 0.0 copy-start.1
  47.0 0.0 copy-start.2
  47.0 7.7 %shard_map.75 = (f32[32,16,128]{2,1,0:T(8,128)}, bf16[768,128]{1,0:T(8,128)(2,1)S(1)}) custom-call(s32[4]{0:T(128)S(1)} %pad_add_fusion.place_ref, f32[16,128]{1,0:T(8,128)S(1)} %get-tuple-element.30.ids_ref.own_ids_ref, f32[32,16,128]{2,1,0:T(8,128)S(1)} %all_to_all.16.recv_ref, f32[256,2048]{1,0:T(8,128)S(1)} %get-tuple-element.40.level_ref, ...), custom_call_target="tpu_custom_call" | custom-call | flops 1000000000 | bytes 1000000 | tf_op jit(solution)/shard_map/pallas_call | solution.py:517
  54.7 4.1 %all-to-all-start.2 = ((f32[32,16,128]{2,1,0:T(8,128)}), f32[32,16,128]{2,1,0:T(8,128)S(1)}, u32[]{:S(2)}, u32[]{:S(2)}) async-start(f32[32,16,128]{2,1,0:T(8,128)} %get-tuple-element.48), calls=%async_computation.2 | async-start | bytes 524288 | tf_op jit(solution)/shard_map/all_to_all | solution.py:552
  58.8 0.0 copy-done.1
  58.8 0.0 copy-done.2
  58.8 3.9 %shard_map.76 = (f32[256,128]{1,0:T(8,128)S(1)}, bf16[256,128]{1,0:T(8,128)(2,1)}, bf16[1024,512]{1,0:T(8,128)(2,1)S(1)}, bf16[320,512]{1,0:T(8,128)(2,1)S(1)}, f32[320,128]{1,0:T(8,128)S(1)}) custom-call(s32[4]{0:T(128)S(1)} %pad_add_fusion.place_ref, s32[1,128]{1,0:T(1,128)S(1)} %bitcast.24, s32[4,128]{1,0:T(4,128)S(1)} %bitcast.22, ...), custom_call_target="tpu_custom_call" | custom-call | flops 1000000000 | bytes 1000000 | tf_op jit(solution)/shard_map/pallas_call | solution.py:517
  62.7 5.0 %all-to-all-done.2.recv_ref = f32[32,16,128]{2,1,0:T(8,128)S(1)} async-done(((f32[32,16,128]{2,1,0:T(8,128)}), f32[32,16,128]{2,1,0:T(8,128)S(1)}, u32[]{:S(2)}, u32[]{:S(2)}) %all-to-all-start.2) | async-done | bytes 262176 | tf_op jit(solution)/shard_map/all_to_all | solution.py:552
  67.7 2.5 %shard_map.77 = f32[16,4,128]{2,1,0:T(4,128)} custom-call(s32[4]{0:T(128)S(1)} %pad_add_fusion.place_ref, f32[32,16,128]{2,1,0:T(8,128)S(1)} %all-to-all-done.2.recv_ref, f32[256,128]{1,0:T(8,128)S(1)} %get-tuple-element.51.level_ref, bf16[1024,512]{1,0:T(8,128)(2,1)S(1)} %get-tuple-element.52.groups_ref, bf16[320,512]{1,0:T(8,128)(2,1)S(1)} %get-tuple-element.53.rows_ref, ...), custom_call_target="tpu_custom_call" | custom-call | flops 1000000000 | bytes 1000000 | tf_op jit(solution)/shard_map/pallas_call | solution.py:517
  (4 shorter events, 0.1 us)
Async XLA Ops:
  0.0 0.9 %copy-start = (f32[16,256]{1,0:T(8,128)S(1)}, f32[16,256]{1,0:T(8,128)}, u32[]{:S(2)}) copy-start(f32[16,256]{1,0:T(8,128)} %param.9) | copy-start | bytes 49156
  25.2 5.0 %collective-permute-start = (f32[64,9,2,128]{3,2,1,0:T(2,128)S(1)}, f32[64,9,2,128]{3,2,1,0:T(2,128)S(1)}, u32[]{:S(2)}, u32[]{:S(2)}) collective-permute-start(f32[64,9,2,128]{3,2,1,0:T(2,128)S(1)} %all_to_all.15), channel_id=1, source_target_pairs={{0,16},{16,0},{1,17},{17,1},{2,18},{18,2},{3,19},{19,3},{4,20},{20... | collective-permute-start | bytes 1769480 | tf_op jit(solution)/shard_map/ppermute | solution.py:548
  47.0 11.8 %copy-start.1 = (s32[128,4]{0,1:T(4,128)S(1)}, s32[128,4]{0,1:T(4,128)}, u32[]{:S(2)}) copy-start(s32[128,4]{0,1:T(4,128)} %param.8) | copy-start | bytes 6148
  47.0 11.8 %copy-start.2 = (s32[128]{0:T(128)S(1)}, s32[128]{0:T(128)}, u32[]{:S(2)}) copy-start(s32[128]{0:T(128)} %param.7) | copy-start | bytes 1540
  54.7 13.0 %all-to-all-start.2 = ((f32[32,16,128]{2,1,0:T(8,128)}), f32[32,16,128]{2,1,0:T(8,128)S(1)}, u32[]{:S(2)}, u32[]{:S(2)}) async-start(f32[32,16,128]{2,1,0:T(8,128)} %get-tuple-element.48), calls=%async_computation.2 | async-start | bytes 524288 | tf_op jit(solution)/shard_map/all_to_all | solution.py:552
